TPU v7x, 32 devices: a whole 2x2x4 slice. The times are simulated.
32 devices in a mesh: dp: 4 (over x, core), ulysses: 4 (over z), blk: 2 (over y).
Axes of the slice: x: 2, y: 2, z: 4, core: 2. Of those that a mesh axis runs over, the one named last changes fastest.
Arguments:
- tokens: bfloat16 [8, 512, 2048], P('dp', ('ulysses', 'blk')), may hold values from -6 to 6
- memory: bfloat16 [8, 512, 2048], P('dp', ('ulysses', 'blk')), may hold values from -6 to 6
- lengths: int32 [8, 8], P('dp'), may hold values from 1 to 480, as said below
- gain_attn: float32 [2048], replicated, may hold values from 0.5 to 1.5
- gain_memory: float32 [2048], replicated, may hold values from 0.5 to 1.5
- gain_ffn: float32 [2048], replicated, may hold values from 0.5 to 1.5
- w_query: bfloat16 [2048, 2048], P(('dp', 'ulysses', 'blk')), may hold values from -0.125 to 0.125
- w_key: bfloat16 [2048, 2048], P(('dp', 'ulysses', 'blk')), may hold values from -0.125 to 0.125
- w_value: bfloat16 [2048, 2048], P(('dp', 'ulysses', 'blk')), may hold values from -0.125 to 0.125
- w_out: bfloat16 [2048, 2048], P(('dp', 'ulysses', 'blk')), may hold values from -0.75 to 0.75
- w_gate: bfloat16 [2048, 5504], P(('dp', 'ulysses', 'blk')), may hold values from -0.125 to 0.125
- w_up: bfloat16 [2048, 5504], P(('dp', 'ulysses', 'blk')), may hold values from -0.125 to 0.125
- w_down: bfloat16 [2048, 5504], P(('dp', 'ulysses', 'blk')), may hold values from -0.078125 to 0.078125
- cotangent: bfloat16 [8, 512, 2048], P('dp', ('ulysses', 'blk')), may hold values from -6 to 6
Outputs:
- output: bfloat16 [8, 512, 2048], P('dp', ('ulysses', 'blk'))
- grad_tokens: bfloat16 [8, 512, 2048], P('dp', ('ulysses', 'blk'))
- grad_memory: bfloat16 [8, 512, 2048], P('dp', ('ulysses', 'blk'))
- grad_gain_attn: float32 [2048], P(('dp', 'ulysses', 'blk'))
- grad_gain_memory: float32 [2048], P(('dp', 'ulysses', 'blk'))
- grad_gain_ffn: float32 [2048], P(('dp', 'ulysses', 'blk'))
- grad_query: float32 [2048, 2048], P('dp', ('ulysses', 'blk'))
- grad_key: float32 [2048, 2048], P('dp', ('ulysses', 'blk'))
- grad_value: float32 [2048, 2048], P('dp', ('ulysses', 'blk'))
- grad_out: float32 [2048, 2048], P('dp', ('ulysses', 'blk'))
- grad_gate: float32 [2048, 5504], P('dp', ('ulysses', 'blk'))
- grad_up: float32 [2048, 5504], P('dp', ('ulysses', 'blk'))
- grad_down: float32 [2048, 5504], P('dp', ('ulysses', 'blk'))
Inputs may be any that keep to these rules, and one draw needn't show every extreme that they name: Each row of lengths gives, in order, the lengths of the 8 documents packed at its start; they sum to less than 512, the rest of the row is padding, and every row has one document of the largest length.
All inputs are finite; a program needn't handle non-finite values.
Results may differ from a plain program's by a relative error of at most 0.018.
Values may be sent and summed in bfloat16 or wider, within the bound.
No kernel may reach another device: no remote copies, remote signals or barrier semaphores. Data moves between devices by JAX's collectives and lax.ppermute only.
A program may use at most 320 MiB of HBM per device.

v0:
```python
import functools

import jax
import jax.numpy as jnp
from jax import lax
from jax.experimental import pallas as pl
from jax.experimental.pallas import tpu as pltpu
from jax.sharding import PartitionSpec as P

H = 16
HD = 128
AXES = ("dp", "ulysses", "blk")
bf16 = jnp.bfloat16
f32 = jnp.float32
epsilon = 1e-06
negative = -1e30


def dot(left, right, over, kind=f32):
    return lax.dot_general(left, right, (over, ((), ())), preferred_element_type=kind)


def times(left, right, kind=f32):
    return dot(left, right, ((1,), (0,)), kind)


def times_transposed(left, right, kind=f32):
    return dot(left, right, ((1,), (1,)), kind)


def transposed_times(left, right, kind=f32):
    return dot(left, right, ((0,), (0,)), kind)


def normalize(values):
    inverse = lax.rsqrt(jnp.mean(values * values, axis=-1, keepdims=True) + epsilon)
    return (values * inverse, inverse)


def norm_back(grad_normed, normed, inverse, gain):
    scaled = grad_normed * gain
    return inverse * (scaled - normed * jnp.mean(scaled * normed, axis=-1, keepdims=True))


def add_low(left, right):
    return (left.astype(f32) + right.astype(f32)).astype(bf16)


def masked_scores(q, k, start, place, key_place, scale):
    scores = times_transposed(q, k) * scale
    allowed = (key_place >= start) & (key_place <= place)
    return jnp.where(allowed, scores, negative)


def attention_parts(q_ref, k_ref, ko_ref, info_ref, places_ref, scale):
    width = q_ref.shape[-1]
    q = q_ref[0, :, 0].reshape(-1, width)
    k = k_ref[0, :, 0].reshape(-1, width)
    ko = ko_ref[0, :, 0].reshape(-1, width)
    start = info_ref[0, 0, :, 0:1]
    place = info_ref[0, 0, :, 1:2]
    own = masked_scores(q, k, start, place, places_ref[0:1, :], scale)
    other = masked_scores(q, ko, start, place, places_ref[1:2, :], scale)
    largest = jnp.maximum(
        jnp.max(own, axis=-1, keepdims=True), jnp.max(other, axis=-1, keepdims=True)
    )
    own = jnp.exp(own - largest)
    other = jnp.exp(other - largest)
    total = jnp.sum(own, axis=-1, keepdims=True) + jnp.sum(other, axis=-1, keepdims=True)
    return q, k, ko, own / total, other / total


def attend_kernel(scale, q_ref, k_ref, v_ref, ko_ref, vo_ref, info_ref, places_ref, out_ref):
    width = q_ref.shape[-1]
    _, _, _, own, other = attention_parts(q_ref, k_ref, ko_ref, info_ref, places_ref, scale)
    v = v_ref[0, :, 0].reshape(-1, width)
    vo = vo_ref[0, :, 0].reshape(-1, width)
    mixed = times(own.astype(bf16), v) + times(other.astype(bf16), vo)
    out_ref[0, :, 0] = mixed.astype(bf16).reshape(out_ref.shape[1], out_ref.shape[3], width)


def attend_back_kernel(
    scale,
    q_ref,
    k_ref,
    v_ref,
    ko_ref,
    vo_ref,
    g_ref,
    info_ref,
    places_ref,
    gq_ref,
    gk_ref,
    gv_ref,
    gko_ref,
    gvo_ref,
):
    width = q_ref.shape[-1]
    q, k, ko, own, other = attention_parts(q_ref, k_ref, ko_ref, info_ref, places_ref, scale)
    v = v_ref[0, :, 0].reshape(-1, width)
    vo = vo_ref[0, :, 0].reshape(-1, width)
    g = g_ref[0, :, 0].reshape(-1, width)
    grad_own = times_transposed(g, v)
    grad_other = times_transposed(g, vo)
    centre = jnp.sum(own * grad_own, axis=-1, keepdims=True) + jnp.sum(
        other * grad_other, axis=-1, keepdims=True
    )
    score_own = (own * (grad_own - centre)).astype(bf16)
    score_other = (other * (grad_other - centre)).astype(bf16)

    def put(ref, value):
        ref[0, :, 0] = value.astype(ref.dtype).reshape(ref.shape[1], ref.shape[3], width)

    put(gq_ref, (times(score_own, k) + times(score_other, ko)) * scale)
    put(gk_ref, transposed_times(score_own, q) * scale)
    put(gko_ref, transposed_times(score_other, q) * scale)
    put(gv_ref, transposed_times(own.astype(bf16), g))
    put(gvo_ref, transposed_times(other.astype(bf16), g))


def attention_call(kernel, inputs, info, places, out_kinds):
    twins, pieces, rows, tok, width = inputs[0].shape
    heads = width // HD
    block = pl.BlockSpec((1, pieces, 1, tok, HD), lambda c, r, h: (c, 0, r, 0, h))
    span = pieces * tok
    flops = 2 * twins * rows * heads * span * span * HD * 2 * len(inputs)
    return pl.pallas_call(
        kernel,
        grid=(twins, rows, heads),
        in_specs=[block] * len(inputs)
        + [
            pl.BlockSpec((1, 1, span, 2), lambda c, r, h: (c, r, 0, 0)),
            pl.BlockSpec(places.shape, lambda c, r, h: (0, 0)),
        ],
        out_specs=[block] * len(out_kinds),
        out_shape=[jax.ShapeDtypeStruct(inputs[0].shape, kind) for kind in out_kinds],
        compiler_params=pltpu.CompilerParams(vmem_limit_bytes=48 * 1024 * 1024),
        cost_estimate=pl.CostEstimate(
            flops=flops,
            bytes_accessed=2 * inputs[0].size * (len(inputs) + len(out_kinds)),
            transcendentals=2 * twins * rows * heads * span * span,
        ),
    )(*inputs, info, places)


def exchange_blocks(blocks, flags):
    for i, flag in enumerate(flags):
        mask = 1 << i
        blocks = [jnp.where(flag, blocks[j ^ mask], blocks[j]) for j in range(len(blocks))]
    return blocks


def flags_of(number, bits):
    return [((number >> i) & 1) == 1 for i in range(bits)]


def split_kernel(weights, group, me_ref, *refs):
    flags = flags_of(me_ref[0], group.bit_length() - 1)
    for i in range(weights):
        cols = refs[i].shape[1] // group
        blocks = [refs[i][:, j * cols : (j + 1) * cols] for j in range(group)]
        for ref, block in zip(refs[weights:], exchange_blocks(blocks, flags)):
            ref[i] = block


def place_kernel(group, me_ref, *refs):
    flags = flags_of(me_ref[0], group.bit_length() - 1)
    out = refs[group]
    rows = refs[0].shape[1]
    for i in range(out.shape[0]):
        blocks = exchange_blocks([ref[i] for ref in refs[:group]], flags)
        for j, block in enumerate(blocks):
            out[i, j * rows : (j + 1) * rows] = block


def permuted(value, flags):
    low = value.shape[1] // 8
    blocks = [value[:, i * low : (i + 1) * low] for i in (0, 2, 1, 3, 4, 6, 5, 7)]
    for mask, flag in ((2, flags[0]), (4, flags[1])):
        blocks = [jnp.where(flag, blocks[j ^ mask], blocks[j]) for j in range(8)]
    return blocks


def restored(value, flags):
    low = value.shape[1] // 8
    blocks = [value[:, i * low : (i + 1) * low] for i in range(8)]
    for mask, flag in ((2, flags[0]), (4, flags[1])):
        blocks = [jnp.where(flag, blocks[j ^ mask], blocks[j]) for j in range(8)]
    return [blocks[i] for i in (0, 2, 1, 3, 4, 6, 5, 7)]


def move_kernel(how, me_ref, *refs):
    flags = [me_ref[0] == 1, me_ref[1] == 1]
    number = len(refs) // 2
    for source, target in zip(refs[:number], refs[number:]):
        low = source.shape[1] // 8
        for i, block in enumerate(how(source[...], flags)):
            target[:, i * low : (i + 1) * low] = block


def local_call(kernel, scalars, inputs, outputs):
    vmem = pl.BlockSpec(memory_space=pltpu.VMEM)
    size = sum(a.size * a.dtype.itemsize for a in [*inputs, *outputs])
    return pl.pallas_call(
        kernel,
        in_specs=[pl.BlockSpec(memory_space=pltpu.SMEM)] + [vmem] * len(inputs),
        out_specs=[vmem] * len(outputs),
        out_shape=outputs,
        compiler_params=pltpu.CompilerParams(vmem_limit_bytes=48 * 1024 * 1024),
        cost_estimate=pl.CostEstimate(flops=0, bytes_accessed=size, transcendentals=0),
    )(scalars, *inputs)


class Places:
    def __init__(self):
        self.dp, self.ul, self.blk = (lax.axis_size(axis) for axis in AXES)
        self.count = self.dp * self.ul * self.blk
        self.me = (
            lax.axis_index("dp") * self.ul + lax.axis_index("ulysses")
        ) * self.blk + lax.axis_index("blk")
        self.group = self.ul * self.blk
        self.half_bit = self.group // 2
        self.twin_bit = self.group
        self.far_bit = 2 * self.group
        self.inner = [1 << i for i in range(self.half_bit.bit_length() - 1)]

    def bit(self, mask):
        return (self.me // mask) % 2

    def swap(self, value, mask):
        return lax.ppermute(value, AXES, [(i, i ^ mask) for i in range(self.count)])

    def send(self, value, mask, chosen):
        return lax.ppermute(
            value, AXES, [(i, i ^ mask) for i in range(self.count) if chosen(i)]
        )

    def block(self):
        return self.bit(self.twin_bit) * self.half_bit + self.me % self.half_bit

    def members(self):
        for place in range(self.group):
            twin, low = divmod(place, self.half_bit)
            yield place, twin * self.twin_bit + low


def column_weights(at, weights):
    rows, width = weights[0].shape
    number, cols = len(weights), width // at.group
    shape = jax.ShapeDtypeStruct((number, rows, cols), bf16)
    mine = at.block().astype(jnp.int32).reshape(1)
    pieces = local_call(
        functools.partial(split_kernel, number, at.group), mine, weights, [shape] * at.group
    )
    pieces = [
        at.swap(piece, mask) if mask else piece for piece, (_, mask) in zip(pieces, at.members())
    ]
    near = local_call(
        functools.partial(place_kernel, at.group),
        mine,
        pieces,
        [jax.ShapeDtypeStruct((number, at.group * rows, cols), bf16)],
    )[0]
    half = at.swap(near, at.half_bit)
    far = at.swap(near, at.far_bit)
    far_half = at.swap(half, at.far_bit)
    return [
        jnp.concatenate([part[i] for part in (near, half, far, far_half)], axis=0)
        for i in range(number)
    ]


def gather(at, value):
    slots = {0: [value]}
    for mask in at.inner[2:]:
        for s in list(slots):
            slots[s ^ mask] = [at.swap(slots[s][0], mask)]
    cut = value.shape[0] // 2
    for s in list(slots):
        (own,) = slots[s]
        by_y = at.swap(own, 1)
        by_z = at.swap(own, 2)
        first = at.swap(by_z[:cut], 1)
        second = at.swap(by_y[cut:], 2)
        slots[s ^ 1], slots[s ^ 2] = [by_y], [by_z]
        slots[s ^ 3] = [first, second]
    whole = jnp.concatenate([part for s in range(at.half_bit) for part in slots[s]], axis=0)
    return jnp.concatenate([whole, at.swap(whole, at.twin_bit)], axis=0)


def scatter(at, terms):
    low = at.half_bit
    tok = terms.shape[0] // at.group
    kept = add_low(terms[: low * tok], at.swap(terms[low * tok :], at.twin_bit))
    slots = {s: kept[s * tok : (s + 1) * tok] for s in range(low)}
    for mask in reversed(at.inner[2:]):
        for s in [s for s in slots if s & mask]:
            slots[s ^ mask] = add_low(slots[s ^ mask], at.swap(slots.pop(s), mask))
    cut = tok // 2
    first = at.swap(slots[3][:cut], 1)
    second = at.swap(slots[3][cut:], 2)
    to_z = jnp.concatenate([add_low(slots[2][:cut], first), slots[2][cut:]])
    to_y = jnp.concatenate([slots[1][:cut], add_low(slots[1][cut:], second)])
    return (
        slots[0].astype(f32)
        + at.swap(to_y, 1).astype(f32)
        + at.swap(to_z, 2).astype(f32)
    )


def reduce_gradient(at, terms):
    rows, cols = terms.shape
    z, twin = at.bit(at.half_bit), at.bit(at.twin_bit)
    kept = add_low(terms[: rows // 2], at.swap(terms[rows // 2 :], at.far_bit))

    def away(i):
        return (i // at.half_bit) % 2 != (i // at.twin_bit) % 2

    given = at.send(kept, at.half_bit, away).reshape(2, 2, rows // 8, cols)
    both = kept.reshape(2, 2, rows // 8, cols).astype(f32) + given[::-1].astype(f32)
    second = twin == 1
    mine = jnp.where(second, both[:, 1], both[:, 0])
    twins = jnp.where(second, both[:, 0], both[:, 1]).astype(bf16)
    given = at.send(twins, at.twin_bit, lambda i: not away(i))
    out = jnp.where(z == twin, mine, given.astype(f32))
    out = jnp.where(z == 1, out[::-1], out)
    return out.reshape(rows // 4, cols)


def reduce_gains(at, terms):
    for mask in (at.far_bit, at.half_bit):
        terms = terms.reshape(terms.shape[0], 2, -1)
        terms = terms[:, 0] + at.swap(terms[:, 1], mask)
    for mask in (at.twin_bit, *reversed(at.inner)):
        terms = terms.reshape(terms.shape[0], 2, -1)
        upper = at.bit(mask) == 1
        there = jnp.where(upper, terms[:, 0], terms[:, 1])
        here = jnp.where(upper, terms[:, 1], terms[:, 0])
        terms = here + at.swap(there, mask)
    return terms


def on_device(
    tokens,
    memory,
    lengths,
    gain_attn,
    gain_memory,
    gain_ffn,
    w_query,
    w_key,
    w_value,
    w_out,
    w_gate,
    w_up,
    w_down,
    cotangent,
):
    at = Places()
    rows_here, tok_row, model_width = tokens.shape
    count = rows_here * tok_row
    group = at.group
    half = group // 2
    head_width = w_query.shape[1]
    own_width = head_width // group
    width = max(own_width, HD)
    row_length = tok_row * at.ul * at.blk
    scale = HD ** (-0.5)

    bounds = jnp.cumsum(lengths, axis=1)
    all_bounds = jnp.stack([bounds, at.swap(bounds, at.twin_bit)])
    position = at.me % group
    own_places = ((position ^ jnp.arange(half, dtype=jnp.int32))[:, None] * tok_row
                  + jnp.arange(tok_row, dtype=jnp.int32)[None]).reshape(-1)
    other_places = ((position ^ half ^ jnp.arange(half, dtype=jnp.int32))[:, None] * tok_row
                    + jnp.arange(tok_row, dtype=jnp.int32)[None]).reshape(-1)
    passed = all_bounds[:, :, None, :] <= own_places[None, None, :, None]
    starts = jnp.max(jnp.where(passed, all_bounds[:, :, None, :], 0), axis=-1)
    info = jnp.stack([starts, jnp.broadcast_to(own_places, starts.shape)], axis=-1)
    key_places = jnp.stack([own_places, other_places])
    here = position * tok_row + jnp.arange(tok_row, dtype=jnp.int32)
    valid = (here[None] < bounds[:, -1:]).astype(f32).reshape(count, 1)

    attn_w = column_weights(at, [w_query, w_key, w_value])
    sides = jnp.stack([at.bit(at.half_bit), at.bit(at.far_bit)]).astype(jnp.int32)
    entry = [a.reshape(count, model_width) for a in (memory, tokens, cotangent)] + [
        gain.reshape(1, model_width) for gain in (gain_attn, gain_memory, gain_ffn)
    ]
    memory, tokens, cotangent, gain_attn, gain_memory, gain_ffn = local_call(
        functools.partial(move_kernel, permuted),
        sides,
        entry,
        [jax.ShapeDtypeStruct(a.shape, a.dtype) for a in entry],
    )
    residual_in = tokens.astype(f32)
    token_normed, token_inverse = normalize(residual_in)
    token_in = (token_normed * gain_attn).astype(bf16)
    memory_normed, memory_inverse = normalize(memory.astype(f32))
    memory_in = (memory_normed * gain_memory).astype(bf16)
    grad_final = cotangent.astype(f32) * valid

    def widen(value):
        if own_width >= HD:
            return value
        mask = 1
        while value.shape[1] < HD:
            given = at.swap(value, mask)
            given = given.reshape(-1, 2, mask * count, given.shape[1])[:, ::-1].reshape(given.shape)
            first = at.bit(mask) == 0
            value = jnp.concatenate(
                [jnp.where(first, value, given), jnp.where(first, given, value)], axis=1
            )
            mask *= 2
        return value

    def narrow(value):
        if own_width >= HD:
            return value
        return lax.dynamic_slice_in_dim(
            value, at.me % (HD // own_width) * own_width, own_width, axis=1
        )

    def heads(value):
        return value.reshape(2, half, rows_here, tok_row, width)

    memory_all = gather(at, memory_in)
    token_all = gather(at, token_in)
    (out_w,) = column_weights(at, [w_out])

    def first_half(i):
        return (i // at.half_bit) % 2 == 0

    def second_half(i):
        return not first_half(i)

    keys = heads(widen(times(memory_all, attn_w[1], bf16)))
    values = heads(widen(times(memory_all, attn_w[2], bf16)))
    other_keys = at.send(keys, at.half_bit, first_half)
    other_values = at.send(values, at.half_bit, first_half)
    queries = heads(widen(times(token_all, attn_w[0], bf16)))
    (mixed,) = attention_call(
        functools.partial(attend_kernel, scale),
        [queries, keys, values, other_keys, other_values],
        info,
        key_places,
        [bf16],
    )
    mixed = narrow(mixed.reshape(group * count, width))

    gate_w, up_w = column_weights(at, [w_gate, w_up])
    (down_w,) = column_weights(at, [w_down])
    final_all = gather(at, grad_final.astype(bf16))

    residual = residual_in + scatter(at, times_transposed(mixed, out_w, bf16))
    ffn_normed, ffn_inverse = normalize(residual)
    ffn_in = (ffn_normed * gain_ffn).astype(bf16)
    ffn_all = gather(at, ffn_in)
    gate = times(ffn_all, gate_w)
    up = times(ffn_all, up_w)
    grad_hidden = times(final_all, down_w)
    gate_sigmoid = jax.nn.sigmoid(gate)
    silu = gate * gate_sigmoid
    hidden = (silu * up).astype(bf16)
    grad_gate_in = (
        grad_hidden * up * gate_sigmoid * (1.0 + gate * (1.0 - gate_sigmoid))
    ).astype(bf16)
    grad_up_in = (grad_hidden * silu).astype(bf16)
    grad_ffn_in = scatter(
        at,
        (times_transposed(grad_gate_in, gate_w) + times_transposed(grad_up_in, up_w)).astype(bf16),
    )
    grad_residual = grad_final + norm_back(grad_ffn_in, ffn_normed, ffn_inverse, gain_ffn)
    grad_branch = grad_residual.astype(bf16)
    branch_all = gather(at, grad_branch)
    grad_mixed = heads(widen(times(branch_all, out_w, bf16)))
    grad_queries, grad_keys, grad_values, grad_other_keys, grad_other_values = attention_call(
        functools.partial(attend_back_kernel, scale),
        [queries, keys, values, other_keys, other_values, grad_mixed],
        info,
        key_places,
        [bf16, f32, f32, bf16, bf16],
    )
    given_keys = at.send(grad_other_keys, at.half_bit, second_half)
    given_values = at.send(grad_other_values, at.half_bit, second_half)
    grad_queries = narrow(grad_queries.reshape(group * count, width))

    output = residual + scatter(at, times_transposed(hidden, down_w, bf16))

    down_term = transposed_times(final_all, hidden, bf16)
    gate_term = transposed_times(ffn_all, grad_gate_in, bf16)
    up_term = transposed_times(ffn_all, grad_up_in, bf16)
    ffn_grads = [reduce_gradient(at, term) for term in (gate_term, up_term, down_term)]

    grad_token_in = scatter(at, times_transposed(grad_queries, attn_w[0], bf16))
    grad_keys = narrow(
        (grad_keys + given_keys.astype(f32)).astype(bf16).reshape(group * count, width)
    )
    grad_values = narrow(
        (grad_values + given_values.astype(f32)).astype(bf16).reshape(group * count, width)
    )
    grad_memory_in = scatter(
        at,
        (
            times_transposed(grad_keys, attn_w[1]) + times_transposed(grad_values, attn_w[2])
        ).astype(bf16),
    )
    query_term = transposed_times(token_all, grad_queries, bf16)
    out_term = transposed_times(branch_all, mixed, bf16)
    key_term = transposed_times(memory_all, grad_keys, bf16)
    value_term = transposed_times(memory_all, grad_values, bf16)
    attn_grads = [
        reduce_gradient(at, term) for term in (query_term, key_term, value_term, out_term)
    ]

    def against(term, weight):
        return jnp.sum(term.astype(f32) * weight.astype(f32), axis=1)

    gain_terms = jnp.stack(
        [
            against(query_term, attn_w[0]) / gain_attn[0],
            (against(key_term, attn_w[1]) + against(value_term, attn_w[2])) / gain_memory[0],
            (against(gate_term, gate_w) + against(up_term, up_w)) / gain_ffn[0],
        ]
    )
    gain_grads = reduce_gains(at, gain_terms)

    grad_tokens = grad_residual + norm_back(grad_token_in, token_normed, token_inverse, gain_attn)
    grad_memory = norm_back(grad_memory_in, memory_normed, memory_inverse, gain_memory)
    leaving = [a.astype(bf16) for a in (output, grad_tokens, grad_memory)]
    leaving = local_call(
        functools.partial(move_kernel, restored),
        sides,
        leaving,
        [jax.ShapeDtypeStruct(a.shape, a.dtype) for a in leaving],
    )
    output, grad_tokens, grad_memory = (
        a.reshape(rows_here, tok_row, model_width) for a in leaving
    )
    return (
        output,
        grad_tokens,
        grad_memory,
        gain_grads[0],
        gain_grads[1],
        gain_grads[2],
        attn_grads[0],
        attn_grads[1],
        attn_grads[2],
        attn_grads[3],
        ffn_grads[0],
        ffn_grads[1],
        ffn_grads[2],
    )


def solution(mesh):
    rows = P("dp", ("ulysses", "blk"), None)
    weight = P(AXES, None)
    grad = P("dp", ("ulysses", "blk"))
    return jax.shard_map(
        on_device,
        mesh=mesh,
        in_specs=(rows, rows, P("dp", None), P(), P(), P()) + (weight,) * 7 + (rows,),
        out_specs=(rows,) * 3 + (P(AXES),) * 3 + (grad,) * 7,
        check_vma=False,
    )
```

profile of v0, /device:TPU:0, one launch (start us, length us, event | category | flops | bytes accessed | tf_op | source)
XLA Modules:
  0.0 900.6 jit_solution(2381266586174570648)
XLA Ops:
  22.0 7.6 collective-permute-done.5.refs_1_
  47.0 4.8 collective-permute-done.23.refs_1_
  52.2 4.9 collective-permute-done.17
  81.0 28.1 %collective-permute-done.12 = bf16[3,512,256]{2,1,0:T(8,128)(2,1)S(1)} collective-permute-done((bf16[3,512,256]{2,1,0:T(8,128)(2,1)S(1)}, bf16[3,512,256]{2,1,0:T(8,128)(2,1)S(1)}, u32[]{:S(2)}, u32[]{:S(2)}) %collective-permute-start.12) | collective-permute-done | bytes 786464 | tf_op jit(solution)/shard_map/ppermute | solution.py:231
  116.7 12.8 %collective-permute-done.14 = bf16[3,512,256]{2,1,0:T(8,128)(2,1)S(1)} collective-permute-done((bf16[3,512,256]{2,1,0:T(8,128)(2,1)S(1)}, bf16[3,512,256]{2,1,0:T(8,128)(2,1)S(1)}, u32[]{:S(2)}, u32[]{:S(2)}) %collective-permute-start.14) | collective-permute-done | bytes 786464 | tf_op jit(solution)/shard_map/ppermute | solution.py:231
  137.9 7.1 collective-permute-done.20.ko_ref
  144.9 8.3 collective-permute-done.21.vo_ref
  153.2 6.2 shard_map.240
  163.4 24.0 %collective-permute-start.54 = (bf16[1,64,688]{2,1,0:T(8,128)(2,1)S(1)}, bf16[1,64,688]{2,1,0:T(8,128)(2,1)S(1)}, u32[]{:S(2)}, u32[]{:S(2)}) collective-permute-start(bf16[1,64,688]{2,1,0:T(8,128)(2,1)S(1)} %get-tuple-element.90), channel_id=1, source_target_pairs={{0,2},{1,3},{2,0},{3,1},{4,6},{5,7},{6,4},{7,5},{8,10},{9,11},{10,... | collective-permute-start | bytes 264200 | tf_op jit(solution)/shard_map/ppermute | solution.py:231
  211.8 12.3 %collective-permute-done.43.refs_1_ = bf16[2,64,688]{2,1,0:T(8,128)(2,1)S(1)} collective-permute-done((bf16[2,64,688]{2,1,0:T(8,128)(2,1)S(1)}, bf16[2,64,688]{2,1,0:T(8,128)(2,1)S(1)}, u32[]{:S(2)}, u32[]{:S(2)}) %collective-permute-start.43) | collective-permute-done | bytes 176160 | tf_op jit(solution)/shard_map/ppermute | solution.py:231
  269.4 22.9 %collective-permute-done.71 = bf16[64,2048]{1,0:T(8,128)(2,1)S(1)} collective-permute-done((bf16[64,2048]{1,0:T(8,128)(2,1)S(1)}, bf16[64,2048]{1,0:T(8,128)(2,1)S(1)}, u32[]{:S(2)}, u32[]{:S(2)}) %collective-permute-start.71) | collective-permute-done | bytes 262176 | tf_op jit(solution)/shard_map/ppermute | solution.py:231
  293.2 7.7 collective-permute-done.39
  307.4 3.8 collective-permute-start.60
  311.2 6.0 collective-permute-done.41
  321.2 24.2 %collective-permute-done.60 = bf16[1,512,688]{1,2,0:T(8,128)(2,1)} collective-permute-done((bf16[1,512,688]{1,2,0:T(8,128)(2,1)}, bf16[1,512,688]{1,2,0:T(8,128)(2,1)}, u32[]{:S(2)}, u32[]{:S(2)}) %collective-permute-start.60) | collective-permute-done | bytes 704544 | tf_op jit(solution)/shard_map/ppermute | solution.py:231
  353.2 13.1 %collective-permute-done.62 = bf16[1,512,688]{1,2,0:T(8,128)(2,1)} collective-permute-done((bf16[1,512,688]{1,2,0:T(8,128)(2,1)}, bf16[1,512,688]{1,2,0:T(8,128)(2,1)}, u32[]{:S(2)}, u32[]{:S(2)}) %collective-permute-start.62) | collective-permute-done | bytes 704544 | tf_op jit(solution)/shard_map/ppermute | solution.py:231
  383.1 12.6 %collective-permute-done.52 = bf16[2,512,688]{1,2,0:T(8,128)(2,1)} collective-permute-done((bf16[2,512,688]{1,2,0:T(8,128)(2,1)}, bf16[2,512,688]{1,2,0:T(8,128)(2,1)}, u32[]{:S(2)}, u32[]{:S(2)}) %collective-permute-start.52) | collective-permute-done | bytes 1409056 | tf_op jit(solution)/shard_map/ppermute | solution.py:231
  406.3 7.1 fusion.51
  413.4 4.8 fusion.53
  418.2 6.8 multiply_convert_fusion
  428.4 6.5 fusion.28
  438.4 8.5 fusion.52
  458.4 10.0 %add_convert_fusion.1 = bf16[1024,2048]{1,0:T(8,128)(2,1)} fusion(f32[1024,2048]{1,0:T(8,128)} %fusion.52, bf16[1024,688]{0,1:T(8,128)(2,1)S(1)} %get-tuple-element.118, bf16[512,688]{1,0:T(8,128)(2,1)S(1)} %bitcast.273, bf16[512,688]{1,0:T(8,128)(2,1)S(1)} %bitcast.264, bf16[512,688]{1,0:T(8,128)(2,1)S(1)} %bitcast.267, bf16[512,688]{1,0:T(8,128)(2,1)S(1)} %copy-done.82), kind=kOutput, calls=%fused_computation.1 | convolution fusion | flops 2901147648 | bytes 16809984 | tf_op jit(solution)/shard_map/dot_general | solution.py:20
  468.4 4.6 copy.180
  485.0 55.8 %collective-permute-done.112 = bf16[1024,688]{0,1:T(8,128)(2,1)} collective-permute-done((bf16[1024,688]{0,1:T(8,128)(2,1)}, bf16[1024,688]{0,1:T(8,128)(2,1)}, u32[]{:S(2)}, u32[]{:S(2)}) %collective-permute-start.112) | collective-permute-done | bytes 1409056 | tf_op jit(solution)/shard_map/ppermute | solution.py:231
  553.7 4.8 reshape.408
  563.3 5.0 reshape.409
  586.4 5.3 collective-permute-done.74
  594.5 46.8 %collective-permute-done.119 = bf16[1024,688]{0,1:T(8,128)(2,1)} collective-permute-done((bf16[1024,688]{0,1:T(8,128)(2,1)}, bf16[1024,688]{0,1:T(8,128)(2,1)}, u32[]{:S(2)}, u32[]{:S(2)}) %collective-permute-start.119) | collective-permute-done | bytes 1409056 | tf_op jit(solution)/shard_map/ppermute | solution.py:234
  641.3 4.6 reshape.400
  648.5 4.6 reshape.398
  655.8 4.6 reshape.396
  662.7 7.9 collective-permute-start.114
  679.9 10.5 %collective-permute-done.79 = bf16[128,2048]{1,0:T(8,128)(2,1)S(1)} collective-permute-done((bf16[128,2048]{1,0:T(8,128)(2,1)S(1)}, bf16[128,2048]{1,0:T(8,128)(2,1)S(1)}, u32[]{:S(2)}, u32[]{:S(2)}) %collective-permute-start.79) | collective-permute-done | bytes 524320 | tf_op jit(solution)/shard_map/ppermute | solution.py:231
  692.8 4.7 collective-permute-done.80
  710.3 9.6 %shard_map.247 = (bf16[2,4,2,64,256]{4,3,2,1,0:T(8,128)(2,1)S(1)}, f32[2,4,2,64,256]{4,3,2,1,0:T(8,128)}, f32[2,4,2,64,256]{4,3,2,1,0:T(8,128)}, bf16[2,4,2,64,2...) custom-call(bf16[2,4,2,64,256]{4,3,2,1,0:T(8,128)(2,1)S(1)} %bitcast.248, ...), custom_call_target="tpu_custom_call" | custom-call | flops 1610612736 | bytes 5767168 | tf_op jit(solution)/shard_map/pallas_call | solution.py:127
  725.5 44.2 %collective-permute-done.89 = bf16[2,4,2,64,256]{4,3,2,1,0:T(8,128)(2,1)S(1)} collective-permute-done((bf16[2,4,2,64,256]{4,3,2,1,0:T(8,128)(2,1)S(1)}, bf16[2,4,2,64,256]{4,3,2,1,0:T(8,128)(2,1)S(1)}, u32[]{:S(2)}, u32[]{:S(2)}) %collective-permute-start.89) | collective-permute-done | bytes 524320 | tf_op jit(solution)/shard_map/ppermute | solution.py:234
  783.8 5.6 fusion.46
  790.1 5.1 collective-permute-done.109
  798.0 6.1 collective-permute-done.100
  813.5 4.9 add_convert_fusion
  828.5 4.5 collective-permute-done.106
  837.7 15.0 %collective-permute-done.104 = bf16[1024,256]{1,0:T(8,128)(2,1)S(1)} collective-permute-done((bf16[1024,256]{1,0:T(8,128)(2,1)S(1)}, bf16[1024,256]{1,0:T(8,128)(2,1)S(1)}, u32[]{:S(2)}, u32[]{:S(2)}) %collective-permute-start.104) | collective-permute-done | bytes 524320 | tf_op jit(solution)/shard_map/ppermute | solution.py:234
  854.5 3.8 collective-permute-done.107
  864.2 6.1 collective-permute-done.86
  877.1 5.0 collective-permute-done.93
  886.3 4.8 collective-permute-done.87
  891.1 5.6 collective-permute-done.94
  (741 shorter events, 367.2 us)
Async XLA Ops:
  8.8 31.0 %collective-permute-start.16 = (bf16[128,2048]{1,0:T(8,128)(2,1)}, bf16[128,2048]{1,0:T(8,128)(2,1)}, u32[]{:S(2)}, u32[]{:S(2)}) collective-permute-start(bf16[128,2048]{1,0:T(8,128)(2,1)} %get-tuple-element.115), channel_id=1, source_target_pairs={{0,2},{1,3},{2,0},{3,1},{4,6},{5,7},{6,4},{7,5},{8,10},{9,11},{10,... | collective-permute-start | bytes 1572872 | tf_op jit(solution)/shard_map/ppermute | solution.py:231
  11.9 29.6 %collective-permute-start.15 = (bf16[128,2048]{1,0:T(8,128)(2,1)}, bf16[128,2048]{1,0:T(8,128)(2,1)}, u32[]{:S(2)}, u32[]{:S(2)}) collective-permute-start(bf16[128,2048]{1,0:T(8,128)(2,1)} %get-tuple-element.115), channel_id=1, source_target_pairs={{0,1},{1,0},{2,3},{3,2},{4,5},{5,4},{6,7},{7,6},{8,9},{9,8},{10,11... | collective-permute-start | bytes 1572872 | tf_op jit(solution)/shard_map/ppermute | solution.py:231
  34.3 36.9 %collective-permute-start.1 = (bf16[128,2048]{1,0:T(8,128)(2,1)}, bf16[128,2048]{1,0:T(8,128)(2,1)S(1)}, u32[]{:S(2)}, u32[]{:S(2)}) collective-permute-start(bf16[128,2048]{1,0:T(8,128)(2,1)} %copy-done.86), channel_id=1, source_target_pairs={{0,2},{1,3},{2,0},{3,1},{4,6},{5,7},{6,4},{7,5},{8,10},{9,11},{10,... | collective-permute-start | bytes 1572872 | tf_op jit(solution)/shard_map/ppermute | solution.py:231
  36.2 36.1 %collective-permute-start = (bf16[128,2048]{1,0:T(8,128)(2,1)}, bf16[128,2048]{1,0:T(8,128)(2,1)S(1)}, u32[]{:S(2)}, u32[]{:S(2)}) collective-permute-start(bf16[128,2048]{1,0:T(8,128)(2,1)} %copy-done.86), channel_id=1, source_target_pairs={{0,1},{1,0},{2,3},{3,2},{4,5},{5,4},{6,7},{7,6},{8,9},{9,8},{10,11... | collective-permute-start | bytes 1572872 | tf_op jit(solution)/shard_map/ppermute | solution.py:231
  65.3 43.8 %collective-permute-start.12 = (bf16[3,512,256]{2,1,0:T(8,128)(2,1)S(1)}, bf16[3,512,256]{2,1,0:T(8,128)(2,1)S(1)}, u32[]{:S(2)}, u32[]{:S(2)}) collective-permute-start(bf16[3,512,256]{2,1,0:T(8,128)(2,1)S(1)} %shard_map.239), channel_id=1, source_target_pairs={{0,4},{1,5},{2,6},{3,7},{4,0},{5,1},{6,2},{7,3},{8,12},{9,13},{10,... | collective-permute-start | bytes 2359304 | tf_op jit(solution)/shard_map/ppermute | solution.py:231
  67.9 61.7 %collective-permute-start.19 = (bf16[512,2048]{1,0:T(8,128)(2,1)}, bf16[512,2048]{1,0:T(8,128)(2,1)S(1)}, u32[]{:S(2)}, u32[]{:S(2)}) collective-permute-start(bf16[512,2048]{1,0:T(8,128)(2,1)} %get-tuple-element.205), channel_id=1, source_target_pairs={{0,8},{1,9},{2,10},{3,11},{4,12},{5,13},{6,14},{7,15},{8,0},{9,1},... | collective-permute-start | bytes 6291464 | tf_op jit(solution)/shard_map/ppermute | solution.py:231
  68.8 45.7 %collective-permute-start.30 = (bf16[1,512,256]{2,1,0:T(8,128)(2,1)S(1)}, bf16[1,512,256]{2,1,0:T(8,128)(2,1)S(1)}, u32[]{:S(2)}, u32[]{:S(2)}) collective-permute-start(bf16[1,512,256]{2,1,0:T(8,128)(2,1)S(1)} %shard_map.242), channel_id=1, source_target_pairs={{0,4},{1,5},{2,6},{3,7},{4,0},{5,1},{6,2},{7,3},{8,12},{9,13},{10,... | collective-permute-start | bytes 786440 | tf_op jit(solution)/shard_map/ppermute | solution.py:231
  72.3 38.3 %collective-permute-start.3 = (bf16[64,2048]{1,0:T(8,128)(2,1)S(1)}, bf16[64,2048]{1,0:T(8,128)(2,1)S(1)}, u32[]{:S(2)}, u32[]{:S(2)}) collective-permute-start(bf16[64,2048]{1,0:T(8,128)(2,1)S(1)} %slice.534), channel_id=1, source_target_pairs={{0,2},{1,3},{2,0},{3,1},{4,6},{5,7},{6,4},{7,5},{8,10},{9,11},{10,... | collective-permute-start | bytes 786440 | tf_op jit(solution)/shard_map/ppermute | solution.py:231
  78.8 37.3 %collective-permute-start.13 = (bf16[3,512,256]{2,1,0:T(8,128)(2,1)S(1)}, bf16[3,512,256]{2,1,0:T(8,128)(2,1)S(1)}, u32[]{:S(2)}, u32[]{:S(2)}) collective-permute-start(bf16[3,512,256]{2,1,0:T(8,128)(2,1)S(1)} %shard_map.239), channel_id=1, source_target_pairs={{0,16},{1,17},{2,18},{3,19},{4,20},{5,21},{6,22},{7,23},{8,24},{9,... | collective-permute-start | bytes 2359304 | tf_op jit(solution)/shard_map/ppermute | solution.py:231
  111.3 24.4 %collective-permute-start.4 = (bf16[512,2048]{1,0:T(8,128)(2,1)S(1)}, bf16[512,2048]{1,0:T(8,128)(2,1)S(1)}, u32[]{:S(2)}, u32[]{:S(2)}) collective-permute-start(bf16[512,2048]{1,0:T(8,128)(2,1)S(1)} %get-tuple-element.209), channel_id=1, source_target_pairs={{0,8},{1,9},{2,10},{3,11},{4,12},{5,13},{6,14},{7,15},{8,0},{9,1},... | collective-permute-start | bytes 6291464 | tf_op jit(solution)/shard_map/ppermute | solution.py:231
  114.6 44.8 %collective-permute-start.31 = (bf16[1,512,256]{2,1,0:T(8,128)(2,1)S(1)}, bf16[1,512,256]{2,1,0:T(8,128)(2,1)S(1)}, u32[]{:S(2)}, u32[]{:S(2)}) collective-permute-start(bf16[1,512,256]{2,1,0:T(8,128)(2,1)S(1)} %shard_map.242), channel_id=1, source_target_pairs={{0,16},{1,17},{2,18},{3,19},{4,20},{5,21},{6,22},{7,23},{8,24},{9,... | collective-permute-start | bytes 786440 | tf_op jit(solution)/shard_map/ppermute | solution.py:231
  116.1 43.3 %collective-permute-start.32 = (bf16[1,512,256]{2,1,0:T(8,128)(2,1)S(1)}, bf16[1,512,256]{2,1,0:T(8,128)(2,1)S(1)}, u32[]{:S(2)}, u32[]{:S(2)}) collective-permute-start(bf16[1,512,256]{2,1,0:T(8,128)(2,1)S(1)} %collective-permute-done.30), channel_id=1, source_target_pairs={{0,16},{1,17},{2,18},{3,19},{4,20},{5,21},{6,22},{7,23},{8,24},{9,... | collective-permute-start | bytes 786440 | tf_op jit(solution)/shard_map/ppermute | solution.py:231
  162.4 26.7 %collective-permute-start.33 = (bf16[512,2048]{1,0:T(8,128)(2,1)}, bf16[512,2048]{1,0:T(8,128)(2,1)}, u32[]{:S(2)}, u32[]{:S(2)}) collective-permute-start(bf16[512,2048]{1,0:T(8,128)(2,1)} %slice.550), channel_id=1, source_target_pairs={{0,8},{1,9},{2,10},{3,11},{4,12},{5,13},{6,14},{7,15},{8,0},{9,1},... | collective-permute-start | bytes 6291464 | tf_op jit(solution)/shard_map/ppermute | solution.py:231
  163.4 34.2 %collective-permute-start.53 = (bf16[1,64,688]{2,1,0:T(8,128)(2,1)S(1)}, bf16[1,64,688]{2,1,0:T(8,128)(2,1)S(1)}, u32[]{:S(2)}, u32[]{:S(2)}) collective-permute-start(bf16[1,64,688]{2,1,0:T(8,128)(2,1)S(1)} %get-tuple-element.89), channel_id=1, source_target_pairs={{0,1},{1,0},{2,3},{3,2},{4,5},{5,4},{6,7},{7,6},{8,9},{9,8},{10,11... | collective-permute-start | bytes 264200 | tf_op jit(solution)/shard_map/ppermute | solution.py:231
  163.4 34.2 %collective-permute-start.54 = (bf16[1,64,688]{2,1,0:T(8,128)(2,1)S(1)}, bf16[1,64,688]{2,1,0:T(8,128)(2,1)S(1)}, u32[]{:S(2)}, u32[]{:S(2)}) collective-permute-start(bf16[1,64,688]{2,1,0:T(8,128)(2,1)S(1)} %get-tuple-element.90), channel_id=1, source_target_pairs={{0,2},{1,3},{2,0},{3,1},{4,6},{5,7},{6,4},{7,5},{8,10},{9,11},{10,... | collective-permute-start | bytes 264200 | tf_op jit(solution)/shard_map/ppermute | solution.py:231
  202.5 49.2 %collective-permute-start.69 = (bf16[128,2048]{1,0:T(8,128)(2,1)}, bf16[128,2048]{1,0:T(8,128)(2,1)}, u32[]{:S(2)}, u32[]{:S(2)}) collective-permute-start(bf16[128,2048]{1,0:T(8,128)(2,1)} %get-tuple-element.109), channel_id=1, source_target_pairs={{0,2},{1,3},{2,0},{3,1},{4,6},{5,7},{6,4},{7,5},{8,10},{9,11},{10,... | collective-permute-start | bytes 1572872 | tf_op jit(solution)/shard_map/ppermute | solution.py:231
  204.3 51.8 %collective-permute-start.68 = (bf16[128,2048]{1,0:T(8,128)(2,1)}, bf16[128,2048]{1,0:T(8,128)(2,1)}, u32[]{:S(2)}, u32[]{:S(2)}) collective-permute-start(bf16[128,2048]{1,0:T(8,128)(2,1)} %get-tuple-element.109), channel_id=1, source_target_pairs={{0,1},{1,0},{2,3},{3,2},{4,5},{5,4},{6,7},{7,6},{8,9},{9,8},{10,11... | collective-permute-start | bytes 1572872 | tf_op jit(solution)/shard_map/ppermute | solution.py:231
  232.2 30.2 %collective-permute-start.37 = (bf16[128,2048]{1,0:T(8,128)(2,1)}, bf16[128,2048]{1,0:T(8,128)(2,1)}, u32[]{:S(2)}, u32[]{:S(2)}) collective-permute-start(bf16[128,2048]{1,0:T(8,128)(2,1)} %pad_maximum_fusion.10), channel_id=1, source_target_pairs={{0,2},{1,3},{2,0},{3,1},{4,6},{5,7},{6,4},{7,5},{8,10},{9,11},{10,... | collective-permute-start | bytes 1572872 | tf_op jit(solution)/shard_map/ppermute | solution.py:231
  235.3 27.6 %collective-permute-start.35 = (bf16[128,2048]{1,0:T(8,128)(2,1)}, bf16[128,2048]{1,0:T(8,128)(2,1)}, u32[]{:S(2)}, u32[]{:S(2)}) collective-permute-start(bf16[128,2048]{1,0:T(8,128)(2,1)} %pad_maximum_fusion.9), channel_id=1, source_target_pairs={{0,1},{1,0},{2,3},{3,2},{4,5},{5,4},{6,7},{7,6},{8,9},{9,8},{10,11... | collective-permute-start | bytes 1572872 | tf_op jit(solution)/shard_map/ppermute | solution.py:231
  240.7 80.5 %collective-permute-start.61 = (bf16[1,512,688]{1,2,0:T(8,128)(2,1)}, bf16[1,512,688]{1,2,0:T(8,128)(2,1)}, u32[]{:S(2)}, u32[]{:S(2)}) collective-permute-start(bf16[1,512,688]{1,2,0:T(8,128)(2,1)} %copy.174), channel_id=1, source_target_pairs={{0,16},{1,17},{2,18},{3,19},{4,20},{5,21},{6,22},{7,23},{8,24},{9,... | collective-permute-start | bytes 2113544 | tf_op jit(solution)/shard_map/ppermute | solution.py:231
  251.7 94.2 %collective-permute-start.50 = (bf16[2,512,688]{1,2,0:T(8,128)(2,1)}, bf16[2,512,688]{1,2,0:T(8,128)(2,1)}, u32[]{:S(2)}, u32[]{:S(2)}) collective-permute-start(bf16[2,512,688]{1,2,0:T(8,128)(2,1)} %copy.166), channel_id=1, source_target_pairs={{0,4},{1,5},{2,6},{3,7},{4,0},{5,1},{6,2},{7,3},{8,12},{9,13},{10,... | collective-permute-start | bytes 4227080 | tf_op jit(solution)/shard_map/ppermute | solution.py:231
  262.5 29.8 %collective-permute-start.71 = (bf16[64,2048]{1,0:T(8,128)(2,1)S(1)}, bf16[64,2048]{1,0:T(8,128)(2,1)S(1)}, u32[]{:S(2)}, u32[]{:S(2)}) collective-permute-start(bf16[64,2048]{1,0:T(8,128)(2,1)S(1)} %slice.578), channel_id=1, source_target_pairs={{0,2},{1,3},{2,0},{3,1},{4,6},{5,7},{6,4},{7,5},{8,10},{9,11},{10,... | collective-permute-start | bytes 786440 | tf_op jit(solution)/shard_map/ppermute | solution.py:231
  265.9 35.1 %collective-permute-start.39 = (bf16[128,2048]{1,0:T(8,128)(2,1)S(1)}, bf16[128,2048]{1,0:T(8,128)(2,1)S(1)}, u32[]{:S(2)}, u32[]{:S(2)}) collective-permute-start(bf16[128,2048]{1,0:T(8,128)(2,1)S(1)} %get-tuple-element.111), channel_id=1, source_target_pairs={{0,2},{1,3},{2,0},{3,1},{4,6},{5,7},{6,4},{7,5},{8,10},{9,11},{10,... | collective-permute-start | bytes 1572872 | tf_op jit(solution)/shard_map/ppermute | solution.py:231
  267.5 34.0 %collective-permute-start.38 = (bf16[128,2048]{1,0:T(8,128)(2,1)S(1)}, bf16[128,2048]{1,0:T(8,128)(2,1)S(1)}, u32[]{:S(2)}, u32[]{:S(2)}) collective-permute-start(bf16[128,2048]{1,0:T(8,128)(2,1)S(1)} %get-tuple-element.111), channel_id=1, source_target_pairs={{0,1},{1,0},{2,3},{3,2},{4,5},{5,4},{6,7},{7,6},{8,9},{9,8},{10,11... | collective-permute-start | bytes 1572872 | tf_op jit(solution)/shard_map/ppermute | solution.py:231
  293.2 86.7 %collective-permute-start.72 = (bf16[512,2048]{1,0:T(8,128)(2,1)}, bf16[512,2048]{1,0:T(8,128)(2,1)}, u32[]{:S(2)}, u32[]{:S(2)}) collective-permute-start(bf16[512,2048]{1,0:T(8,128)(2,1)} %get-tuple-element.197), channel_id=1, source_target_pairs={{0,8},{1,9},{2,10},{3,11},{4,12},{5,13},{6,14},{7,15},{8,0},{9,1},... | collective-permute-start | bytes 6291464 | tf_op jit(solution)/shard_map/ppermute | solution.py:231
  307.4 37.9 %collective-permute-start.60 = (bf16[1,512,688]{1,2,0:T(8,128)(2,1)}, bf16[1,512,688]{1,2,0:T(8,128)(2,1)}, u32[]{:S(2)}, u32[]{:S(2)}) collective-permute-start(bf16[1,512,688]{1,2,0:T(8,128)(2,1)} %copy.174), channel_id=1, source_target_pairs={{0,4},{1,5},{2,6},{3,7},{4,0},{5,1},{6,2},{7,3},{8,12},{9,13},{10,... | collective-permute-start | bytes 2113544 | tf_op jit(solution)/shard_map/ppermute | solution.py:231
  317.2 51.4 %collective-permute-start.51 = (bf16[2,512,688]{1,2,0:T(8,128)(2,1)}, bf16[2,512,688]{1,2,0:T(8,128)(2,1)}, u32[]{:S(2)}, u32[]{:S(2)}) collective-permute-start(bf16[2,512,688]{1,2,0:T(8,128)(2,1)} %copy.166), channel_id=1, source_target_pairs={{0,16},{1,17},{2,18},{3,19},{4,20},{5,21},{6,22},{7,23},{8,24},{9,... | collective-permute-start | bytes 4227080 | tf_op jit(solution)/shard_map/ppermute | solution.py:231
  321.2 81.7 %collective-permute-start.42 = (bf16[512,2048]{1,0:T(8,128)(2,1)}, bf16[512,2048]{1,0:T(8,128)(2,1)}, u32[]{:S(2)}, u32[]{:S(2)}) collective-permute-start(bf16[512,2048]{1,0:T(8,128)(2,1)} %get-tuple-element.201), channel_id=1, source_target_pairs={{0,8},{1,9},{2,10},{3,11},{4,12},{5,13},{6,14},{7,15},{8,0},{9,1},... | collective-permute-start | bytes 6291464 | tf_op jit(solution)/shard_map/ppermute | solution.py:231
  345.9 49.8 %collective-permute-start.52 = (bf16[2,512,688]{1,2,0:T(8,128)(2,1)}, bf16[2,512,688]{1,2,0:T(8,128)(2,1)}, u32[]{:S(2)}, u32[]{:S(2)}) collective-permute-start(bf16[2,512,688]{1,2,0:T(8,128)(2,1)} %collective-permute-done.50), channel_id=1, source_target_pairs={{0,16},{1,17},{2,18},{3,19},{4,20},{5,21},{6,22},{7,23},{8,24},{9,... | collective-permute-start | bytes 4227080 | tf_op jit(solution)/shard_map/ppermute | solution.py:231
  448.1 110.4 %collective-permute-start.118 = (bf16[1024,688]{0,1:T(8,128)(2,1)}, bf16[1024,688]{0,1:T(8,128)(2,1)}, u32[]{:S(2)}, u32[]{:S(2)}) collective-permute-start(bf16[1024,688]{0,1:T(8,128)(2,1)} %slice.643), channel_id=1, source_target_pairs={{0,16},{1,17},{2,18},{3,19},{4,20},{5,21},{6,22},{7,23},{8,24},{9,... | collective-permute-start | bytes 4227080 | tf_op jit(solution)/shard_map/ppermute | solution.py:231
  450.1 118.2 %collective-permute-start.63 = (bf16[512,2048]{1,0:T(8,128)(2,1)}, bf16[512,2048]{1,0:T(8,128)(2,1)}, u32[]{:S(2)}, u32[]{:S(2)}) collective-permute-start(bf16[512,2048]{1,0:T(8,128)(2,1)} %slice.569), channel_id=1, source_target_pairs={{0,8},{1,9},{2,10},{3,11},{4,12},{5,13},{6,14},{7,15},{8,0},{9,1},... | collective-permute-start | bytes 6291464 | tf_op jit(solution)/shard_map/ppermute | solution.py:231
  456.4 92.6 %collective-permute-start.115 = (bf16[1024,688]{0,1:T(8,128)(2,1)}, bf16[1024,688]{0,1:T(8,128)(2,1)}, u32[]{:S(2)}, u32[]{:S(2)}) collective-permute-start(bf16[1024,688]{0,1:T(8,128)(2,1)} %slice.639), channel_id=1, source_target_pairs={{0,16},{1,17},{2,18},{3,19},{4,20},{5,21},{6,22},{7,23},{8,24},{9,... | collective-permute-start | bytes 4227080 | tf_op jit(solution)/shard_map/ppermute | solution.py:231
  457.8 83.0 %collective-permute-start.112 = (bf16[1024,688]{0,1:T(8,128)(2,1)}, bf16[1024,688]{0,1:T(8,128)(2,1)}, u32[]{:S(2)}, u32[]{:S(2)}) collective-permute-start(bf16[1024,688]{0,1:T(8,128)(2,1)} %slice.635), channel_id=1, source_target_pairs={{0,16},{1,17},{2,18},{3,19},{4,20},{5,21},{6,22},{7,23},{8,24},{9,... | collective-permute-start | bytes 4227080 | tf_op jit(solution)/shard_map/ppermute | solution.py:231
  482.4 90.2 %collective-permute-start.73 = (bf16[512,2048]{1,0:T(8,128)(2,1)}, bf16[512,2048]{1,0:T(8,128)(2,1)}, u32[]{:S(2)}, u32[]{:S(2)}) collective-permute-start(bf16[512,2048]{1,0:T(8,128)(2,1)} %slice.580), channel_id=1, source_target_pairs={{0,8},{1,9},{2,10},{3,11},{4,12},{5,13},{6,14},{7,15},{8,0},{9,1},... | collective-permute-start | bytes 6291464 | tf_op jit(solution)/shard_map/ppermute | solution.py:231
  543.9 111.9 %collective-permute-start.113 = (bf16[1024,688]{0,1:T(8,128)(2,1)}, bf16[1024,688]{0,1:T(8,128)(2,1)}, u32[]{:S(2)}, u32[]{:S(2)}) collective-permute-start(bf16[1024,688]{0,1:T(8,128)(2,1)} %add_convert_fusion.9), channel_id=1, source_target_pairs={{4,0},{5,1},{6,2},{7,3},{8,12},{9,13},{10,14},{11,15},{20,16},{21,... | collective-permute-start | bytes 4227080 | tf_op jit(solution)/shard_map/ppermute | solution.py:234
  552.4 96.1 %collective-permute-start.116 = (bf16[1024,688]{0,1:T(8,128)(2,1)}, bf16[1024,688]{0,1:T(8,128)(2,1)}, u32[]{:S(2)}, u32[]{:S(2)}) collective-permute-start(bf16[1024,688]{0,1:T(8,128)(2,1)} %add_convert_fusion.8), channel_id=1, source_target_pairs={{4,0},{5,1},{6,2},{7,3},{8,12},{9,13},{10,14},{11,15},{20,16},{21,... | collective-permute-start | bytes 4227080 | tf_op jit(solution)/shard_map/ppermute | solution.py:234
  562.0 79.3 %collective-permute-start.119 = (bf16[1024,688]{0,1:T(8,128)(2,1)}, bf16[1024,688]{0,1:T(8,128)(2,1)}, u32[]{:S(2)}, u32[]{:S(2)}) collective-permute-start(bf16[1024,688]{0,1:T(8,128)(2,1)} %add_convert_fusion.7), channel_id=1, source_target_pairs={{4,0},{5,1},{6,2},{7,3},{8,12},{9,13},{10,14},{11,15},{20,16},{21,... | collective-permute-start | bytes 4227080 | tf_op jit(solution)/shard_map/ppermute | solution.py:234
  585.1 86.2 %collective-permute-start.67 = (bf16[128,2048]{1,0:T(8,128)(2,1)}, bf16[128,2048]{1,0:T(8,128)(2,1)}, u32[]{:S(2)}, u32[]{:S(2)}) collective-permute-start(bf16[128,2048]{1,0:T(8,128)(2,1)} %pad_maximum_fusion.12), channel_id=1, source_target_pairs={{0,2},{1,3},{2,0},{3,1},{4,6},{5,7},{6,4},{7,5},{8,10},{9,11},{10,... | collective-permute-start | bytes 1572872 | tf_op jit(solution)/shard_map/ppermute | solution.py:231
  591.6 81.3 %collective-permute-start.65 = (bf16[128,2048]{1,0:T(8,128)(2,1)}, bf16[128,2048]{1,0:T(8,128)(2,1)}, u32[]{:S(2)}, u32[]{:S(2)}) collective-permute-start(bf16[128,2048]{1,0:T(8,128)(2,1)} %pad_maximum_fusion.11), channel_id=1, source_target_pairs={{0,1},{1,0},{2,3},{3,2},{4,5},{5,4},{6,7},{7,6},{8,9},{9,8},{10,11... | collective-permute-start | bytes 1572872 | tf_op jit(solution)/shard_map/ppermute | solution.py:231
  641.3 31.7 %collective-permute-start.77 = (bf16[128,2048]{1,0:T(8,128)(2,1)}, bf16[128,2048]{1,0:T(8,128)(2,1)}, u32[]{:S(2)}, u32[]{:S(2)}) collective-permute-start(bf16[128,2048]{1,0:T(8,128)(2,1)} %pad_maximum_fusion.14), channel_id=1, source_target_pairs={{0,2},{1,3},{2,0},{3,1},{4,6},{5,7},{6,4},{7,5},{8,10},{9,11},{10,... | collective-permute-start | bytes 1572872 | tf_op jit(solution)/shard_map/ppermute | solution.py:231
  648.5 24.5 %collective-permute-start.75 = (bf16[128,2048]{1,0:T(8,128)(2,1)}, bf16[128,2048]{1,0:T(8,128)(2,1)}, u32[]{:S(2)}, u32[]{:S(2)}) collective-permute-start(bf16[128,2048]{1,0:T(8,128)(2,1)} %pad_maximum_fusion.13), channel_id=1, source_target_pairs={{0,1},{1,0},{2,3},{3,2},{4,5},{5,4},{6,7},{7,6},{8,9},{9,8},{10,11... | collective-permute-start | bytes 1572872 | tf_op jit(solution)/shard_map/ppermute | solution.py:231
  662.7 38.7 %collective-permute-start.114 = (bf16[2,256,688]{1,2,0:T(8,128)(2,1)S(1)}, bf16[2,256,688]{1,2,0:T(8,128)(2,1)S(1)}, u32[]{:S(2)}, u32[]{:S(2)}) collective-permute-start(bf16[2,256,688]{1,2,0:T(8,128)(2,1)S(1)} %fusion.24), channel_id=1, source_target_pairs={{0,8},{1,9},{2,10},{3,11},{12,4},{13,5},{14,6},{15,7},{16,24},{17,... | collective-permute-start | bytes 2113544 | tf_op jit(solution)/shard_map/ppermute | solution.py:234
  671.3 31.7 %collective-permute-start.117 = (bf16[2,256,688]{1,2,0:T(8,128)(2,1)S(1)}, bf16[2,256,688]{1,2,0:T(8,128)(2,1)S(1)}, u32[]{:S(2)}, u32[]{:S(2)}) collective-permute-start(bf16[2,256,688]{1,2,0:T(8,128)(2,1)S(1)} %fusion.25), channel_id=1, source_target_pairs={{0,8},{1,9},{2,10},{3,11},{12,4},{13,5},{14,6},{15,7},{16,24},{17,... | collective-permute-start | bytes 2113544 | tf_op jit(solution)/shard_map/ppermute | solution.py:234
  719.9 52.6 %collective-permute-start.88 = (bf16[2,4,2,64,256]{4,3,2,1,0:T(8,128)(2,1)S(1)}, bf16[2,4,2,64,256]{4,3,2,1,0:T(8,128)(2,1)S(1)}, u32[]{:S(2)}, u32[]{:S(2)}) collective-permute-start(bf16[2,4,2,64,256]{4,3,2,1,0:T(8,128)(2,1)S(1)} %get-tuple-element.99), channel_id=1, source_target_pairs={{4,0},{5,1},{6,2},{7,3},{12,8},{13,9},{14,10},{15,11},{20,16},{21,... | collective-permute-start | bytes 1572872 | tf_op jit(solution)/shard_map/ppermute | solution.py:234
  721.2 48.5 %collective-permute-start.89 = (bf16[2,4,2,64,256]{4,3,2,1,0:T(8,128)(2,1)S(1)}, bf16[2,4,2,64,256]{4,3,2,1,0:T(8,128)(2,1)S(1)}, u32[]{:S(2)}, u32[]{:S(2)}) collective-permute-start(bf16[2,4,2,64,256]{4,3,2,1,0:T(8,128)(2,1)S(1)} %get-tuple-element.101), channel_id=1, source_target_pairs={{4,0},{5,1},{6,2},{7,3},{12,8},{13,9},{14,10},{15,11},{20,16},{21,... | collective-permute-start | bytes 1572872 | tf_op jit(solution)/shard_map/ppermute | solution.py:234
  783.7 74.8 %collective-permute-start.83 = (bf16[512,2048]{1,0:T(8,128)(2,1)}, bf16[512,2048]{1,0:T(8,128)(2,1)}, u32[]{:S(2)}, u32[]{:S(2)}) collective-permute-start(bf16[512,2048]{1,0:T(8,128)(2,1)} %slice.591), channel_id=1, source_target_pairs={{0,8},{1,9},{2,10},{3,11},{4,12},{5,13},{6,14},{7,15},{8,0},{9,1},... | collective-permute-start | bytes 6291464 | tf_op jit(solution)/shard_map/ppermute | solution.py:231
  796.6 24.1 %collective-permute-start.110 = (bf16[1024,256]{1,0:T(8,128)(2,1)S(1)}, bf16[1024,256]{1,0:T(8,128)(2,1)}, u32[]{:S(2)}, u32[]{:S(2)}) collective-permute-start(bf16[1024,256]{1,0:T(8,128)(2,1)S(1)} %add_convert_fusion.10), channel_id=1, source_target_pairs={{4,0},{5,1},{6,2},{7,3},{8,12},{9,13},{10,14},{11,15},{20,16},{21,... | collective-permute-start | bytes 1572872 | tf_op jit(solution)/shard_map/ppermute | solution.py:234
  820.7 51.2 %collective-permute-start.90 = (bf16[512,2048]{1,0:T(8,128)(2,1)S(1)}, bf16[512,2048]{1,0:T(8,128)(2,1)S(1)}, u32[]{:S(2)}, u32[]{:S(2)}) collective-permute-start(bf16[512,2048]{1,0:T(8,128)(2,1)S(1)} %slice.600), channel_id=1, source_target_pairs={{0,8},{1,9},{2,10},{3,11},{4,12},{5,13},{6,14},{7,15},{8,0},{9,1},... | collective-permute-start | bytes 6291464 | tf_op jit(solution)/shard_map/ppermute | solution.py:231
  (221 other events, 2705.6 us)
where the time goes:
time: 910 us; the launch traced here: 901 us
  waiting for transfers between devices  430 us (47%)
  starting transfers between devices  155 us (17%)
  local copies, waits for them, and re-layouts  146 us (16%)
  matrix products  83.1 us (9%)
  other arithmetic  60.8 us (7%)
  Pallas kernels  22 us (2%)
    ppermute x103, waiting for transfers between devices, swap(): return lax.ppermute(value, AXES, [(i, i ^ mask) for i in range(self.count)])  305 us
    ppermute x18, waiting for transfers between devices, send(): lax.ppermute(value, AXES, [(i, i ^ mask) for i in range(self.count) if ch...  125 us
    ppermute x103, starting transfers between devices, swap(): return lax.ppermute(value, AXES, [(i, i ^ mask) for i in range(self.count)])  120 us
    dot_general x21, matrix products, dot(): lax.dot_general(left, right, (over, ((), ())), preferred_element_type=kind)  83.1 us
    unnamed x328, local copies, waits for them, and re-layouts  49.6 us
    ppermute x18, starting transfers between devices, send(): lax.ppermute(value, AXES, [(i, i ^ mask) for i in range(self.count) if ch...  34.2 us
    convert_element_type x17, other arithmetic, add_low(): return (left.astype(f32) + right.astype(f32)).astype(bf16)  27.2 us
    reshape x9, local copies, waits for them, and re-layouts, reduce_gradient(): given = at.send(kept, at.half_bit, away).reshape(2, 2, rows // 8, cols)  21.8 us
  transfers between devices with their start and end apart: 121, of which 50 were waited for; matrix products, arithmetic and copies ran while one was open for 24% of the time, Pallas kernels for 1%

commit v1 on v0

v1 whole, which is shorter than its diff:
```python
import functools

import jax
import jax.numpy as jnp
from jax import lax
from jax.experimental import pallas as pl
from jax.experimental.pallas import tpu as pltpu
from jax.sharding import PartitionSpec as P

H = 16
HD = 128
AXES = ("dh", "dl", "uh", "ul", "blk")
GROUP = ("dl", "ul", "blk")
INNER = ("ul", "blk")
bf16 = jnp.bfloat16
f32 = jnp.float32
epsilon = 1e-06
negative = -1e30


def dot(left, right, over, kind=f32):
    return lax.dot_general(left, right, (over, ((), ())), preferred_element_type=kind)


def times(left, right, kind=f32):
    return dot(left, right, ((1,), (0,)), kind)


def times_transposed(left, right, kind=f32):
    return dot(left, right, ((1,), (1,)), kind)


def transposed_times(left, right, kind=f32):
    return dot(left, right, ((0,), (0,)), kind)


def normalize(values):
    inverse = lax.rsqrt(jnp.mean(values * values, axis=-1, keepdims=True) + epsilon)
    return (values * inverse, inverse)


def norm_back(grad_normed, normed, inverse, gain):
    scaled = grad_normed * gain
    return inverse * (scaled - normed * jnp.mean(scaled * normed, axis=-1, keepdims=True))


def add_low(left, right):
    return (left.astype(f32) + right.astype(f32)).astype(bf16)


def masked_scores(q, k, start, place, key_place, scale):
    scores = times_transposed(q, k) * scale
    allowed = (key_place >= start) & (key_place <= place)
    return jnp.where(allowed, scores, negative)


def attention_parts(q_ref, kv_ref, okv_ref, info_ref, places_ref, scale):
    q = q_ref[0, :, 0].reshape(-1, HD)
    kv = kv_ref[0, :, 0].reshape(-1, 2 * HD)
    okv = okv_ref[0, :, 0].reshape(-1, 2 * HD)
    start = info_ref[0, 0, :, 0:1]
    place = info_ref[0, 0, :, 1:2]
    own = masked_scores(q, kv[:, :HD], start, place, places_ref[0:1, :], scale)
    other = masked_scores(q, okv[:, :HD], start, place, places_ref[1:2, :], scale)
    largest = jnp.maximum(
        jnp.max(own, axis=-1, keepdims=True), jnp.max(other, axis=-1, keepdims=True)
    )
    own = jnp.exp(own - largest)
    other = jnp.exp(other - largest)
    total = jnp.sum(own, axis=-1, keepdims=True) + jnp.sum(other, axis=-1, keepdims=True)
    return q, kv, okv, own / total, other / total


def attend_kernel(scale, q_ref, kv_ref, okv_ref, info_ref, places_ref, out_ref):
    _, kv, okv, own, other = attention_parts(q_ref, kv_ref, okv_ref, info_ref, places_ref, scale)
    mixed = times(own.astype(bf16), kv[:, HD:]) + times(other.astype(bf16), okv[:, HD:])
    out_ref[0, :, 0] = mixed.astype(bf16).reshape(out_ref.shape[1], out_ref.shape[3], HD)


def attend_back_kernel(
    scale, q_ref, kv_ref, okv_ref, g_ref, info_ref, places_ref, gq_ref, gkv_ref, gokv_ref
):
    q, kv, okv, own, other = attention_parts(q_ref, kv_ref, okv_ref, info_ref, places_ref, scale)
    g = g_ref[0, :, 0].reshape(-1, HD)
    grad_own = times_transposed(g, kv[:, HD:])
    grad_other = times_transposed(g, okv[:, HD:])
    centre = jnp.sum(own * grad_own, axis=-1, keepdims=True) + jnp.sum(
        other * grad_other, axis=-1, keepdims=True
    )
    score_own = (own * (grad_own - centre)).astype(bf16)
    score_other = (other * (grad_other - centre)).astype(bf16)

    def put(ref, lanes, value):
        ref[0, :, 0, :, lanes] = value.astype(ref.dtype).reshape(ref.shape[1], ref.shape[3], HD)

    first, second = slice(0, HD), slice(HD, 2 * HD)
    put(gokv_ref, first, transposed_times(score_other, q) * scale)
    put(gokv_ref, second, transposed_times(other.astype(bf16), g))
    put(gkv_ref, first, transposed_times(score_own, q) * scale)
    put(gkv_ref, second, transposed_times(own.astype(bf16), g))
    put(gq_ref, first, (times(score_own, kv[:, :HD]) + times(score_other, okv[:, :HD])) * scale)


def attention_call(kernel, inputs, info, places, outputs):
    twins, pieces, rows, tok, width = inputs[0].shape
    heads = width // HD
    span = pieces * tok

    def block(array):
        return pl.BlockSpec(
            (1, pieces, 1, tok, array.shape[-1] // heads), lambda c, r, h: (c, 0, r, 0, h)
        )

    return pl.pallas_call(
        kernel,
        grid=(twins, rows, heads),
        in_specs=[block(a) for a in inputs]
        + [
            pl.BlockSpec((1, 1, span, 2), lambda c, r, h: (c, r, 0, 0)),
            pl.BlockSpec(places.shape, lambda c, r, h: (0, 0)),
        ],
        out_specs=[block(a) for a in outputs],
        out_shape=outputs,
        compiler_params=pltpu.CompilerParams(vmem_limit_bytes=48 * 1024 * 1024),
        cost_estimate=pl.CostEstimate(flops=1, bytes_accessed=1, transcendentals=0),
    )(*inputs, info, places)


def twins_kernel(sides_ref, kept_ref, given_ref, out_ref):
    out_ref[...] = add_low(kept_ref[...], given_ref[...])


def owner_kernel(unit, sides_ref, kept_ref, given_ref, twins_ref, *outs):
    mine = kept_ref[...].astype(f32) + given_ref[...].astype(f32)
    mine = jnp.where(sides_ref[0] == sides_ref[1], mine, twins_ref[...].astype(f32))
    if len(outs) == 1:
        outs[0][...] = mine
        return
    for i in range(mine.shape[1] // unit):
        j = i // 2 * unit
        outs[i % 2][:, j : j + unit] = mine[:, i * unit : (i + 1) * unit]


def halves_call(turned, kernel, sides, inputs, maps, outputs):
    rows = inputs[0].shape[1 if turned else 0] // 4

    def block(pick, array):
        if turned:
            return pl.BlockSpec((array.shape[0], rows), lambda i, s: (0, pick(i, s[0], s[1])))
        return pl.BlockSpec((rows, array.shape[1]), lambda i, s: (pick(i, s[0], s[1]), 0))

    return pl.pallas_call(
        kernel,
        grid_spec=pltpu.PrefetchScalarGridSpec(
            num_scalar_prefetch=1,
            grid=(2,),
            in_specs=[block(pick, a) for pick, a in zip(maps, inputs)],
            out_specs=[block(lambda i, z, t: i, a) for a in outputs],
        ),
        out_shape=outputs,
        cost_estimate=pl.CostEstimate(
            flops=0,
            bytes_accessed=sum(a.size * a.dtype.itemsize for a in [*inputs, *outputs]),
            transcendentals=0,
        ),
    )(sides, *inputs)


def split_kernel(unit, *refs):
    *sources, out = refs
    number = len(sources)
    for j in range(out.shape[0]):
        cols = out.shape[2] // number
        for i, source in enumerate(sources):
            for u in range(cols // unit):
                place = (u * number + i) * unit
                first = j * cols + u * unit
                out[j, :, place : place + unit] = source[:, first : first + unit]


def stack_kernel(*refs):
    *sources, out = refs
    rows, cols = sources[0].shape[0], out.shape[2]
    for i, source in enumerate(sources):
        for j in range(out.shape[0]):
            out[j, i * rows : (i + 1) * rows] = source[:, j * cols : (j + 1) * cols]


def turn_kernel(source, *outs):
    rows = source.shape[1] // len(outs)
    for i, out in enumerate(outs):
        blocks = source[:, i * rows : (i + 1) * rows]
        out[...] = blocks.reshape(-1, blocks.shape[-1]).T


def permuted(value, flags):
    low = value.shape[1] // 8
    blocks = [value[:, i * low : (i + 1) * low] for i in (0, 2, 1, 3, 4, 6, 5, 7)]
    for mask, flag in ((2, flags[0]), (4, flags[1])):
        blocks = [jnp.where(flag, blocks[j ^ mask], blocks[j]) for j in range(8)]
    return blocks


def restored(value, flags):
    low = value.shape[1] // 8
    blocks = [value[:, i * low : (i + 1) * low] for i in range(8)]
    for mask, flag in ((2, flags[0]), (4, flags[1])):
        blocks = [jnp.where(flag, blocks[j ^ mask], blocks[j]) for j in range(8)]
    return [blocks[i] for i in (0, 2, 1, 3, 4, 6, 5, 7)]


def move_kernel(how, me_ref, *refs):
    flags = [me_ref[0] == 1, me_ref[1] == 1]
    number = len(refs) // 2
    for source, target in zip(refs[:number], refs[number:]):
        low = source.shape[1] // 8
        for i, block in enumerate(how(source[...], flags)):
            target[:, i * low : (i + 1) * low] = block


def local_call(kernel, scalars, inputs, outputs):
    vmem = pl.BlockSpec(memory_space=pltpu.VMEM)
    size = sum(a.size * a.dtype.itemsize for a in [*inputs, *outputs])
    return pl.pallas_call(
        kernel,
        in_specs=[pl.BlockSpec(memory_space=pltpu.SMEM)] * len(scalars) + [vmem] * len(inputs),
        out_specs=[vmem] * len(outputs),
        out_shape=outputs,
        compiler_params=pltpu.CompilerParams(vmem_limit_bytes=48 * 1024 * 1024),
        cost_estimate=pl.CostEstimate(flops=0, bytes_accessed=size, transcendentals=0),
    )(*scalars, *inputs)


class Places:
    def __init__(self):
        self.count = lax.axis_size(AXES)
        self.me = lax.axis_index(AXES)
        self.group = lax.axis_size(GROUP)
        self.half_bit = self.group // 2
        self.twin_bit = self.group
        self.far_bit = 2 * self.group
        self.z = lax.axis_index("uh")
        self.x = lax.axis_index("dh")
        self.twin = lax.axis_index("dl")

    def swap(self, value, mask):
        return lax.ppermute(value, AXES, [(i, i ^ mask) for i in range(self.count)])

    def send(self, value, mask, chosen):
        return lax.ppermute(
            value, AXES, [(i, i ^ mask) for i in range(self.count) if chosen(i)]
        )


def after(value, *others):
    return lax.optimization_barrier((value, others))[0]


def near_weights(at, weights, unit, *others):
    rows, width = weights[0].shape
    number, cols = len(weights), width // at.group
    kernel = functools.partial(split_kernel, unit) if unit else stack_kernel
    shape = (at.group, rows, number * cols) if unit else (at.group, number * rows, cols)
    (blocks,) = local_call(kernel, [], weights, [jax.ShapeDtypeStruct(shape, bf16)])
    if others:
        blocks = after(blocks, *others)
    near = lax.all_to_all(blocks, GROUP, split_axis=0, concat_axis=0, tiled=True)
    if unit:
        return near.reshape(at.group * rows, number * cols)
    return local_call(
        turn_kernel,
        [],
        [near],
        [jax.ShapeDtypeStruct((cols, at.group * rows), bf16)] * number,
    )


def gather(at, value):
    return lax.all_gather(value, GROUP, axis=0, tiled=True)


def scatter(at, pairs, product=times_transposed, before=(), behind=()):
    def term(side):
        total = None
        for left, right in pairs:
            part = lax.dynamic_slice_in_dim(left, side * (left.shape[0] // 2), left.shape[0] // 2)
            part = product(part, right)
            total = part if total is None else total + part
        return total

    given = at.swap(term(1 - at.twin).astype(bf16), at.twin_bit)
    kept = (term(at.twin) + given.astype(f32)).astype(bf16)
    kept = kept.reshape(at.half_bit, -1, kept.shape[1])
    if before:
        kept = after(kept, *before)
    kept = lax.all_to_all(kept, INNER, split_axis=0, concat_axis=0, tiled=True)
    if behind:
        kept = after(kept, *behind)
    return jnp.sum(kept.astype(f32), axis=0)


class Gradient:
    def __init__(self, at, pairs, turned=False):
        self.at, self.turned = at, turned
        cut = pairs[0][0].shape[1] // 2
        self.first = [(left[:, :cut], right) for left, right in pairs]
        self.there = self.product([(left[:, cut:], right) for left, right in pairs]).astype(bf16)
        self.given = at.swap(self.there, at.far_bit)

    def product(self, pairs):
        if self.turned:
            ((left, right),) = pairs
            return transposed_times(right, left)
        terms = [transposed_times(left, right) for left, right in pairs]
        return terms[0] if len(terms) == 1 else jnp.concatenate(terms, axis=1)

    def away(self, i):
        return (i // self.at.half_bit) % 2 != (i // self.at.twin_bit) % 2

    def across(self, *others):
        self.here = self.product(self.first)
        kept = (self.here + self.given.astype(f32)).astype(bf16)
        self.kept = after(kept, *others) if others else kept
        self.back = self.at.send(self.kept, self.at.half_bit, self.away)

    def call(self, kernel, inputs, maps, widths, kind):
        sides = jnp.stack([self.at.z, self.at.twin]).astype(jnp.int32)
        span = self.kept.shape[1 if self.turned else 0] // 2
        outs = [
            jax.ShapeDtypeStruct((width, span) if self.turned else (span, width), kind)
            for width in widths
        ]
        return halves_call(self.turned, kernel, sides, inputs, maps, outs)

    def to_twin(self):
        (twins,) = self.call(
            twins_kernel,
            [self.kept, self.back],
            [lambda i, z, t: 2 * i + 1 - t, lambda i, z, t: 2 * (1 - i) + 1 - t],
            [self.kept.shape[0 if self.turned else 1]],
            bf16,
        )
        self.twins = self.at.send(twins, self.at.twin_bit, lambda i: not self.away(i))

    def finish(self, unit=None):
        cols = self.kept.shape[0 if self.turned else 1]
        outs = self.call(
            functools.partial(owner_kernel, unit),
            [self.kept, self.back, self.twins],
            [
                lambda i, z, t: 2 * (i ^ z) + t,
                lambda i, z, t: 2 * (1 - (i ^ z)) + t,
                lambda i, z, t: i ^ z,
            ],
            [cols // 2, cols // 2] if unit else [cols],
            f32,
        )
        return [out.T if self.turned else out for out in outs]


def reduce_gains(at, terms):
    number, width = terms.shape
    terms = terms.reshape(number, 2, 2, 2, -1)
    terms = jnp.where(at.x == 1, terms[:, ::-1], terms)
    terms = jnp.where(at.z == 1, terms[:, :, ::-1], terms)
    terms = terms.transpose(0, 1, 3, 2, 4).reshape(number, at.count, -1).transpose(1, 0, 2)
    terms = lax.all_to_all(terms, AXES, split_axis=0, concat_axis=0, tiled=True)
    return jnp.sum(terms, axis=0)


def on_device(
    tokens,
    memory,
    lengths,
    gain_attn,
    gain_memory,
    gain_ffn,
    w_query,
    w_key,
    w_value,
    w_out,
    w_gate,
    w_up,
    w_down,
    cotangent,
):
    at = Places()
    rows_here, tok_row, model_width = tokens.shape
    count = rows_here * tok_row
    group = at.group
    half = group // 2
    head_width = w_query.shape[1]
    own_width = head_width // group
    width = max(own_width, HD)
    scale = HD ** (-0.5)

    bounds = jnp.cumsum(lengths, axis=1)
    twin_bounds = at.swap(bounds, at.twin_bit)
    first = at.twin == 0
    all_bounds = jnp.stack(
        [jnp.where(first, bounds, twin_bounds), jnp.where(first, twin_bounds, bounds)]
    )
    span = half * tok_row
    places = jnp.arange(span, dtype=jnp.int32)
    own_places = at.z * span + places
    other_places = (1 - at.z) * span + places
    passed = all_bounds[:, :, None, :] <= own_places[None, None, :, None]
    starts = jnp.max(jnp.where(passed, all_bounds[:, :, None, :], 0), axis=-1)
    info = jnp.stack([starts, jnp.broadcast_to(own_places, starts.shape)], axis=-1)
    key_places = jnp.stack([own_places, other_places])
    position = at.me % group
    here = position * tok_row + jnp.arange(tok_row, dtype=jnp.int32)
    valid = (here[None] < bounds[:, -1:]).astype(f32).reshape(count, 1)

    unit = min(own_width, HD)
    cache_near = near_weights(at, [w_key, w_value], unit)
    query_near = near_weights(at, [w_query, w_out], own_width, cache_near)
    sides = jnp.stack([at.z, at.x]).astype(jnp.int32)
    entry = [a.reshape(count, model_width) for a in (memory, tokens, cotangent)] + [
        gain.reshape(1, model_width) for gain in (gain_attn, gain_memory, gain_ffn)
    ]
    memory, tokens, cotangent, gain_attn, gain_memory, gain_ffn = local_call(
        functools.partial(move_kernel, permuted),
        [sides],
        entry,
        [jax.ShapeDtypeStruct(a.shape, a.dtype) for a in entry],
    )
    residual_in = tokens.astype(f32)
    token_normed, token_inverse = normalize(residual_in)
    token_in = (token_normed * gain_attn).astype(bf16)
    memory_normed, memory_inverse = normalize(memory.astype(f32))
    memory_in = (memory_normed * gain_memory).astype(bf16)
    grad_final = cotangent.astype(f32) * valid

    parts = HD // own_width if own_width < HD else 1

    def widen(value):
        if parts == 1:
            return value
        assert parts == lax.axis_size("blk")
        return lax.all_gather(value, "blk", axis=1, tiled=True)

    def narrow(value):
        if parts == 1:
            return value
        return lax.dynamic_slice_in_dim(
            value, lax.axis_index("blk") * own_width, own_width, axis=1
        )

    def heads(value):
        return value.reshape(2, half, rows_here, tok_row, -1)

    memory_all = gather(at, after(memory_in, cache_near))
    cache_half = at.swap(cache_near, at.half_bit)
    cache_far = at.swap(cache_near, at.far_bit)
    cache_far_half = at.swap(cache_half, at.far_bit)
    cache_w = jnp.concatenate([cache_near, cache_half, cache_far, cache_far_half], axis=0)
    memory_all = after(memory_all, cache_half, cache_far, query_near, info)
    query_later = after(query_near, cache_half)
    query_half = at.swap(query_later, at.half_bit)
    query_far = at.swap(query_later, at.far_bit)
    token_all = gather(at, after(token_in, memory_all))
    memory_all = after(memory_all, query_half, query_far, cache_w)

    def first_half(i):
        return (i // at.half_bit) % 2 == 0

    def second_half(i):
        return not first_half(i)

    cache = times(memory_all, cache_w, bf16)
    if parts > 1:
        cache = jnp.concatenate(
            [widen(cache[:, :own_width]), widen(cache[:, own_width:])], axis=1
        )
    cache = heads(cache)
    other_cache = at.send(cache, at.half_bit, first_half)
    token_all = after(token_all, other_cache)
    query_far_half = at.swap(after(query_half, cache), at.far_bit)
    query_parts = [query_near, query_half, query_far, query_far_half]
    query_w = jnp.concatenate([part[:, :own_width] for part in query_parts], axis=0)
    out_w = jnp.concatenate([part[:, own_width:] for part in query_parts], axis=0)
    queries = heads(widen(times(token_all, query_w, bf16)))
    gate_near, up_near, down_near = near_weights(
        at, [w_gate, w_up, w_down], None, query_near, cache
    )
    (mixed,) = attention_call(
        functools.partial(attend_kernel, scale),
        [after(queries, gate_near), cache, other_cache],
        info,
        key_places,
        [queries],
    )
    gate_far, up_far, down_far = (
        at.swap(near, at.far_bit) for near in (gate_near, up_near, down_near)
    )
    mixed = narrow(mixed.reshape(group * count, width))
    mixed = after(mixed, gate_far)
    gate_half = at.swap(after(gate_near, other_cache), at.half_bit)

    def whole(near, half_part, far_part, far_half_part):
        return jnp.concatenate([near, half_part, far_part, far_half_part], axis=1)

    residual = residual_in + scatter(
        at, [(mixed, out_w)], times_transposed, (gate_half,), (up_far,)
    )
    ffn_normed, ffn_inverse = normalize(residual)
    ffn_in = (ffn_normed * gain_ffn).astype(bf16)
    up_half = at.swap(after(up_near, gate_half), at.half_bit)
    gate_w = whole(gate_near, gate_half, gate_far, at.swap(gate_half, at.far_bit))
    ffn_all = after(gather(at, ffn_in), up_half, down_far, gate_w)
    final_all = gather(at, after(grad_final.astype(bf16), ffn_all))
    down_half = at.swap(after(down_near, up_half), at.half_bit)
    gate = times_transposed(ffn_all, gate_w)
    up_w = whole(up_near, up_half, up_far, at.swap(up_half, at.far_bit))
    up = times_transposed(ffn_all, after(up_w, gate))
    down_w = whole(
        down_near, after(down_half, up), down_far, at.swap(down_half, at.far_bit)
    )
    grad_hidden = times_transposed(final_all, down_w)
    gate_sigmoid = jax.nn.sigmoid(gate)
    silu = gate * gate_sigmoid
    hidden = (silu * up).astype(bf16)
    grad_gate_in = (
        grad_hidden * up * gate_sigmoid * (1.0 + gate * (1.0 - gate_sigmoid))
    ).astype(bf16)
    grad_up_in = (grad_hidden * silu).astype(bf16)
    gate_grad = Gradient(at, [(ffn_all, grad_gate_in)], True)
    up_grad = Gradient(at, [(ffn_all, grad_up_in)], True)
    grad_ffn_in = scatter(
        at,
        [(after(grad_gate_in, gate_grad.there), gate_w), (grad_up_in, up_w)],
        times,
        (),
        (up_grad.there,),
    )
    grad_residual = grad_final + norm_back(grad_ffn_in, ffn_normed, ffn_inverse, gain_ffn)
    gain_ffn_term = jnp.sum(grad_ffn_in * ffn_normed, axis=0)
    grad_branch = grad_residual.astype(bf16)
    hidden = after(hidden, grad_branch)
    down_grad = Gradient(at, [(final_all, hidden)], True)
    branch_all = gather(at, after(grad_branch, gate_grad.given))
    gate_grad.across(grad_branch)
    up_grad.across()
    gathered = branch_all
    branch_all = after(branch_all, gate_grad.kept, up_grad.kept)
    grad_mixed = heads(widen(times(branch_all, out_w, bf16)))
    grad_queries, grad_cache, grad_other_cache = attention_call(
        functools.partial(attend_back_kernel, scale),
        [queries, cache, other_cache, after(grad_mixed, gate_grad.back)],
        info,
        key_places,
        [
            queries,
            jax.ShapeDtypeStruct(cache.shape, f32),
            cache,
        ],
    )
    given_cache = at.send(grad_other_cache, at.half_bit, second_half)
    grad_queries = narrow(grad_queries.reshape(group * count, width))
    output = residual + scatter(at, [(hidden, down_w)], times, (gathered,))
    gate_grad.to_twin()
    (gate_out,) = gate_grad.finish()
    query_grad = Gradient(at, [(token_all, grad_queries), (branch_all, mixed)])

    grad_token_in = scatter(at, [(grad_queries, query_w)])
    given_cache = after(given_cache, gate_out, up_grad.back, query_grad.there, down_grad.given)
    down_grad.across(given_cache)
    up_grad.to_twin()
    grad_cache = (grad_cache + given_cache.astype(f32)).astype(bf16)
    grad_cache = grad_cache.reshape(group * count, 2 * width)
    if parts > 1:
        grad_cache = jnp.concatenate(
            [narrow(grad_cache[:, :width]), narrow(grad_cache[:, width:])], axis=1
        )
    cache_grad = Gradient(at, [(memory_all, grad_cache)])
    query_grad.across(down_grad.back)
    cache_grad.across(down_grad.back)
    grad_memory_in = scatter(
        at,
        [(after(grad_cache, cache_grad.there), cache_w)],
        times_transposed,
        (),
        (query_grad.back, up_grad.twins),
    )
    for grad in (down_grad, query_grad, cache_grad):
        grad.to_twin()
    (up_out,), (down_out,) = (grad.finish() for grad in (up_grad, down_grad))
    query_out, out_out = query_grad.finish(own_width)
    key_out, value_out = cache_grad.finish(unit)

    cut = model_width // 2
    gain_memory_term = (
        jnp.concatenate(
            [
                jnp.sum(cache_grad.here * cache_w[:cut].astype(f32), axis=1),
                jnp.sum(cache_grad.there.astype(f32) * cache_w[cut:].astype(f32), axis=1),
            ]
        )
        / gain_memory[0]
    )
    gain_attn_term = jnp.sum(grad_token_in * token_normed, axis=0)
    gain_grads = reduce_gains(at, jnp.stack([gain_attn_term, gain_memory_term, gain_ffn_term]))

    grad_tokens = grad_residual + norm_back(grad_token_in, token_normed, token_inverse, gain_attn)
    grad_memory = norm_back(grad_memory_in, memory_normed, memory_inverse, gain_memory)
    leaving = [a.astype(bf16) for a in (output, grad_tokens, grad_memory)]
    leaving = local_call(
        functools.partial(move_kernel, restored),
        [sides],
        leaving,
        [jax.ShapeDtypeStruct(a.shape, a.dtype) for a in leaving],
    )
    output, grad_tokens, grad_memory = (
        a.reshape(rows_here, tok_row, model_width) for a in leaving
    )
    return (
        output,
        grad_tokens,
        grad_memory,
        gain_grads[0],
        gain_grads[1],
        gain_grads[2],
        query_out,
        key_out,
        value_out,
        out_out,
        gate_out,
        up_out,
        down_out,
    )


def solution(mesh):
    dp, ulysses, blk = (mesh.shape[axis] for axis in ("dp", "ulysses", "blk"))
    mesh = jax.sharding.Mesh(mesh.devices.reshape(dp // 2, 2, 2, ulysses // 2, blk), AXES)
    dp, places = ("dh", "dl"), ("uh", "ul", "blk")
    rows = P(dp, places, None)
    weight = P(AXES, None)
    grad = P(dp, places)
    return jax.shard_map(
        on_device,
        mesh=mesh,
        in_specs=(rows, rows, P(dp, None), P(), P(), P()) + (weight,) * 7 + (rows,),
        out_specs=(rows,) * 3 + (P(AXES),) * 3 + (grad,) * 7,
        check_vma=False,
    )
```

time: 910 us -> 718 us (0.79)
  local copies, waits for them, and re-layouts: 146 us -> 39 us
  waiting for transfers between devices: 430 us -> 353 us
  starting transfers between devices: 155 us -> 105 us
  Pallas kernels: 22 us -> 54.2 us
  other arithmetic: 60.8 us -> 31.5 us
  matrix products: 83.1 us -> 110 us
  between operations: 3.82 us -> 15.5 us
    ppermute x103 -> x26, waiting for transfers between devices: 305 us -> 207 us  [swap(): return lax.ppermute(value, AXES, [(i, i ^ mask) for i in range(self.count)])]
    ppermute x103 -> x26, starting transfers between devices: 120 us -> 40 us  [swap(): return lax.ppermute(value, AXES, [(i, i ^ mask) for i in range(self.count)])]
    all_to_all x0 -> x9, waiting for transfers between devices: none -> 66.1 us  [the longest x5 35.7 us: scatter(): kept = lax.all_to_all(kept, INNER, split_axis=0, concat_axis=0, tiled=True)]
    ppermute x18 -> x12, waiting for transfers between devices: 125 us -> 61.9 us  [send(): lax.ppermute(value, AXES, [(i, i ^ mask) for i in range(self.count) if ch...]
    all_to_all x0 -> x9, starting transfers between devices: none -> 39.4 us  [the longest x5 22.7 us: scatter(): kept = lax.all_to_all(kept, INNER, split_axis=0, concat_axis=0, tiled=True)]
    pallas_call x12 -> x18, Pallas kernels: 22 us -> 54.2 us  [the longest x10 29.1 us: halves_call(): pl.pallas_call(kernel, grid_spec=pltpu.PrefetchScalarGridSpec(num_scalar_...]
    dot_general x21 -> x30, matrix products: 83.1 us -> 110 us  [dot(): lax.dot_general(left, right, (over, ((), ())), preferred_element_type=kind)]
    reshape x15 -> x1, local copies, waits for them, and re-layouts: 25.8 us -> 0.1 us  [reduce_gains(): terms.transpose(0, 1, 3, 2, 4).reshape(number, at.count, -1)]
  transfers between devices with their start and end apart: 121 -> 52, of which waited for: 50 -> 28; matrix products, arithmetic and copies ran while one was open for 24% -> 19% of each run, Pallas kernels for 1% -> 8%
where the time goes in v1:
time: 718 us; the launch traced here: 708 us
  waiting for transfers between devices  353 us (49%)
  matrix products  110 us (15%)
  starting transfers between devices  105 us (15%)
  Pallas kernels  54.2 us (8%)
  local copies, waits for them, and re-layouts  39 us (5%)
  other arithmetic  31.5 us (4%)
  between operations  15.5 us (2%)
    ppermute x26, waiting for transfers between devices, swap(): return lax.ppermute(value, AXES, [(i, i ^ mask) for i in range(self.count)])  207 us
    dot_general x30, matrix products, dot(): lax.dot_general(left, right, (over, ((), ())), preferred_element_type=kind)  110 us
    ppermute x12, waiting for transfers between devices, send(): lax.ppermute(value, AXES, [(i, i ^ mask) for i in range(self.count) if ch...  61.9 us
    ppermute x26, starting transfers between devices, swap(): return lax.ppermute(value, AXES, [(i, i ^ mask) for i in range(self.count)])  40 us
    all_to_all x5, waiting for transfers between devices, scatter(): kept = lax.all_to_all(kept, INNER, split_axis=0, concat_axis=0, tiled=True)  35.7 us
    pallas_call x10, Pallas kernels, halves_call(): pl.pallas_call(kernel, grid_spec=pltpu.PrefetchScalarGridSpec(num_scalar_...  29.1 us
    all_to_all x3, waiting for transfers between devices, near_weights(): lax.all_to_all(blocks, GROUP, split_axis=0, concat_axis=0, tiled=True)  27 us
    unnamed x159, local copies, waits for them, and re-layouts  27 us
  transfers between devices with their start and end apart: 52, of which 28 were waited for; matrix products, arithmetic and copies ran while one was open for 19% of the time, Pallas kernels for 8%

profile of v1, /device:TPU:0, one launch (start us, length us, event | category | flops | bytes accessed | tf_op | source)
XLA Modules:
  0.0 708.2 jit_solution(4083400235016544685)
XLA Ops:
  10.1 5.3 all-to-all-start
  18.4 6.3 all-to-all-done
  26.3 4.2 all-to-all-start.1
  39.1 18.6 %collective-permute-done = bf16[512,512]{1,0:T(8,128)(2,1)} collective-permute-done((bf16[512,512]{1,0:T(8,128)(2,1)}, bf16[512,512]{1,0:T(8,128)(2,1)}, u32[]{:S(2)}, u32[]{:S(2)}) %collective-permute-start) | collective-permute-done | bytes 524320 | tf_op jit(solution)/shard_map/ppermute | solution.py:247
  57.7 11.3 %all-gather.6.cloned.1.call-done = bf16[1024,2048]{1,0:T(8,128)(2,1)} async-done(((bf16[128,2048]{1,0:T(8,128)(2,1)}), bf16[1024,2048]{1,0:T(8,128)(2,1)}) %all-gather.6.cloned.1.call-update) | async-done | bytes 4194320 | tf_op jit(solution)/shard_map/all_gather | solution.py:279
  76.0 19.4 %collective-permute-done.3 = bf16[512,512]{1,0:T(8,128)(2,1)S(1)} collective-permute-done((bf16[512,512]{1,0:T(8,128)(2,1)}, bf16[512,512]{1,0:T(8,128)(2,1)S(1)}, u32[]{:S(2)}, u32[]{:S(2)}) %collective-permute-start.3) | collective-permute-done | bytes 524320 | tf_op jit(solution)/shard_map/ppermute | solution.py:247
  97.2 4.9 fusion.103
  105.7 3.7 collective-permute-start.6
  115.5 20.7 %all-to-all-done.2.source = bf16[8,192,688]{2,1,0:T(8,128)(2,1)S(1)} async-done(((bf16[8,192,688]{2,1,0:T(8,128)(2,1)}), bf16[8,192,688]{2,1,0:T(8,128)(2,1)S(1)}, u32[]{:S(2)}, u32[]{:S(2)}) %all-to-all-start.2) | async-done | bytes 2113568 | tf_op jit(solution)/shard_map/all_to_all | solution.py:267
  142.5 12.1 %collective-permute-done.6.okv_ref = bf16[2,4,2,64,512]{4,3,2,1,0:T(8,128)(2,1)} collective-permute-done((bf16[2,4,2,64,512]{4,3,2,1,0:T(8,128)(2,1)}, bf16[2,4,2,64,512]{4,3,2,1,0:T(8,128)(2,1)}, u32[]{:S(2)}, u32[]{:S(2)}) %collective-permute-start.6) | collective-permute-done | bytes 1048608 | tf_op jit(solution)/shard_map/ppermute | solution.py:250
  154.6 3.7 fusion.102
  158.4 7.4 %shard_map.242 = bf16[2,4,2,64,256]{4,3,2,1,0:T(8,128)(2,1)S(1)} custom-call(bf16[2,4,2,64,256]{4,3,2,1,0:T(8,128)(2,1)S(1)} %bitcast.77, bf16[2,4,2,64,512]{4,3,2,1,0:T(8,128)(2,1)S(1)} %bitcast.75, bf16[2,4,2,64,512]{4,3,2,1,0:T(8,128)(2,1)} %collective-permute-done.6.okv_ref, s32[2,2,256,2]{3,2,1,0:T(8,128)S(1)} %copy-done, ...), custom_call_target="tpu_custom_call" | custom-call | flops 1 | bytes 1 | tf_op jit(solution)/shard_map/pallas_call | solution.py:114
  168.1 12.6 %collective-permute-start.10 = (bf16[688,512]{1,0:T(8,128)(2,1)}, bf16[688,512]{1,0:T(8,128)(2,1)}, u32[]{:S(2)}, u32[]{:S(2)}) collective-permute-start(bf16[688,512]{1,0:T(8,128)(2,1)} %get-tuple-element.82), channel_id=1, source_target_pairs={{0,4},{1,5},{2,6},{3,7},{4,0},{5,1},{6,2},{7,3},{8,12},{9,13},{10,... | collective-permute-start | bytes 2113544 | tf_op jit(solution)/shard_map/ppermute | solution.py:247
  180.7 4.1 add_convert_fusion.5
  184.7 27.8 %collective-permute-done.10 = bf16[688,512]{1,0:T(8,128)(2,1)} collective-permute-done((bf16[688,512]{1,0:T(8,128)(2,1)}, bf16[688,512]{1,0:T(8,128)(2,1)}, u32[]{:S(2)}, u32[]{:S(2)}) %collective-permute-start.10) | collective-permute-done | bytes 704544 | tf_op jit(solution)/shard_map/ppermute | solution.py:247
  212.5 4.4 all-to-all-start.3
  218.6 16.5 %collective-permute-done.11 = bf16[688,512]{1,0:T(8,128)(2,1)} collective-permute-done((bf16[688,512]{1,0:T(8,128)(2,1)}, bf16[688,512]{1,0:T(8,128)(2,1)}, u32[]{:S(2)}, u32[]{:S(2)}) %collective-permute-start.11) | collective-permute-done | bytes 704544 | tf_op jit(solution)/shard_map/ppermute | solution.py:247
  235.0 7.3 %all-to-all-done.3 = bf16[4,128,2048]{2,1,0:T(8,128)(2,1)} async-done(((bf16[4,128,2048]{2,1,0:T(8,128)(2,1)}), bf16[4,128,2048]{2,1,0:T(8,128)(2,1)}, u32[]{:S(2)}, u32[]{:S(2)}) %all-to-all-start.3) | async-done | bytes 2097184 | tf_op jit(solution)/shard_map/all_to_all | solution.py:296
  260.3 19.2 %collective-permute-done.14 = bf16[688,512]{1,0:T(8,128)(2,1)} collective-permute-done((bf16[688,512]{1,0:T(8,128)(2,1)}, bf16[688,512]{1,0:T(8,128)(2,1)}, u32[]{:S(2)}, u32[]{:S(2)}) %collective-permute-start.14) | collective-permute-done | bytes 704544 | tf_op jit(solution)/shard_map/ppermute | solution.py:247
  281.9 6.5 all-gather.10.cloned.1.call-done
  296.1 26.7 %collective-permute-done.16 = bf16[688,512]{1,0:T(8,128)(2,1)S(1)} collective-permute-done((bf16[688,512]{1,0:T(8,128)(2,1)}, bf16[688,512]{1,0:T(8,128)(2,1)S(1)}, u32[]{:S(2)}, u32[]{:S(2)}) %collective-permute-start.16) | collective-permute-done | bytes 704544 | tf_op jit(solution)/shard_map/ppermute | solution.py:247
  324.4 7.6 %fusion.109 = f32[1024,688]{0,1:T(8,128)} fusion(bf16[1024,2048]{1,0:T(8,128)(2,1)S(1)} %copy-done.66, bf16[688,2048]{1,0:T(8,128)(2,1)} %constant_dynamic-update-slice_fusion), kind=kOutput, calls=%fused_computation.175 | convolution fusion | flops 2885681152 | bytes 9830400 | tf_op jit(solution)/shard_map/dot_general | solution.py:22
  331.9 4.7 fusion.110
  341.3 10.0 %multiply_convert_fusion.1 = (bf16[1024,688]{0,1:T(8,128)(2,1)S(1)}, bf16[1024,688]{0,1:T(8,128)(2,1)S(1)}, bf16[1024,688]{0,1:T(8,128)(2,1)}) fusion(f32[1024,688]{0,1:T(8,128)} %fusion.109, f32[1024,688]{0,1:T(8,128)} %fusion.110, bf16[1024,2048]{1,0:T(8,128)(2,1)} %all-gather.12.cloned.1.call-done, bf16[688,2048]{1,0:T(8,128)(2,1)} %constant_dynamic-update-slice_fusion.8), kind=kOutput, calls=%fused_computation.19 | convolution fusion | flops 2896248832 | bytes 16875520 | tf_op jit(solution)/shard_map/dot_general | solution.py:22
  357.7 3.8 add_convert_fusion.4
  369.7 4.4 all-to-all-start.4
  375.9 4.7 fusion.29
  380.6 20.2 %all-to-all-done.4 = bf16[4,128,2048]{2,1,0:T(8,128)(2,1)} async-done(((bf16[4,128,2048]{2,1,0:T(8,128)(2,1)}), bf16[4,128,2048]{2,1,0:T(8,128)(2,1)}, u32[]{:S(2)}, u32[]{:S(2)}) %all-to-all-start.4) | async-done | bytes 2097184 | tf_op jit(solution)/shard_map/all_to_all | solution.py:296
  408.1 5.4 convolution_convert_fusion.3
  420.0 27.0 %collective-permute-done.21 = bf16[688,1024]{1,0:T(8,128)(2,1)S(1)} collective-permute-done((bf16[688,1024]{1,0:T(8,128)(2,1)}, bf16[688,1024]{1,0:T(8,128)(2,1)S(1)}, u32[]{:S(2)}, u32[]{:S(2)}) %collective-permute-start.21) | collective-permute-done | bytes 1409056 | tf_op jit(solution)/shard_map/ppermute | solution.py:247
  451.0 3.8 collective-permute-done.22.given_ref
  459.8 5.8 add_convert_fusion.2
  465.6 4.7 all-to-all-start.5
  473.9 10.0 %shard_map.243 = (bf16[2,4,2,64,256]{4,3,2,1,0:T(8,128)(2,1)S(1)}, f32[2,4,2,64,512]{4,3,2,1,0:T(8,128)}, bf16[2,4,2,64,512]{4,3,2,1,0:T(8,128)(2,1)}) custom-call(bf16[2,4,2,64,256]{4,3,2,1,0:T(8,128)(2,1)S(1)} %bitcast.78, bf16[2,4,2,64,512]{4,3,2,1,0:T(8,128)(2,1)S(1)} %bitcast.76, bf16[2,4,2,64,512]{4,3,2,1,0:T(8,128)(2,1)} %collective-permute-done.6.okv_ref, ...), custom_call_target="tpu_custom_call" | custom-call | flops 1 | bytes 1 | tf_op jit(solution)/shard_map/pallas_call | solution.py:114
  498.9 23.5 %collective-permute-done.27 = bf16[688,1024]{1,0:T(8,128)(2,1)} collective-permute-done((bf16[688,1024]{1,0:T(8,128)(2,1)}, bf16[688,1024]{1,0:T(8,128)(2,1)}, u32[]{:S(2)}, u32[]{:S(2)}) %collective-permute-start.27) | collective-permute-done | bytes 1409056 | tf_op jit(solution)/shard_map/ppermute | solution.py:247
  522.4 18.2 %collective-permute-done.24 = bf16[2,4,2,64,512]{4,3,2,1,0:T(8,128)(2,1)} collective-permute-done((bf16[2,4,2,64,512]{4,3,2,1,0:T(8,128)(2,1)}, bf16[2,4,2,64,512]{4,3,2,1,0:T(8,128)(2,1)}, u32[]{:S(2)}, u32[]{:S(2)}) %collective-permute-start.24) | collective-permute-done | bytes 1048608 | tf_op jit(solution)/shard_map/ppermute | solution.py:250
  543.2 3.8 add_convert_fusion.1
  547.0 4.4 all-to-all-start.6
  551.5 4.6 multiply_reduce_fusion
  559.1 4.1 add_convert_fusion.6.kept_ref
  566.5 4.0 add_convert_fusion
  570.5 8.3 %all-to-all-done.6 = bf16[4,128,2048]{2,1,0:T(8,128)(2,1)} async-done(((bf16[4,128,2048]{2,1,0:T(8,128)(2,1)}), bf16[4,128,2048]{2,1,0:T(8,128)(2,1)}, u32[]{:S(2)}, u32[]{:S(2)}) %all-to-all-start.6) | async-done | bytes 2097184 | tf_op jit(solution)/shard_map/all_to_all | solution.py:296
  578.8 4.7 all-to-all-start.7
  590.8 20.4 %collective-permute-done.34 = bf16[1024,512]{1,0:T(8,128)(2,1)} collective-permute-done((bf16[1024,512]{1,0:T(8,128)(2,1)}, bf16[1024,512]{1,0:T(8,128)(2,1)}, u32[]{:S(2)}, u32[]{:S(2)}) %collective-permute-start.34) | collective-permute-done | bytes 1048608 | tf_op jit(solution)/shard_map/ppermute | solution.py:247
  619.6 4.2 collective-permute-start.32
  634.3 20.0 %collective-permute-done.31.given_ref = bf16[1024,512]{1,0:T(8,128)(2,1)} collective-permute-done((bf16[1024,512]{1,0:T(8,128)(2,1)S(1)}, bf16[1024,512]{1,0:T(8,128)(2,1)}, u32[]{:S(2)}, u32[]{:S(2)}) %collective-permute-start.31) | collective-permute-done | bytes 1048608 | tf_op jit(solution)/shard_map/ppermute | solution.py:250
  659.1 6.5 collective-permute-done.35.given_ref
  688.5 3.7 all-to-all-start.8
  (334 shorter events, 207.8 us)
Async XLA Ops:
  10.1 14.6 %all-to-all-start = ((bf16[8,64,512]{2,1,0:T(8,128)(2,1)}), bf16[8,64,512]{2,1,0:T(8,128)(2,1)}, u32[]{:S(2)}, u32[]{:S(2)}) async-start(bf16[8,64,512]{2,1,0:T(8,128)(2,1)} %shard_map.238), calls=%async_computation | async-start | bytes 1048576 | tf_op jit(solution)/shard_map/all_to_all | solution.py:267
  15.4 53.6 %all-gather.6.cloned.1.call-start = ((), (), s32[]{:S(2)}) async-start(), calls=%async_computation.9 | async-start | bytes 4718592 | tf_op jit(solution)/shard_map/all_gather | solution.py:279
  25.0 10.9 %collective-permute-start.2 = (s32[2,8]{1,0:T(2,128)S(1)}, s32[2,8]{1,0:T(2,128)S(1)}, u32[]{:S(2)}, u32[]{:S(2)}) collective-permute-start(s32[2,8]{1,0:T(2,128)S(1)} %reduce_window_sum.11), channel_id=1, source_target_pairs={{0,8},{1,9},{2,10},{3,11},{4,12},{5,13},{6,14},{7,15},{8,0},{9,1},... | collective-permute-start | bytes 200 | tf_op jit(solution)/shard_map/ppermute | solution.py:247
  26.3 31.4 %all-to-all-start.1 = ((bf16[8,64,512]{2,1,0:T(8,128)(2,1)}), bf16[8,64,512]{2,1,0:T(8,128)(2,1)}, u32[]{:S(2)}, u32[]{:S(2)}) async-start(bf16[8,64,512]{2,1,0:T(8,128)(2,1)} %shard_map.239), calls=%async_computation.1 | async-start | bytes 1048576 | tf_op jit(solution)/shard_map/all_to_all | solution.py:267
  30.5 124.2 %all-gather.8.cloned.1.call-start = ((), (), s32[]{:S(2)}) async-start(), calls=%async_computation.10 | async-start | bytes 4718592 | tf_op jit(solution)/shard_map/all_gather | solution.py:279
  31.5 26.2 %collective-permute-start = (bf16[512,512]{1,0:T(8,128)(2,1)}, bf16[512,512]{1,0:T(8,128)(2,1)}, u32[]{:S(2)}, u32[]{:S(2)}) collective-permute-start(bf16[512,512]{1,0:T(8,128)(2,1)} %bitcast.10), channel_id=1, source_target_pairs={{0,4},{1,5},{2,6},{3,7},{4,0},{5,1},{6,2},{7,3},{8,12},{9,13},{10,... | collective-permute-start | bytes 1572872 | tf_op jit(solution)/shard_map/ppermute | solution.py:247
  34.4 23.4 %collective-permute-start.1 = (bf16[512,512]{1,0:T(8,128)(2,1)}, bf16[512,512]{1,0:T(8,128)(2,1)}, u32[]{:S(2)}, u32[]{:S(2)}) collective-permute-start(bf16[512,512]{1,0:T(8,128)(2,1)} %bitcast.10), channel_id=1, source_target_pairs={{0,16},{1,17},{2,18},{3,19},{4,20},{5,21},{6,22},{7,23},{8,24},{9,... | collective-permute-start | bytes 1572872 | tf_op jit(solution)/shard_map/ppermute | solution.py:247
  69.0 26.4 %collective-permute-start.3 = (bf16[512,512]{1,0:T(8,128)(2,1)}, bf16[512,512]{1,0:T(8,128)(2,1)S(1)}, u32[]{:S(2)}, u32[]{:S(2)}) collective-permute-start(bf16[512,512]{1,0:T(8,128)(2,1)} %bitcast.11), channel_id=1, source_target_pairs={{0,4},{1,5},{2,6},{3,7},{4,0},{5,1},{6,2},{7,3},{8,12},{9,13},{10,... | collective-permute-start | bytes 1572872 | tf_op jit(solution)/shard_map/ppermute | solution.py:247
  71.9 23.5 %collective-permute-start.4 = (bf16[512,512]{1,0:T(8,128)(2,1)}, bf16[512,512]{1,0:T(8,128)(2,1)S(1)}, u32[]{:S(2)}, u32[]{:S(2)}) collective-permute-start(bf16[512,512]{1,0:T(8,128)(2,1)} %bitcast.11), channel_id=1, source_target_pairs={{0,16},{1,17},{2,18},{3,19},{4,20},{5,21},{6,22},{7,23},{8,24},{9,... | collective-permute-start | bytes 1572872 | tf_op jit(solution)/shard_map/ppermute | solution.py:247
  73.4 23.8 %collective-permute-start.5 = (bf16[512,512]{1,0:T(8,128)(2,1)}, bf16[512,512]{1,0:T(8,128)(2,1)S(1)}, u32[]{:S(2)}, u32[]{:S(2)}) collective-permute-start(bf16[512,512]{1,0:T(8,128)(2,1)} %collective-permute-done), channel_id=1, source_target_pairs={{0,16},{1,17},{2,18},{3,19},{4,20},{5,21},{6,22},{7,23},{8,24},{9,... | collective-permute-start | bytes 1572872 | tf_op jit(solution)/shard_map/ppermute | solution.py:247
  102.1 34.2 %all-to-all-start.2 = ((bf16[8,192,688]{2,1,0:T(8,128)(2,1)}), bf16[8,192,688]{2,1,0:T(8,128)(2,1)S(1)}, u32[]{:S(2)}, u32[]{:S(2)}) async-start(bf16[8,192,688]{2,1,0:T(8,128)(2,1)} %shard_map.240), calls=%async_computation.2 | async-start | bytes 4718592 | tf_op jit(solution)/shard_map/all_to_all | solution.py:267
  105.7 48.9 %collective-permute-start.6 = (bf16[2,4,2,64,512]{4,3,2,1,0:T(8,128)(2,1)}, bf16[2,4,2,64,512]{4,3,2,1,0:T(8,128)(2,1)}, u32[]{:S(2)}, u32[]{:S(2)}) collective-permute-start(bf16[2,4,2,64,512]{4,3,2,1,0:T(8,128)(2,1)} %bitcast.74), channel_id=1, source_target_pairs={{0,4},{1,5},{2,6},{3,7},{8,12},{9,13},{10,14},{11,15},{16,20},{17,... | collective-permute-start | bytes 3145736 | tf_op jit(solution)/shard_map/ppermute | solution.py:250
  109.4 31.3 %collective-permute-start.7 = (bf16[512,512]{1,0:T(8,128)(2,1)}, bf16[512,512]{1,0:T(8,128)(2,1)}, u32[]{:S(2)}, u32[]{:S(2)}) collective-permute-start(bf16[512,512]{1,0:T(8,128)(2,1)} %copy-done.40), channel_id=1, source_target_pairs={{0,16},{1,17},{2,18},{3,19},{4,20},{5,21},{6,22},{7,23},{8,24},{9,... | collective-permute-start | bytes 1572872 | tf_op jit(solution)/shard_map/ppermute | solution.py:247
  139.2 26.6 %collective-permute-start.8 = (bf16[688,512]{1,0:T(8,128)(2,1)}, bf16[688,512]{1,0:T(8,128)(2,1)}, u32[]{:S(2)}, u32[]{:S(2)}) collective-permute-start(bf16[688,512]{1,0:T(8,128)(2,1)} %get-tuple-element.82), channel_id=1, source_target_pairs={{0,16},{1,17},{2,18},{3,19},{4,20},{5,21},{6,22},{7,23},{8,24},{9,... | collective-permute-start | bytes 2113544 | tf_op jit(solution)/shard_map/ppermute | solution.py:247
  168.1 12.6 %collective-permute-start.9 = (bf16[512,2048]{1,0:T(8,128)(2,1)}, bf16[512,2048]{1,0:T(8,128)(2,1)}, u32[]{:S(2)}, u32[]{:S(2)}) collective-permute-start(bf16[512,2048]{1,0:T(8,128)(2,1)} %convolution_convert_fusion.1), channel_id=1, source_target_pairs={{0,8},{1,9},{2,10},{3,11},{4,12},{5,13},{6,14},{7,15},{8,0},{9,1},... | collective-permute-start | bytes 6291464 | tf_op jit(solution)/shard_map/ppermute | solution.py:247
  168.1 44.4 %collective-permute-start.10 = (bf16[688,512]{1,0:T(8,128)(2,1)}, bf16[688,512]{1,0:T(8,128)(2,1)}, u32[]{:S(2)}, u32[]{:S(2)}) collective-permute-start(bf16[688,512]{1,0:T(8,128)(2,1)} %get-tuple-element.82), channel_id=1, source_target_pairs={{0,4},{1,5},{2,6},{3,7},{4,0},{5,1},{6,2},{7,3},{8,12},{9,13},{10,... | collective-permute-start | bytes 2113544 | tf_op jit(solution)/shard_map/ppermute | solution.py:247
  212.5 29.7 %all-to-all-start.3 = ((bf16[4,128,2048]{2,1,0:T(8,128)(2,1)}), bf16[4,128,2048]{2,1,0:T(8,128)(2,1)}, u32[]{:S(2)}, u32[]{:S(2)}) async-start(bf16[4,128,2048]{2,1,0:T(8,128)(2,1)} %bitcast.107), calls=%async_computation.3 | async-start | bytes 4194304 | tf_op jit(solution)/shard_map/all_to_all | solution.py:296
  217.0 71.5 %all-gather.10.cloned.1.call-start = ((), (), s32[]{:S(2)}) async-start(), calls=%async_computation.11 | async-start | bytes 4718592 | tf_op jit(solution)/shard_map/all_gather | solution.py:279
  217.0 18.0 %collective-permute-start.11 = (bf16[688,512]{1,0:T(8,128)(2,1)}, bf16[688,512]{1,0:T(8,128)(2,1)}, u32[]{:S(2)}, u32[]{:S(2)}) collective-permute-start(bf16[688,512]{1,0:T(8,128)(2,1)} %copy-done.5), channel_id=1, source_target_pairs={{0,16},{1,17},{2,18},{3,19},{4,20},{5,21},{6,22},{7,23},{8,24},{9,... | collective-permute-start | bytes 2113544 | tf_op jit(solution)/shard_map/ppermute | solution.py:247
  246.6 94.7 %all-gather.12.cloned.1.call-start = ((), (), s32[]{:S(2)}) async-start(), calls=%async_computation.12 | async-start | bytes 4718592 | tf_op jit(solution)/shard_map/all_gather | solution.py:279
  247.2 34.3 %collective-permute-start.13 = (bf16[688,512]{1,0:T(8,128)(2,1)}, bf16[688,512]{1,0:T(8,128)(2,1)}, u32[]{:S(2)}, u32[]{:S(2)}) collective-permute-start(bf16[688,512]{1,0:T(8,128)(2,1)} %copy-done.4), channel_id=1, source_target_pairs={{0,16},{1,17},{2,18},{3,19},{4,20},{5,21},{6,22},{7,23},{8,24},{9,... | collective-permute-start | bytes 2113544 | tf_op jit(solution)/shard_map/ppermute | solution.py:247
  248.7 33.2 %collective-permute-start.12 = (bf16[688,512]{1,0:T(8,128)(2,1)}, bf16[688,512]{1,0:T(8,128)(2,1)}, u32[]{:S(2)}, u32[]{:S(2)}) collective-permute-start(bf16[688,512]{1,0:T(8,128)(2,1)} %copy-done.5), channel_id=1, source_target_pairs={{0,4},{1,5},{2,6},{3,7},{4,0},{5,1},{6,2},{7,3},{8,12},{9,13},{10,... | collective-permute-start | bytes 2113544 | tf_op jit(solution)/shard_map/ppermute | solution.py:247
  251.3 28.2 %collective-permute-start.14 = (bf16[688,512]{1,0:T(8,128)(2,1)}, bf16[688,512]{1,0:T(8,128)(2,1)}, u32[]{:S(2)}, u32[]{:S(2)}) collective-permute-start(bf16[688,512]{1,0:T(8,128)(2,1)} %collective-permute-done.10), channel_id=1, source_target_pairs={{0,16},{1,17},{2,18},{3,19},{4,20},{5,21},{6,22},{7,23},{8,24},{9,... | collective-permute-start | bytes 2113544 | tf_op jit(solution)/shard_map/ppermute | solution.py:247
  288.5 34.3 %collective-permute-start.16 = (bf16[688,512]{1,0:T(8,128)(2,1)}, bf16[688,512]{1,0:T(8,128)(2,1)S(1)}, u32[]{:S(2)}, u32[]{:S(2)}) collective-permute-start(bf16[688,512]{1,0:T(8,128)(2,1)} %copy-done.4), channel_id=1, source_target_pairs={{0,4},{1,5},{2,6},{3,7},{4,0},{5,1},{6,2},{7,3},{8,12},{9,13},{10,... | collective-permute-start | bytes 2113544 | tf_op jit(solution)/shard_map/ppermute | solution.py:247
  288.6 35.7 %collective-permute-start.15 = (bf16[688,512]{1,0:T(8,128)(2,1)}, bf16[688,512]{1,0:T(8,128)(2,1)S(1)}, u32[]{:S(2)}, u32[]{:S(2)}) collective-permute-start(bf16[688,512]{1,0:T(8,128)(2,1)} %collective-permute-done.12), channel_id=1, source_target_pairs={{0,16},{1,17},{2,18},{3,19},{4,20},{5,21},{6,22},{7,23},{8,24},{9,... | collective-permute-start | bytes 2113544 | tf_op jit(solution)/shard_map/ppermute | solution.py:247
  322.8 17.6 %collective-permute-start.17 = (bf16[688,512]{1,0:T(8,128)(2,1)S(1)}, bf16[688,512]{1,0:T(8,128)(2,1)S(1)}, u32[]{:S(2)}, u32[]{:S(2)}) collective-permute-start(bf16[688,512]{1,0:T(8,128)(2,1)S(1)} %collective-permute-done.16), channel_id=1, source_target_pairs={{0,16},{1,17},{2,18},{3,19},{4,20},{5,21},{6,22},{7,23},{8,24},{9,... | collective-permute-start | bytes 2113544 | tf_op jit(solution)/shard_map/ppermute | solution.py:247
  369.7 31.2 %all-to-all-start.4 = ((bf16[4,128,2048]{2,1,0:T(8,128)(2,1)}), bf16[4,128,2048]{2,1,0:T(8,128)(2,1)}, u32[]{:S(2)}, u32[]{:S(2)}) async-start(bf16[4,128,2048]{2,1,0:T(8,128)(2,1)} %bitcast.103), calls=%async_computation.4 | async-start | bytes 4194304 | tf_op jit(solution)/shard_map/all_to_all | solution.py:296
  374.1 91.5 %all-gather.14.cloned.1.call-start = ((), (), s32[]{:S(2)}) async-start(), calls=%async_computation.13 | async-start | bytes 4718592 | tf_op jit(solution)/shard_map/all_gather | solution.py:279
  374.3 33.7 %collective-permute-start.20 = (bf16[688,1024]{1,0:T(8,128)(2,1)}, bf16[688,1024]{1,0:T(8,128)(2,1)}, u32[]{:S(2)}, u32[]{:S(2)}) collective-permute-start(bf16[688,1024]{1,0:T(8,128)(2,1)} %fusion.26), channel_id=1, source_target_pairs={{0,16},{1,17},{2,18},{3,19},{4,20},{5,21},{6,22},{7,23},{8,24},{9,... | collective-permute-start | bytes 4227080 | tf_op jit(solution)/shard_map/ppermute | solution.py:247
  413.5 46.3 %collective-permute-start.19 = (bf16[512,2048]{1,0:T(8,128)(2,1)}, bf16[512,2048]{1,0:T(8,128)(2,1)}, u32[]{:S(2)}, u32[]{:S(2)}) collective-permute-start(bf16[512,2048]{1,0:T(8,128)(2,1)} %convolution_convert_fusion.3), channel_id=1, source_target_pairs={{0,8},{1,9},{2,10},{3,11},{4,12},{5,13},{6,14},{7,15},{8,0},{9,1},... | collective-permute-start | bytes 6291464 | tf_op jit(solution)/shard_map/ppermute | solution.py:247
  413.5 33.5 %collective-permute-start.21 = (bf16[688,1024]{1,0:T(8,128)(2,1)}, bf16[688,1024]{1,0:T(8,128)(2,1)S(1)}, u32[]{:S(2)}, u32[]{:S(2)}) collective-permute-start(bf16[688,1024]{1,0:T(8,128)(2,1)} %fusion.29), channel_id=1, source_target_pairs={{0,16},{1,17},{2,18},{3,19},{4,20},{5,21},{6,22},{7,23},{8,24},{9,... | collective-permute-start | bytes 4227080 | tf_op jit(solution)/shard_map/ppermute | solution.py:247
  418.1 36.7 %collective-permute-start.22 = (bf16[688,1024]{1,0:T(8,128)(2,1)S(1)}, bf16[688,1024]{1,0:T(8,128)(2,1)}, u32[]{:S(2)}, u32[]{:S(2)}) collective-permute-start(bf16[688,1024]{1,0:T(8,128)(2,1)S(1)} %add_convert_fusion.8.kept_ref), channel_id=1, source_target_pairs={{4,0},{5,1},{6,2},{7,3},{8,12},{9,13},{10,14},{11,15},{20,16},{21,... | collective-permute-start | bytes 4227080 | tf_op jit(solution)/shard_map/ppermute | solution.py:250
  449.7 49.1 %collective-permute-start.26 = (bf16[688,1024]{1,0:T(8,128)(2,1)}, bf16[688,1024]{1,0:T(8,128)(2,1)}, u32[]{:S(2)}, u32[]{:S(2)}) collective-permute-start(bf16[688,1024]{1,0:T(8,128)(2,1)} %add_convert_fusion.7.kept_ref), channel_id=1, source_target_pairs={{4,0},{5,1},{6,2},{7,3},{8,12},{9,13},{10,14},{11,15},{20,16},{21,... | collective-permute-start | bytes 4227080 | tf_op jit(solution)/shard_map/ppermute | solution.py:250
  457.6 34.2 %collective-permute-start.25 = (bf16[688,512]{1,0:T(8,128)(2,1)}, bf16[688,512]{1,0:T(8,128)(2,1)}, u32[]{:S(2)}, u32[]{:S(2)}) collective-permute-start(bf16[688,512]{1,0:T(8,128)(2,1)} %shard_map.244), channel_id=1, source_target_pairs={{0,8},{1,9},{2,10},{3,11},{12,4},{13,5},{14,6},{15,7},{16,24},{17,... | collective-permute-start | bytes 2113544 | tf_op jit(solution)/shard_map/ppermute | solution.py:250
  465.6 81.4 %all-to-all-start.5 = ((bf16[4,128,2048]{2,1,0:T(8,128)(2,1)}), bf16[4,128,2048]{2,1,0:T(8,128)(2,1)}, u32[]{:S(2)}, u32[]{:S(2)}) async-start(bf16[4,128,2048]{2,1,0:T(8,128)(2,1)} %bitcast.105), calls=%async_computation.5 | async-start | bytes 4194304 | tf_op jit(solution)/shard_map/all_to_all | solution.py:296
  486.1 57.2 %collective-permute-start.23 = (bf16[512,2048]{1,0:T(8,128)(2,1)}, bf16[512,2048]{1,0:T(8,128)(2,1)}, u32[]{:S(2)}, u32[]{:S(2)}) collective-permute-start(bf16[512,2048]{1,0:T(8,128)(2,1)} %convolution_convert_fusion), channel_id=1, source_target_pairs={{0,8},{1,9},{2,10},{3,11},{4,12},{5,13},{6,14},{7,15},{8,0},{9,1},... | collective-permute-start | bytes 6291464 | tf_op jit(solution)/shard_map/ppermute | solution.py:247
  489.8 32.6 %collective-permute-start.27 = (bf16[688,1024]{1,0:T(8,128)(2,1)}, bf16[688,1024]{1,0:T(8,128)(2,1)}, u32[]{:S(2)}, u32[]{:S(2)}) collective-permute-start(bf16[688,1024]{1,0:T(8,128)(2,1)} %fusion.32), channel_id=1, source_target_pairs={{0,16},{1,17},{2,18},{3,19},{4,20},{5,21},{6,22},{7,23},{8,24},{9,... | collective-permute-start | bytes 4227080 | tf_op jit(solution)/shard_map/ppermute | solution.py:247
  490.4 50.2 %collective-permute-start.24 = (bf16[2,4,2,64,512]{4,3,2,1,0:T(8,128)(2,1)}, bf16[2,4,2,64,512]{4,3,2,1,0:T(8,128)(2,1)}, u32[]{:S(2)}, u32[]{:S(2)}) collective-permute-start(bf16[2,4,2,64,512]{4,3,2,1,0:T(8,128)(2,1)} %get-tuple-element.105), channel_id=1, source_target_pairs={{4,0},{5,1},{6,2},{7,3},{12,8},{13,9},{14,10},{15,11},{20,16},{21,... | collective-permute-start | bytes 3145736 | tf_op jit(solution)/shard_map/ppermute | solution.py:250
  547.0 31.8 %all-to-all-start.6 = ((bf16[4,128,2048]{2,1,0:T(8,128)(2,1)}), bf16[4,128,2048]{2,1,0:T(8,128)(2,1)}, u32[]{:S(2)}, u32[]{:S(2)}) async-start(bf16[4,128,2048]{2,1,0:T(8,128)(2,1)} %bitcast.106), calls=%async_computation.6 | async-start | bytes 4194304 | tf_op jit(solution)/shard_map/all_to_all | solution.py:296
  563.2 26.1 %collective-permute-start.29 = (bf16[1024,512]{1,0:T(8,128)(2,1)S(1)}, bf16[1024,512]{1,0:T(8,128)(2,1)}, u32[]{:S(2)}, u32[]{:S(2)}) collective-permute-start(bf16[1024,512]{1,0:T(8,128)(2,1)S(1)} %pad_maximum_fusion.3), channel_id=1, source_target_pairs={{0,16},{1,17},{2,18},{3,19},{4,20},{5,21},{6,22},{7,23},{8,24},{9,... | collective-permute-start | bytes 3145736 | tf_op jit(solution)/shard_map/ppermute | solution.py:247
  564.5 46.7 %collective-permute-start.34 = (bf16[1024,512]{1,0:T(8,128)(2,1)}, bf16[1024,512]{1,0:T(8,128)(2,1)}, u32[]{:S(2)}, u32[]{:S(2)}) collective-permute-start(bf16[1024,512]{1,0:T(8,128)(2,1)} %get-tuple-element.146), channel_id=1, source_target_pairs={{0,16},{1,17},{2,18},{3,19},{4,20},{5,21},{6,22},{7,23},{8,24},{9,... | collective-permute-start | bytes 3145736 | tf_op jit(solution)/shard_map/ppermute | solution.py:247
  565.2 48.9 %collective-permute-start.30 = (bf16[688,1024]{1,0:T(8,128)(2,1)}, bf16[688,1024]{1,0:T(8,128)(2,1)}, u32[]{:S(2)}, u32[]{:S(2)}) collective-permute-start(bf16[688,1024]{1,0:T(8,128)(2,1)} %add_convert_fusion.6.kept_ref), channel_id=1, source_target_pairs={{4,0},{5,1},{6,2},{7,3},{8,12},{9,13},{10,14},{11,15},{20,16},{21,... | collective-permute-start | bytes 4227080 | tf_op jit(solution)/shard_map/ppermute | solution.py:250
  578.8 105.1 %all-to-all-start.7 = ((bf16[4,128,2048]{2,1,0:T(8,128)(2,1)}), bf16[4,128,2048]{2,1,0:T(8,128)(2,1)}, u32[]{:S(2)}, u32[]{:S(2)}) async-start(bf16[4,128,2048]{2,1,0:T(8,128)(2,1)} %bitcast.104), calls=%async_computation.7 | async-start | bytes 4194304 | tf_op jit(solution)/shard_map/all_to_all | solution.py:296
  614.2 40.2 %collective-permute-start.31 = (bf16[1024,512]{1,0:T(8,128)(2,1)S(1)}, bf16[1024,512]{1,0:T(8,128)(2,1)}, u32[]{:S(2)}, u32[]{:S(2)}) collective-permute-start(bf16[1024,512]{1,0:T(8,128)(2,1)S(1)} %fusion.5.kept_ref), channel_id=1, source_target_pairs={{4,0},{5,1},{6,2},{7,3},{8,12},{9,13},{10,14},{11,15},{20,16},{21,... | collective-permute-start | bytes 3145736 | tf_op jit(solution)/shard_map/ppermute | solution.py:250
  615.5 50.1 %collective-permute-start.35 = (bf16[1024,512]{1,0:T(8,128)(2,1)S(1)}, bf16[1024,512]{1,0:T(8,128)(2,1)}, u32[]{:S(2)}, u32[]{:S(2)}) collective-permute-start(bf16[1024,512]{1,0:T(8,128)(2,1)S(1)} %get-tuple-element.115.kept_ref), channel_id=1, source_target_pairs={{4,0},{5,1},{6,2},{7,3},{8,12},{9,13},{10,14},{11,15},{20,16},{21,... | collective-permute-start | bytes 3145736 | tf_op jit(solution)/shard_map/ppermute | solution.py:250
  631.2 40.8 %collective-permute-start.37 = (bf16[688,512]{1,0:T(8,128)(2,1)}, bf16[688,512]{1,0:T(8,128)(2,1)}, u32[]{:S(2)}, u32[]{:S(2)}) collective-permute-start(bf16[688,512]{1,0:T(8,128)(2,1)} %shard_map.253), channel_id=1, source_target_pairs={{0,8},{1,9},{2,10},{3,11},{12,4},{13,5},{14,6},{15,7},{16,24},{17,... | collective-permute-start | bytes 2113544 | tf_op jit(solution)/shard_map/ppermute | solution.py:250
  657.0 18.2 %collective-permute-start.33 = (bf16[512,512]{1,0:T(8,128)(2,1)}, bf16[512,512]{1,0:T(8,128)(2,1)}, u32[]{:S(2)}, u32[]{:S(2)}) collective-permute-start(bf16[512,512]{1,0:T(8,128)(2,1)} %shard_map.248), channel_id=1, source_target_pairs={{0,8},{1,9},{2,10},{3,11},{12,4},{13,5},{14,6},{15,7},{16,24},{17,... | collective-permute-start | bytes 1572872 | tf_op jit(solution)/shard_map/ppermute | solution.py:250
  688.5 10.9 %all-to-all-start.8 = ((f32[32,1,192]{2,1,0:T(1,128)}), f32[32,1,192]{2,1,0:T(1,128)S(1)}, u32[]{:S(2)}, u32[]{:S(2)}) async-start(f32[32,1,192]{2,1,0:T(1,128)} %reshape.212), calls=%async_computation.8 | async-start | bytes 65536 | tf_op jit(solution)/shard_map/all_to_all | solution.py:367
  (77 other events, 764.6 us)
Sparse Core Ops, SparseCore 0:
  24.9 44.0 all-gather.5
  71.2 41.6 all-gather.7
  246.7 41.7 all-gather.9
  290.5 45.0 all-gather.11
  408.2 41.5 all-gather.13

commit v2 on v1

--- a/solution.py
+++ b/solution.py
@@ -293,6 +293,7 @@
     kept = kept.reshape(at.half_bit, -1, kept.shape[1])
     if before:
         kept = after(kept, *before)
+    at.kept = kept
     kept = lax.all_to_all(kept, INNER, split_axis=0, concat_axis=0, tiled=True)
     if behind:
         kept = after(kept, *behind)
@@ -475,6 +476,7 @@
         )
     cache = heads(cache)
     other_cache = at.send(cache, at.half_bit, first_half)
+    gathered_tokens = token_all
     token_all = after(token_all, other_cache)
     query_far_half = at.swap(after(query_half, cache), at.far_bit)
     query_parts = [query_near, query_half, query_far, query_far_half]
@@ -482,7 +484,7 @@
     out_w = jnp.concatenate([part[:, own_width:] for part in query_parts], axis=0)
     queries = heads(widen(times(token_all, query_w, bf16)))
     gate_near, up_near, down_near = near_weights(
-        at, [w_gate, w_up, w_down], None, query_near, cache
+        at, [w_gate, w_up, w_down], None, gathered_tokens, cache
     )
     (mixed,) = attention_call(
         functools.partial(attend_kernel, scale),
@@ -501,18 +503,18 @@
     def whole(near, half_part, far_part, far_half_part):
         return jnp.concatenate([near, half_part, far_part, far_half_part], axis=1)
 
+    up_half = at.swap(after(up_near, gate_half), at.half_bit)
     residual = residual_in + scatter(
-        at, [(mixed, out_w)], times_transposed, (gate_half,), (up_far,)
+        at, [(mixed, out_w)], times_transposed, (gate_half,), (up_half, up_far)
     )
     ffn_normed, ffn_inverse = normalize(residual)
     ffn_in = (ffn_normed * gain_ffn).astype(bf16)
-    up_half = at.swap(after(up_near, gate_half), at.half_bit)
+    down_half = at.swap(after(down_near, up_half), at.half_bit)
     gate_w = whole(gate_near, gate_half, gate_far, at.swap(gate_half, at.far_bit))
-    ffn_all = after(gather(at, ffn_in), up_half, down_far, gate_w)
-    final_all = gather(at, after(grad_final.astype(bf16), ffn_all))
-    down_half = at.swap(after(down_near, up_half), at.half_bit)
+    up_w = whole(up_near, up_half, up_far, at.swap(up_half, at.far_bit))
+    ffn_all = after(gather(at, ffn_in), down_half, down_far, gate_w, up_w)
+    final_all = gather(at, after(grad_final.astype(bf16), other_cache))
     gate = times_transposed(ffn_all, gate_w)
-    up_w = whole(up_near, up_half, up_far, at.swap(up_half, at.far_bit))
     up = times_transposed(ffn_all, after(up_w, gate))
     down_w = whole(
         down_near, after(down_half, up), down_far, at.swap(down_half, at.far_bit)
@@ -547,7 +549,7 @@
     grad_mixed = heads(widen(times(branch_all, out_w, bf16)))
     grad_queries, grad_cache, grad_other_cache = attention_call(
         functools.partial(attend_back_kernel, scale),
-        [queries, cache, other_cache, after(grad_mixed, gate_grad.back)],
+        [queries, cache, other_cache, grad_mixed],
         info,
         key_places,
         [
@@ -558,14 +560,14 @@
     )
     given_cache = at.send(grad_other_cache, at.half_bit, second_half)
     grad_queries = narrow(grad_queries.reshape(group * count, width))
-    output = residual + scatter(at, [(hidden, down_w)], times, (gathered,))
+    grad_token_in = scatter(at, [(grad_queries, query_w)])
     gate_grad.to_twin()
     (gate_out,) = gate_grad.finish()
     query_grad = Gradient(at, [(token_all, grad_queries), (branch_all, mixed)])
 
-    grad_token_in = scatter(at, [(grad_queries, query_w)])
-    given_cache = after(given_cache, gate_out, up_grad.back, query_grad.there, down_grad.given)
-    down_grad.across(given_cache)
+    given_cache = after(
+        given_cache, gate_out, up_grad.back, query_grad.given, down_grad.given
+    )
     up_grad.to_twin()
     grad_cache = (grad_cache + given_cache.astype(f32)).astype(bf16)
     grad_cache = grad_cache.reshape(group * count, 2 * width)
@@ -574,21 +576,20 @@
             [narrow(grad_cache[:, :width]), narrow(grad_cache[:, width:])], axis=1
         )
     cache_grad = Gradient(at, [(memory_all, grad_cache)])
-    query_grad.across(down_grad.back)
-    cache_grad.across(down_grad.back)
+    down_grad.across(grad_cache)
+    before = (cache_grad.given, down_grad.back)
+    cache_grad.across()
     grad_memory_in = scatter(
         at,
-        [(after(grad_cache, cache_grad.there), cache_w)],
+        [(after(grad_cache, cache_grad.there, down_grad.kept), cache_w)],
         times_transposed,
-        (),
-        (query_grad.back, up_grad.twins),
-    )
-    for grad in (down_grad, query_grad, cache_grad):
-        grad.to_twin()
-    (up_out,), (down_out,) = (grad.finish() for grad in (up_grad, down_grad))
-    query_out, out_out = query_grad.finish(own_width)
-    key_out, value_out = cache_grad.finish(unit)
-
+        before,
+        (up_grad.twins,),
+    )
+    query_grad.across(cache_grad.kept)
+    down_grad.to_twin()
+    (up_out,) = up_grad.finish()
+    cache_grad.to_twin()
     cut = model_width // 2
     gain_memory_term = (
         jnp.concatenate(
@@ -600,17 +601,36 @@
         / gain_memory[0]
     )
     gain_attn_term = jnp.sum(grad_token_in * token_normed, axis=0)
-    gain_grads = reduce_gains(at, jnp.stack([gain_attn_term, gain_memory_term, gain_ffn_term]))
-
-    grad_tokens = grad_residual + norm_back(grad_token_in, token_normed, token_inverse, gain_attn)
-    grad_memory = norm_back(grad_memory_in, memory_normed, memory_inverse, gain_memory)
-    leaving = [a.astype(bf16) for a in (output, grad_tokens, grad_memory)]
-    leaving = local_call(
-        functools.partial(move_kernel, restored),
-        [sides],
-        leaving,
-        [jax.ShapeDtypeStruct(a.shape, a.dtype) for a in leaving],
-    )
+    gain_terms = jnp.stack([gain_attn_term, gain_memory_term, gain_ffn_term])
+    gain_grads = reduce_gains(at, gain_terms)
+
+    def left(value):
+        value = value.astype(bf16)
+        (value,) = local_call(
+            functools.partial(move_kernel, restored),
+            [sides],
+            [value],
+            [jax.ShapeDtypeStruct(value.shape, value.dtype)],
+        )
+        return value
+
+    output_term = scatter(
+        at,
+        [(after(hidden, at.kept, cache_grad.kept), down_w)],
+        times,
+        (cache_grad.back, gain_grads),
+        (query_grad.back, cache_grad.twins, up_out, down_grad.twins),
+    )
+    grad_tokens = left(
+        grad_residual + norm_back(grad_token_in, token_normed, token_inverse, gain_attn)
+    )
+    grad_memory = left(norm_back(grad_memory_in, memory_normed, memory_inverse, gain_memory))
+    output = left(residual + output_term)
+    leaving = [output, grad_tokens, grad_memory]
+    query_grad.to_twin()
+    (down_out,) = down_grad.finish()
+    query_out, out_out = query_grad.finish(own_width)
+    key_out, value_out = cache_grad.finish(unit)
     output, grad_tokens, grad_memory = (
         a.reshape(rows_here, tok_row, model_width) for a in leaving
     )

time: 718 us -> 754 us (1.050)
  waiting for transfers between devices: 353 us -> 383 us
    ppermute x12, waiting for transfers between devices: 61.9 us -> 93.3 us  [send(): lax.ppermute(value, AXES, [(i, i ^ mask) for i in range(self.count) if ch...]
    all_to_all x1, waiting for transfers between devices: 3.29 us -> 30.9 us  [reduce_gains(): terms = lax.all_to_all(terms, AXES, split_axis=0, concat_axis=0, tiled=True)]
    ppermute x26, waiting for transfers between devices: 207 us -> 191 us  [swap(): return lax.ppermute(value, AXES, [(i, i ^ mask) for i in range(self.count)])]
    all_to_all x5, waiting for transfers between devices: 35.7 us -> 22 us  [scatter(): kept = lax.all_to_all(kept, INNER, split_axis=0, concat_axis=0, tiled=True)]
    unnamed x159 -> x155, local copies, waits for them, and re-layouts: 27 us -> 22.2 us
  transfers between devices with their start and end apart: 52 -> 52, of which waited for: 28 -> 24; matrix products, arithmetic and copies ran while one was open for 19% -> 19% of each run, Pallas kernels for 8% -> 7%
where the time goes in v2:
time: 754 us; the launch traced here: 744 us
  waiting for transfers between devices  383 us (51%)
  matrix products  114 us (15%)
  starting transfers between devices  108 us (14%)
  Pallas kernels  56.7 us (8%)
  local copies, waits for them, and re-layouts  34.6 us (5%)
  other arithmetic  31.9 us (4%)
  between operations  15.5 us (2%)
    ppermute x26, waiting for transfers between devices, swap(): return lax.ppermute(value, AXES, [(i, i ^ mask) for i in range(self.count)])  191 us
    dot_general x30, matrix products, dot(): lax.dot_general(left, right, (over, ((), ())), preferred_element_type=kind)  114 us
    ppermute x12, waiting for transfers between devices, send(): lax.ppermute(value, AXES, [(i, i ^ mask) for i in range(self.count) if ch...  93.3 us
    ppermute x26, starting transfers between devices, swap(): return lax.ppermute(value, AXES, [(i, i ^ mask) for i in range(self.count)])  40.8 us
    all_to_all x1, waiting for transfers between devices, reduce_gains(): terms = lax.all_to_all(terms, AXES, split_axis=0, concat_axis=0, tiled=True)  30.9 us
    pallas_call x10, Pallas kernels, halves_call(): pl.pallas_call(kernel, grid_spec=pltpu.PrefetchScalarGridSpec(num_scalar_...  29.2 us
    all_to_all x3, waiting for transfers between devices, near_weights(): lax.all_to_all(blocks, GROUP, split_axis=0, concat_axis=0, tiled=True)  24.5 us
    all_to_all x5, starting transfers between devices, scatter(): kept = lax.all_to_all(kept, INNER, split_axis=0, concat_axis=0, tiled=True)  22.5 us
  transfers between devices with their start and end apart: 52, of which 24 were waited for; matrix products, arithmetic and copies ran while one was open for 19% of the time, Pallas kernels for 7%

profile of v2, /device:TPU:0, one launch (start us, length us, event | category | flops | bytes accessed | tf_op | source)
XLA Modules:
  0.0 743.6 jit_solution(1986589716032357573)
XLA Ops:
  10.1 5.3 all-to-all-start
  18.4 6.3 all-to-all-done
  26.3 4.1 all-to-all-start.1
  39.1 18.5 %collective-permute-done = bf16[512,512]{1,0:T(8,128)(2,1)} collective-permute-done((bf16[512,512]{1,0:T(8,128)(2,1)}, bf16[512,512]{1,0:T(8,128)(2,1)}, u32[]{:S(2)}, u32[]{:S(2)}) %collective-permute-start) | collective-permute-done | bytes 524320 | tf_op jit(solution)/shard_map/ppermute | solution.py:247
  57.7 11.3 %all-gather.6.cloned.1.call-done = bf16[1024,2048]{1,0:T(8,128)(2,1)} async-done(((bf16[128,2048]{1,0:T(8,128)(2,1)}), bf16[1024,2048]{1,0:T(8,128)(2,1)}) %all-gather.6.cloned.1.call-update) | async-done | bytes 4194320 | tf_op jit(solution)/shard_map/all_gather | solution.py:279
  76.0 19.5 %collective-permute-done.3 = bf16[512,512]{1,0:T(8,128)(2,1)} collective-permute-done((bf16[512,512]{1,0:T(8,128)(2,1)}, bf16[512,512]{1,0:T(8,128)(2,1)}, u32[]{:S(2)}, u32[]{:S(2)}) %collective-permute-start.3) | collective-permute-done | bytes 524320 | tf_op jit(solution)/shard_map/ppermute | solution.py:247
  98.0 4.7 fusion.103
  102.7 8.9 %all-gather.8.cloned.1.call-done = bf16[1024,2048]{1,0:T(8,128)(2,1)} async-done(((bf16[128,2048]{1,0:T(8,128)(2,1)}), bf16[1024,2048]{1,0:T(8,128)(2,1)}) %all-gather.8.cloned.1.call-update) | async-done | bytes 4194320 | tf_op jit(solution)/shard_map/all_gather | solution.py:279
  111.6 3.6 all-to-all-start.2
  115.3 3.6 collective-permute-start.6
  126.0 18.1 %all-to-all-done.2.source = bf16[8,192,688]{2,1,0:T(8,128)(2,1)S(1)} async-done(((bf16[8,192,688]{2,1,0:T(8,128)(2,1)}), bf16[8,192,688]{2,1,0:T(8,128)(2,1)S(1)}, u32[]{:S(2)}, u32[]{:S(2)}) %all-to-all-start.2) | async-done | bytes 2113568 | tf_op jit(solution)/shard_map/all_to_all | solution.py:267
  148.0 16.2 %collective-permute-done.6.okv_ref = bf16[2,4,2,64,512]{4,3,2,1,0:T(8,128)(2,1)} collective-permute-done((bf16[2,4,2,64,512]{4,3,2,1,0:T(8,128)(2,1)}, bf16[2,4,2,64,512]{4,3,2,1,0:T(8,128)(2,1)}, u32[]{:S(2)}, u32[]{:S(2)}) %collective-permute-start.6) | collective-permute-done | bytes 1048608 | tf_op jit(solution)/shard_map/ppermute | solution.py:250
  167.9 7.5 %shard_map.242 = bf16[2,4,2,64,256]{4,3,2,1,0:T(8,128)(2,1)S(1)} custom-call(bf16[2,4,2,64,256]{4,3,2,1,0:T(8,128)(2,1)S(1)} %bitcast.77, bf16[2,4,2,64,512]{4,3,2,1,0:T(8,128)(2,1)S(1)} %bitcast.75, bf16[2,4,2,64,512]{4,3,2,1,0:T(8,128)(2,1)} %collective-permute-done.6.okv_ref, s32[2,2,256,2]{3,2,1,0:T(8,128)S(1)} %copy-done, ...), custom_call_target="tpu_custom_call" | custom-call | flops 1 | bytes 1 | tf_op jit(solution)/shard_map/pallas_call | solution.py:114
  177.5 8.8 %collective-permute-start.10 = (bf16[688,512]{1,0:T(8,128)(2,1)}, bf16[688,512]{1,0:T(8,128)(2,1)}, u32[]{:S(2)}, u32[]{:S(2)}) collective-permute-start(bf16[688,512]{1,0:T(8,128)(2,1)} %get-tuple-element.80), channel_id=1, source_target_pairs={{0,4},{1,5},{2,6},{3,7},{4,0},{5,1},{6,2},{7,3},{8,12},{9,13},{10,... | collective-permute-start | bytes 2113544 | tf_op jit(solution)/shard_map/ppermute | solution.py:247
  186.3 4.0 add_convert_fusion.5
  190.3 27.8 %collective-permute-done.10 = bf16[688,512]{1,0:T(8,128)(2,1)} collective-permute-done((bf16[688,512]{1,0:T(8,128)(2,1)}, bf16[688,512]{1,0:T(8,128)(2,1)}, u32[]{:S(2)}, u32[]{:S(2)}) %collective-permute-start.10) | collective-permute-done | bytes 704544 | tf_op jit(solution)/shard_map/ppermute | solution.py:247
  218.1 4.5 all-to-all-start.3
  224.9 15.6 %collective-permute-done.12 = bf16[688,512]{1,0:T(8,128)(2,1)} collective-permute-done((bf16[688,512]{1,0:T(8,128)(2,1)}, bf16[688,512]{1,0:T(8,128)(2,1)}, u32[]{:S(2)}, u32[]{:S(2)}) %collective-permute-start.12) | collective-permute-done | bytes 704544 | tf_op jit(solution)/shard_map/ppermute | solution.py:247
  240.5 20.2 %collective-permute-done.11 = bf16[688,512]{1,0:T(8,128)(2,1)} collective-permute-done((bf16[688,512]{1,0:T(8,128)(2,1)}, bf16[688,512]{1,0:T(8,128)(2,1)}, u32[]{:S(2)}, u32[]{:S(2)}) %collective-permute-start.11) | collective-permute-done | bytes 704544 | tf_op jit(solution)/shard_map/ppermute | solution.py:247
  284.5 19.5 %collective-permute-done.15 = bf16[688,512]{1,0:T(8,128)(2,1)S(1)} collective-permute-done((bf16[688,512]{1,0:T(8,128)(2,1)}, bf16[688,512]{1,0:T(8,128)(2,1)S(1)}, u32[]{:S(2)}, u32[]{:S(2)}) %collective-permute-start.15) | collective-permute-done | bytes 704544 | tf_op jit(solution)/shard_map/ppermute | solution.py:247
  308.6 10.5 %collective-permute-done.16 = bf16[688,512]{1,0:T(8,128)(2,1)S(1)} collective-permute-done((bf16[688,512]{1,0:T(8,128)(2,1)}, bf16[688,512]{1,0:T(8,128)(2,1)S(1)}, u32[]{:S(2)}, u32[]{:S(2)}) %collective-permute-start.16) | collective-permute-done | bytes 704544 | tf_op jit(solution)/shard_map/ppermute | solution.py:247
  320.1 8.0 %fusion.109 = f32[1024,688]{0,1:T(8,128)} fusion(bf16[1024,2048]{1,0:T(8,128)(2,1)} %all-gather.10.cloned.1.call-done, bf16[688,2048]{1,0:T(8,128)(2,1)} %copy-done.30), kind=kOutput, calls=%fused_computation.175 | convolution fusion | flops 2885681152 | bytes 9830400 | tf_op jit(solution)/shard_map/dot_general | solution.py:22
  328.1 6.6 fusion.110
  341.2 9.8 %multiply_convert_fusion.1 = (bf16[1024,688]{0,1:T(8,128)(2,1)S(1)}, bf16[1024,688]{0,1:T(8,128)(2,1)S(1)}, bf16[1024,688]{0,1:T(8,128)(2,1)}) fusion(f32[1024,688]{0,1:T(8,128)} %fusion.109, f32[1024,688]{0,1:T(8,128)} %fusion.110, bf16[1024,2048]{1,0:T(8,128)(2,1)} %all-gather.12.cloned.1.call-done, bf16[688,2048]{1,0:T(8,128)(2,1)} %constant_dynamic-update-slice_fusion.8), kind=kOutput, calls=%fused_computation.19 | convolution fusion | flops 2896248832 | bytes 16875520 | tf_op jit(solution)/shard_map/dot_general | solution.py:22
  351.0 4.7 fusion.74
  363.2 3.7 fusion.77
  369.4 4.5 all-to-all-start.4
  375.5 4.7 fusion.29
  380.2 19.9 %all-to-all-done.4 = bf16[4,128,2048]{2,1,0:T(8,128)(2,1)} async-done(((bf16[4,128,2048]{2,1,0:T(8,128)(2,1)}), bf16[4,128,2048]{2,1,0:T(8,128)(2,1)}, u32[]{:S(2)}, u32[]{:S(2)}) %all-to-all-start.4) | async-done | bytes 2097184 | tf_op jit(solution)/shard_map/all_to_all | solution.py:297
  409.0 30.9 %collective-permute-done.20 = bf16[688,1024]{1,0:T(8,128)(2,1)S(1)} collective-permute-done((bf16[688,1024]{1,0:T(8,128)(2,1)}, bf16[688,1024]{1,0:T(8,128)(2,1)S(1)}, u32[]{:S(2)}, u32[]{:S(2)}) %collective-permute-start.20) | collective-permute-done | bytes 1409056 | tf_op jit(solution)/shard_map/ppermute | solution.py:247
  439.9 4.8 add_convert_fusion.7.kept_ref
  446.4 4.1 add_convert_fusion.8.kept_ref
  456.1 3.6 fusion.101
  459.8 9.9 %shard_map.243 = (bf16[2,4,2,64,256]{4,3,2,1,0:T(8,128)(2,1)S(1)}, f32[2,4,2,64,512]{4,3,2,1,0:T(8,128)}, bf16[2,4,2,64,512]{4,3,2,1,0:T(8,128)(2,1)}) custom-call(bf16[2,4,2,64,256]{4,3,2,1,0:T(8,128)(2,1)S(1)} %bitcast.78, bf16[2,4,2,64,512]{4,3,2,1,0:T(8,128)(2,1)S(1)} %bitcast.76, bf16[2,4,2,64,512]{4,3,2,1,0:T(8,128)(2,1)} %collective-permute-done.6.okv_ref, ...), custom_call_target="tpu_custom_call" | custom-call | flops 1 | bytes 1 | tf_op jit(solution)/shard_map/pallas_call | solution.py:114
  477.9 67.8 %collective-permute-done.22.given_ref = bf16[688,1024]{1,0:T(8,128)(2,1)} collective-permute-done((bf16[688,1024]{1,0:T(8,128)(2,1)}, bf16[688,1024]{1,0:T(8,128)(2,1)}, u32[]{:S(2)}, u32[]{:S(2)}) %collective-permute-start.22) | collective-permute-done | bytes 1409056 | tf_op jit(solution)/shard_map/ppermute | solution.py:250
  552.0 5.1 add_convert_fusion.6.kept_ref
  563.7 3.7 add_convert_fusion
  567.3 4.7 all-to-all-start.5
  582.3 4.0 add_convert_fusion.2
  586.2 19.2 %collective-permute-done.28 = bf16[1024,512]{1,0:T(8,128)(2,1)S(1)} collective-permute-done((bf16[1024,512]{1,0:T(8,128)(2,1)S(1)}, bf16[1024,512]{1,0:T(8,128)(2,1)S(1)}, u32[]{:S(2)}, u32[]{:S(2)}) %collective-permute-start.28) | collective-permute-done | bytes 1048608 | tf_op jit(solution)/shard_map/ppermute | solution.py:247
  605.4 9.3 %collective-permute-done.29.given_ref = bf16[688,1024]{1,0:T(8,128)(2,1)S(1)} collective-permute-done((bf16[688,1024]{1,0:T(8,128)(2,1)S(1)}, bf16[688,1024]{1,0:T(8,128)(2,1)S(1)}, u32[]{:S(2)}, u32[]{:S(2)}) %collective-permute-start.29) | collective-permute-done | bytes 1409056 | tf_op jit(solution)/shard_map/ppermute | solution.py:250
  615.9 4.4 all-to-all-start.8
  628.5 3.7 multiply_reduce_fusion.1
  632.2 5.2 convolution_convert_fusion.2
  649.0 8.8 %all-to-all-start.6 = ((f32[32,1,192]{2,1,0:T(1,128)}), f32[32,1,192]{2,1,0:T(1,128)S(1)}, u32[]{:S(2)}, u32[]{:S(2)}) async-start(f32[32,1,192]{2,1,0:T(1,128)} %reshape.212), calls=%async_computation.6 | async-start | bytes 65536 | tf_op jit(solution)/shard_map/all_to_all | solution.py:368
  657.7 5.8 add_convert_fusion.1
  663.5 30.9 %all-to-all-done.6 = f32[32,1,192]{2,1,0:T(1,128)S(1)} async-done(((f32[32,1,192]{2,1,0:T(1,128)}), f32[32,1,192]{2,1,0:T(1,128)S(1)}, u32[]{:S(2)}, u32[]{:S(2)}) %all-to-all-start.6) | async-done | bytes 24608 | tf_op jit(solution)/shard_map/all_to_all | solution.py:368
  695.8 4.5 all-to-all-start.7
  (332 shorter events, 197.3 us)
Async XLA Ops:
  10.1 14.6 %all-to-all-start = ((bf16[8,64,512]{2,1,0:T(8,128)(2,1)}), bf16[8,64,512]{2,1,0:T(8,128)(2,1)}, u32[]{:S(2)}, u32[]{:S(2)}) async-start(bf16[8,64,512]{2,1,0:T(8,128)(2,1)} %shard_map.238), calls=%async_computation | async-start | bytes 1048576 | tf_op jit(solution)/shard_map/all_to_all | solution.py:267
  15.4 53.6 %all-gather.6.cloned.1.call-start = ((), (), s32[]{:S(2)}) async-start(), calls=%async_computation.9 | async-start | bytes 4718592 | tf_op jit(solution)/shard_map/all_gather | solution.py:279
  25.0 10.9 %collective-permute-start.2 = (s32[2,8]{1,0:T(2,128)S(1)}, s32[2,8]{1,0:T(2,128)S(1)}, u32[]{:S(2)}, u32[]{:S(2)}) collective-permute-start(s32[2,8]{1,0:T(2,128)S(1)} %reduce_window_sum.11), channel_id=1, source_target_pairs={{0,8},{1,9},{2,10},{3,11},{4,12},{5,13},{6,14},{7,15},{8,0},{9,1},... | collective-permute-start | bytes 200 | tf_op jit(solution)/shard_map/ppermute | solution.py:247
  26.3 31.4 %all-to-all-start.1 = ((bf16[8,64,512]{2,1,0:T(8,128)(2,1)}), bf16[8,64,512]{2,1,0:T(8,128)(2,1)}, u32[]{:S(2)}, u32[]{:S(2)}) async-start(bf16[8,64,512]{2,1,0:T(8,128)(2,1)} %shard_map.239), calls=%async_computation.1 | async-start | bytes 1048576 | tf_op jit(solution)/shard_map/all_to_all | solution.py:267
  30.5 81.2 %all-gather.8.cloned.1.call-start = ((), (), s32[]{:S(2)}) async-start(), calls=%async_computation.10 | async-start | bytes 4718592 | tf_op jit(solution)/shard_map/all_gather | solution.py:279
  31.5 26.2 %collective-permute-start = (bf16[512,512]{1,0:T(8,128)(2,1)}, bf16[512,512]{1,0:T(8,128)(2,1)}, u32[]{:S(2)}, u32[]{:S(2)}) collective-permute-start(bf16[512,512]{1,0:T(8,128)(2,1)} %bitcast.10), channel_id=1, source_target_pairs={{0,4},{1,5},{2,6},{3,7},{4,0},{5,1},{6,2},{7,3},{8,12},{9,13},{10,... | collective-permute-start | bytes 1572872 | tf_op jit(solution)/shard_map/ppermute | solution.py:247
  34.4 23.3 %collective-permute-start.1 = (bf16[512,512]{1,0:T(8,128)(2,1)}, bf16[512,512]{1,0:T(8,128)(2,1)}, u32[]{:S(2)}, u32[]{:S(2)}) collective-permute-start(bf16[512,512]{1,0:T(8,128)(2,1)} %bitcast.10), channel_id=1, source_target_pairs={{0,16},{1,17},{2,18},{3,19},{4,20},{5,21},{6,22},{7,23},{8,24},{9,... | collective-permute-start | bytes 1572872 | tf_op jit(solution)/shard_map/ppermute | solution.py:247
  69.0 26.5 %collective-permute-start.3 = (bf16[512,512]{1,0:T(8,128)(2,1)}, bf16[512,512]{1,0:T(8,128)(2,1)}, u32[]{:S(2)}, u32[]{:S(2)}) collective-permute-start(bf16[512,512]{1,0:T(8,128)(2,1)} %bitcast.11), channel_id=1, source_target_pairs={{0,4},{1,5},{2,6},{3,7},{4,0},{5,1},{6,2},{7,3},{8,12},{9,13},{10,... | collective-permute-start | bytes 1572872 | tf_op jit(solution)/shard_map/ppermute | solution.py:247
  71.9 23.6 %collective-permute-start.4 = (bf16[512,512]{1,0:T(8,128)(2,1)}, bf16[512,512]{1,0:T(8,128)(2,1)}, u32[]{:S(2)}, u32[]{:S(2)}) collective-permute-start(bf16[512,512]{1,0:T(8,128)(2,1)} %bitcast.11), channel_id=1, source_target_pairs={{0,16},{1,17},{2,18},{3,19},{4,20},{5,21},{6,22},{7,23},{8,24},{9,... | collective-permute-start | bytes 1572872 | tf_op jit(solution)/shard_map/ppermute | solution.py:247
  73.4 23.8 %collective-permute-start.5 = (bf16[512,512]{1,0:T(8,128)(2,1)}, bf16[512,512]{1,0:T(8,128)(2,1)S(1)}, u32[]{:S(2)}, u32[]{:S(2)}) collective-permute-start(bf16[512,512]{1,0:T(8,128)(2,1)} %collective-permute-done), channel_id=1, source_target_pairs={{0,16},{1,17},{2,18},{3,19},{4,20},{5,21},{6,22},{7,23},{8,24},{9,... | collective-permute-start | bytes 1572872 | tf_op jit(solution)/shard_map/ppermute | solution.py:247
  111.6 32.5 %all-to-all-start.2 = ((bf16[8,192,688]{2,1,0:T(8,128)(2,1)}), bf16[8,192,688]{2,1,0:T(8,128)(2,1)S(1)}, u32[]{:S(2)}, u32[]{:S(2)}) async-start(bf16[8,192,688]{2,1,0:T(8,128)(2,1)} %shard_map.240), calls=%async_computation.2 | async-start | bytes 4718592 | tf_op jit(solution)/shard_map/all_to_all | solution.py:267
  115.3 48.9 %collective-permute-start.6 = (bf16[2,4,2,64,512]{4,3,2,1,0:T(8,128)(2,1)}, bf16[2,4,2,64,512]{4,3,2,1,0:T(8,128)(2,1)}, u32[]{:S(2)}, u32[]{:S(2)}) collective-permute-start(bf16[2,4,2,64,512]{4,3,2,1,0:T(8,128)(2,1)} %bitcast.74), channel_id=1, source_target_pairs={{0,4},{1,5},{2,6},{3,7},{8,12},{9,13},{10,14},{11,15},{16,20},{17,... | collective-permute-start | bytes 3145736 | tf_op jit(solution)/shard_map/ppermute | solution.py:250
  118.9 28.0 %collective-permute-start.7 = (bf16[512,512]{1,0:T(8,128)(2,1)}, bf16[512,512]{1,0:T(8,128)(2,1)}, u32[]{:S(2)}, u32[]{:S(2)}) collective-permute-start(bf16[512,512]{1,0:T(8,128)(2,1)} %collective-permute-done.3), channel_id=1, source_target_pairs={{0,16},{1,17},{2,18},{3,19},{4,20},{5,21},{6,22},{7,23},{8,24},{9,... | collective-permute-start | bytes 1572872 | tf_op jit(solution)/shard_map/ppermute | solution.py:247
  145.4 29.9 %collective-permute-start.8 = (bf16[688,512]{1,0:T(8,128)(2,1)}, bf16[688,512]{1,0:T(8,128)(2,1)S(1)}, u32[]{:S(2)}, u32[]{:S(2)}) collective-permute-start(bf16[688,512]{1,0:T(8,128)(2,1)} %get-tuple-element.80), channel_id=1, source_target_pairs={{0,16},{1,17},{2,18},{3,19},{4,20},{5,21},{6,22},{7,23},{8,24},{9,... | collective-permute-start | bytes 2113544 | tf_op jit(solution)/shard_map/ppermute | solution.py:247
  177.5 40.6 %collective-permute-start.10 = (bf16[688,512]{1,0:T(8,128)(2,1)}, bf16[688,512]{1,0:T(8,128)(2,1)}, u32[]{:S(2)}, u32[]{:S(2)}) collective-permute-start(bf16[688,512]{1,0:T(8,128)(2,1)} %get-tuple-element.80), channel_id=1, source_target_pairs={{0,4},{1,5},{2,6},{3,7},{4,0},{5,1},{6,2},{7,3},{8,12},{9,13},{10,... | collective-permute-start | bytes 2113544 | tf_op jit(solution)/shard_map/ppermute | solution.py:247
  218.1 44.8 %all-to-all-start.3 = ((bf16[4,128,2048]{2,1,0:T(8,128)(2,1)}), bf16[4,128,2048]{2,1,0:T(8,128)(2,1)}, u32[]{:S(2)}, u32[]{:S(2)}) async-start(bf16[4,128,2048]{2,1,0:T(8,128)(2,1)} %bitcast.107), calls=%async_computation.3 | async-start | bytes 4194304 | tf_op jit(solution)/shard_map/all_to_all | solution.py:297
  222.6 97.5 %all-gather.10.cloned.1.call-start = ((), (), s32[]{:S(2)}) async-start(), calls=%async_computation.11 | async-start | bytes 4718592 | tf_op jit(solution)/shard_map/all_gather | solution.py:279
  222.6 17.9 %collective-permute-start.12 = (bf16[688,512]{1,0:T(8,128)(2,1)}, bf16[688,512]{1,0:T(8,128)(2,1)}, u32[]{:S(2)}, u32[]{:S(2)}) collective-permute-start(bf16[688,512]{1,0:T(8,128)(2,1)} %copy-done.6), channel_id=1, source_target_pairs={{0,16},{1,17},{2,18},{3,19},{4,20},{5,21},{6,22},{7,23},{8,24},{9,... | collective-permute-start | bytes 2113544 | tf_op jit(solution)/shard_map/ppermute | solution.py:247
  224.1 36.6 %collective-permute-start.11 = (bf16[688,512]{1,0:T(8,128)(2,1)}, bf16[688,512]{1,0:T(8,128)(2,1)}, u32[]{:S(2)}, u32[]{:S(2)}) collective-permute-start(bf16[688,512]{1,0:T(8,128)(2,1)} %copy-done.6), channel_id=1, source_target_pairs={{0,4},{1,5},{2,6},{3,7},{4,0},{5,1},{6,2},{7,3},{8,12},{9,13},{10,... | collective-permute-start | bytes 2113544 | tf_op jit(solution)/shard_map/ppermute | solution.py:247
  267.2 74.0 %all-gather.12.cloned.1.call-start = ((), (), s32[]{:S(2)}) async-start(), calls=%async_computation.12 | async-start | bytes 4718592 | tf_op jit(solution)/shard_map/all_gather | solution.py:279
  269.9 50.2 %collective-permute-start.14 = (bf16[688,512]{1,0:T(8,128)(2,1)}, bf16[688,512]{1,0:T(8,128)(2,1)}, u32[]{:S(2)}, u32[]{:S(2)}) collective-permute-start(bf16[688,512]{1,0:T(8,128)(2,1)} %copy-done.4), channel_id=1, source_target_pairs={{0,16},{1,17},{2,18},{3,19},{4,20},{5,21},{6,22},{7,23},{8,24},{9,... | collective-permute-start | bytes 2113544 | tf_op jit(solution)/shard_map/ppermute | solution.py:247
  273.5 30.5 %collective-permute-start.15 = (bf16[688,512]{1,0:T(8,128)(2,1)}, bf16[688,512]{1,0:T(8,128)(2,1)S(1)}, u32[]{:S(2)}, u32[]{:S(2)}) collective-permute-start(bf16[688,512]{1,0:T(8,128)(2,1)} %collective-permute-done.10), channel_id=1, source_target_pairs={{0,16},{1,17},{2,18},{3,19},{4,20},{5,21},{6,22},{7,23},{8,24},{9,... | collective-permute-start | bytes 2113544 | tf_op jit(solution)/shard_map/ppermute | solution.py:247
  275.3 31.7 %collective-permute-start.13 = (bf16[688,512]{1,0:T(8,128)(2,1)S(1)}, bf16[688,512]{1,0:T(8,128)(2,1)}, u32[]{:S(2)}, u32[]{:S(2)}) collective-permute-start(bf16[688,512]{1,0:T(8,128)(2,1)S(1)} %copy-done.5), channel_id=1, source_target_pairs={{0,4},{1,5},{2,6},{3,7},{4,0},{5,1},{6,2},{7,3},{8,12},{9,13},{10,... | collective-permute-start | bytes 2113544 | tf_op jit(solution)/shard_map/ppermute | solution.py:247
  276.6 42.5 %collective-permute-start.16 = (bf16[688,512]{1,0:T(8,128)(2,1)}, bf16[688,512]{1,0:T(8,128)(2,1)S(1)}, u32[]{:S(2)}, u32[]{:S(2)}) collective-permute-start(bf16[688,512]{1,0:T(8,128)(2,1)} %collective-permute-done.11), channel_id=1, source_target_pairs={{0,16},{1,17},{2,18},{3,19},{4,20},{5,21},{6,22},{7,23},{8,24},{9,... | collective-permute-start | bytes 2113544 | tf_op jit(solution)/shard_map/ppermute | solution.py:247
  307.1 31.8 %collective-permute-start.17 = (bf16[688,512]{1,0:T(8,128)(2,1)}, bf16[688,512]{1,0:T(8,128)(2,1)}, u32[]{:S(2)}, u32[]{:S(2)}) collective-permute-start(bf16[688,512]{1,0:T(8,128)(2,1)} %collective-permute-done.13), channel_id=1, source_target_pairs={{0,16},{1,17},{2,18},{3,19},{4,20},{5,21},{6,22},{7,23},{8,24},{9,... | collective-permute-start | bytes 2113544 | tf_op jit(solution)/shard_map/ppermute | solution.py:247
  369.4 30.6 %all-to-all-start.4 = ((bf16[4,128,2048]{2,1,0:T(8,128)(2,1)}), bf16[4,128,2048]{2,1,0:T(8,128)(2,1)}, u32[]{:S(2)}, u32[]{:S(2)}) async-start(bf16[4,128,2048]{2,1,0:T(8,128)(2,1)} %bitcast.103), calls=%async_computation.4 | async-start | bytes 4194304 | tf_op jit(solution)/shard_map/all_to_all | solution.py:297
  373.9 82.2 %all-gather.14.cloned.1.call-start = ((), (), s32[]{:S(2)}) async-start(), calls=%async_computation.13 | async-start | bytes 4718592 | tf_op jit(solution)/shard_map/all_gather | solution.py:279
  373.9 33.4 %collective-permute-start.19 = (bf16[688,1024]{1,0:T(8,128)(2,1)}, bf16[688,1024]{1,0:T(8,128)(2,1)}, u32[]{:S(2)}, u32[]{:S(2)}) collective-permute-start(bf16[688,1024]{1,0:T(8,128)(2,1)} %fusion.26), channel_id=1, source_target_pairs={{0,16},{1,17},{2,18},{3,19},{4,20},{5,21},{6,22},{7,23},{8,24},{9,... | collective-permute-start | bytes 4227080 | tf_op jit(solution)/shard_map/ppermute | solution.py:247
  407.4 32.5 %collective-permute-start.20 = (bf16[688,1024]{1,0:T(8,128)(2,1)}, bf16[688,1024]{1,0:T(8,128)(2,1)S(1)}, u32[]{:S(2)}, u32[]{:S(2)}) collective-permute-start(bf16[688,1024]{1,0:T(8,128)(2,1)} %fusion.29), channel_id=1, source_target_pairs={{0,16},{1,17},{2,18},{3,19},{4,20},{5,21},{6,22},{7,23},{8,24},{9,... | collective-permute-start | bytes 4227080 | tf_op jit(solution)/shard_map/ppermute | solution.py:247
  444.6 116.6 %collective-permute-start.24 = (bf16[688,1024]{1,0:T(8,128)(2,1)}, bf16[688,1024]{1,0:T(8,128)(2,1)}, u32[]{:S(2)}, u32[]{:S(2)}) collective-permute-start(bf16[688,1024]{1,0:T(8,128)(2,1)} %add_convert_fusion.7.kept_ref), channel_id=1, source_target_pairs={{4,0},{5,1},{6,2},{7,3},{8,12},{9,13},{10,14},{11,15},{20,16},{21,... | collective-permute-start | bytes 4227080 | tf_op jit(solution)/shard_map/ppermute | solution.py:250
  450.5 95.2 %collective-permute-start.22 = (bf16[688,1024]{1,0:T(8,128)(2,1)}, bf16[688,1024]{1,0:T(8,128)(2,1)}, u32[]{:S(2)}, u32[]{:S(2)}) collective-permute-start(bf16[688,1024]{1,0:T(8,128)(2,1)} %add_convert_fusion.8.kept_ref), channel_id=1, source_target_pairs={{4,0},{5,1},{6,2},{7,3},{8,12},{9,13},{10,14},{11,15},{20,16},{21,... | collective-permute-start | bytes 4227080 | tf_op jit(solution)/shard_map/ppermute | solution.py:250
  454.5 96.1 %collective-permute-start.26 = (bf16[688,1024]{1,0:T(8,128)(2,1)}, bf16[688,1024]{1,0:T(8,128)(2,1)}, u32[]{:S(2)}, u32[]{:S(2)}) collective-permute-start(bf16[688,1024]{1,0:T(8,128)(2,1)} %fusion.32), channel_id=1, source_target_pairs={{0,16},{1,17},{2,18},{3,19},{4,20},{5,21},{6,22},{7,23},{8,24},{9,... | collective-permute-start | bytes 4227080 | tf_op jit(solution)/shard_map/ppermute | solution.py:247
  469.6 91.6 %collective-permute-start.21 = (bf16[2,4,2,64,512]{4,3,2,1,0:T(8,128)(2,1)}, bf16[2,4,2,64,512]{4,3,2,1,0:T(8,128)(2,1)}, u32[]{:S(2)}, u32[]{:S(2)}) collective-permute-start(bf16[2,4,2,64,512]{4,3,2,1,0:T(8,128)(2,1)} %get-tuple-element.100), channel_id=1, source_target_pairs={{4,0},{5,1},{6,2},{7,3},{12,8},{13,9},{14,10},{15,11},{20,16},{21,... | collective-permute-start | bytes 3145736 | tf_op jit(solution)/shard_map/ppermute | solution.py:250
  473.1 90.5 %collective-permute-start.32 = (bf16[512,2048]{1,0:T(8,128)(2,1)}, bf16[512,2048]{1,0:T(8,128)(2,1)}, u32[]{:S(2)}, u32[]{:S(2)}) collective-permute-start(bf16[512,2048]{1,0:T(8,128)(2,1)} %convolution_convert_fusion), channel_id=1, source_target_pairs={{0,8},{1,9},{2,10},{3,11},{4,12},{5,13},{6,14},{7,15},{8,0},{9,1},... | collective-permute-start | bytes 6291464 | tf_op jit(solution)/shard_map/ppermute | solution.py:247
  545.7 15.5 %collective-permute-start.25 = (bf16[1024,512]{1,0:T(8,128)(2,1)S(1)}, bf16[1024,512]{1,0:T(8,128)(2,1)}, u32[]{:S(2)}, u32[]{:S(2)}) collective-permute-start(bf16[1024,512]{1,0:T(8,128)(2,1)S(1)} %pad_maximum_fusion.3), channel_id=1, source_target_pairs={{0,16},{1,17},{2,18},{3,19},{4,20},{5,21},{6,22},{7,23},{8,24},{9,... | collective-permute-start | bytes 3145736 | tf_op jit(solution)/shard_map/ppermute | solution.py:247
  567.3 48.6 %all-to-all-start.5 = ((bf16[4,128,2048]{2,1,0:T(8,128)(2,1)}), bf16[4,128,2048]{2,1,0:T(8,128)(2,1)}, u32[]{:S(2)}, u32[]{:S(2)}) async-start(bf16[4,128,2048]{2,1,0:T(8,128)(2,1)} %bitcast.106), calls=%async_computation.5 | async-start | bytes 4194304 | tf_op jit(solution)/shard_map/all_to_all | solution.py:297
  578.1 36.6 %collective-permute-start.29 = (bf16[688,1024]{1,0:T(8,128)(2,1)S(1)}, bf16[688,1024]{1,0:T(8,128)(2,1)S(1)}, u32[]{:S(2)}, u32[]{:S(2)}) collective-permute-start(bf16[688,1024]{1,0:T(8,128)(2,1)S(1)} %copy-done.28), channel_id=1, source_target_pairs={{4,0},{5,1},{6,2},{7,3},{8,12},{9,13},{10,14},{11,15},{20,16},{21,... | collective-permute-start | bytes 4227080 | tf_op jit(solution)/shard_map/ppermute | solution.py:250
  579.4 26.0 %collective-permute-start.28 = (bf16[1024,512]{1,0:T(8,128)(2,1)S(1)}, bf16[1024,512]{1,0:T(8,128)(2,1)S(1)}, u32[]{:S(2)}, u32[]{:S(2)}) collective-permute-start(bf16[1024,512]{1,0:T(8,128)(2,1)S(1)} %get-tuple-element.142), channel_id=1, source_target_pairs={{0,16},{1,17},{2,18},{3,19},{4,20},{5,21},{6,22},{7,23},{8,24},{9,... | collective-permute-start | bytes 3145736 | tf_op jit(solution)/shard_map/ppermute | solution.py:247
  615.9 29.4 %all-to-all-start.8 = ((bf16[4,128,2048]{2,1,0:T(8,128)(2,1)}), bf16[4,128,2048]{2,1,0:T(8,128)(2,1)}, u32[]{:S(2)}, u32[]{:S(2)}) async-start(bf16[4,128,2048]{2,1,0:T(8,128)(2,1)} %bitcast.105), calls=%async_computation.8 | async-start | bytes 4194304 | tf_op jit(solution)/shard_map/all_to_all | solution.py:297
  623.2 22.1 %collective-permute-start.35 = (bf16[688,512]{1,0:T(8,128)(2,1)}, bf16[688,512]{1,0:T(8,128)(2,1)}, u32[]{:S(2)}, u32[]{:S(2)}) collective-permute-start(bf16[688,512]{1,0:T(8,128)(2,1)} %shard_map.247), channel_id=1, source_target_pairs={{0,8},{1,9},{2,10},{3,11},{12,4},{13,5},{14,6},{15,7},{16,24},{17,... | collective-permute-start | bytes 2113544 | tf_op jit(solution)/shard_map/ppermute | solution.py:250
  637.4 20.3 %collective-permute-start.30 = (bf16[512,2048]{1,0:T(8,128)(2,1)}, bf16[512,2048]{1,0:T(8,128)(2,1)}, u32[]{:S(2)}, u32[]{:S(2)}) collective-permute-start(bf16[512,2048]{1,0:T(8,128)(2,1)} %convolution_convert_fusion.2), channel_id=1, source_target_pairs={{0,8},{1,9},{2,10},{3,11},{4,12},{5,13},{6,14},{7,15},{8,0},{9,1},... | collective-permute-start | bytes 6291464 | tf_op jit(solution)/shard_map/ppermute | solution.py:247
  640.6 55.2 %collective-permute-start.31 = (bf16[1024,512]{1,0:T(8,128)(2,1)}, bf16[1024,512]{1,0:T(8,128)(2,1)}, u32[]{:S(2)}, u32[]{:S(2)}) collective-permute-start(bf16[1024,512]{1,0:T(8,128)(2,1)} %get-tuple-element.127.kept_ref), channel_id=1, source_target_pairs={{4,0},{5,1},{6,2},{7,3},{8,12},{9,13},{10,14},{11,15},{20,16},{21,... | collective-permute-start | bytes 3145736 | tf_op jit(solution)/shard_map/ppermute | solution.py:250
  642.0 64.0 %collective-permute-start.33 = (bf16[1024,512]{1,0:T(8,128)(2,1)}, bf16[1024,512]{1,0:T(8,128)(2,1)}, u32[]{:S(2)}, u32[]{:S(2)}) collective-permute-start(bf16[1024,512]{1,0:T(8,128)(2,1)} %fusion.5.kept_ref), channel_id=1, source_target_pairs={{4,0},{5,1},{6,2},{7,3},{8,12},{9,13},{10,14},{11,15},{20,16},{21,... | collective-permute-start | bytes 3145736 | tf_op jit(solution)/shard_map/ppermute | solution.py:250
  649.0 45.5 %all-to-all-start.6 = ((f32[32,1,192]{2,1,0:T(1,128)}), f32[32,1,192]{2,1,0:T(1,128)S(1)}, u32[]{:S(2)}, u32[]{:S(2)}) async-start(f32[32,1,192]{2,1,0:T(1,128)} %reshape.212), calls=%async_computation.6 | async-start | bytes 65536 | tf_op jit(solution)/shard_map/all_to_all | solution.py:368
  695.8 37.1 %all-to-all-start.7 = ((bf16[4,128,2048]{2,1,0:T(8,128)(2,1)}), bf16[4,128,2048]{2,1,0:T(8,128)(2,1)}, u32[]{:S(2)}, u32[]{:S(2)}) async-start(bf16[4,128,2048]{2,1,0:T(8,128)(2,1)} %bitcast.104), calls=%async_computation.7 | async-start | bytes 4194304 | tf_op jit(solution)/shard_map/all_to_all | solution.py:297
  703.1 15.5 %collective-permute-start.36 = (bf16[688,512]{1,0:T(8,128)(2,1)}, bf16[688,512]{1,0:T(8,128)(2,1)}, u32[]{:S(2)}, u32[]{:S(2)}) collective-permute-start(bf16[688,512]{1,0:T(8,128)(2,1)} %shard_map.249), channel_id=1, source_target_pairs={{0,8},{1,9},{2,10},{3,11},{12,4},{13,5},{14,6},{15,7},{16,24},{17,... | collective-permute-start | bytes 2113544 | tf_op jit(solution)/shard_map/ppermute | solution.py:250
  708.6 13.2 %collective-permute-start.37 = (bf16[512,512]{1,0:T(8,128)(2,1)}, bf16[512,512]{1,0:T(8,128)(2,1)}, u32[]{:S(2)}, u32[]{:S(2)}) collective-permute-start(bf16[512,512]{1,0:T(8,128)(2,1)} %shard_map.253), channel_id=1, source_target_pairs={{0,8},{1,9},{2,10},{3,11},{12,4},{13,5},{14,6},{15,7},{16,24},{17,... | collective-permute-start | bytes 1572872 | tf_op jit(solution)/shard_map/ppermute | solution.py:250
  713.4 11.4 %collective-permute-start.34 = (bf16[512,512]{1,0:T(8,128)(2,1)}, bf16[512,512]{1,0:T(8,128)(2,1)}, u32[]{:S(2)}, u32[]{:S(2)}) collective-permute-start(bf16[512,512]{1,0:T(8,128)(2,1)} %shard_map.246), channel_id=1, source_target_pairs={{0,8},{1,9},{2,10},{3,11},{12,4},{13,5},{14,6},{15,7},{16,24},{17,... | collective-permute-start | bytes 1572872 | tf_op jit(solution)/shard_map/ppermute | solution.py:250
  (75 other events, 733.6 us)
Sparse Core Ops, SparseCore 0:
  24.9 44.0 all-gather.5
  71.2 40.4 all-gather.7
  267.3 43.3 all-gather.9
  312.7 28.4 all-gather.11
  407.5 30.1 all-gather.13

commit v3 on v2

--- a/solution.py
+++ b/solution.py
@@ -253,6 +253,8 @@
 
 
 def after(value, *others):
+    if not others:
+        return value
     return lax.optimization_barrier((value, others))[0]
 
 
@@ -456,12 +458,12 @@
     cache_far = at.swap(cache_near, at.far_bit)
     cache_far_half = at.swap(cache_half, at.far_bit)
     cache_w = jnp.concatenate([cache_near, cache_half, cache_far, cache_far_half], axis=0)
-    memory_all = after(memory_all, cache_half, cache_far, query_near, info)
+    memory_all = after(memory_all, cache_half, cache_far, info, )
     query_later = after(query_near, cache_half)
     query_half = at.swap(query_later, at.half_bit)
     query_far = at.swap(query_later, at.far_bit)
     token_all = gather(at, after(token_in, memory_all))
-    memory_all = after(memory_all, query_half, query_far, cache_w)
+    memory_all = after(memory_all, cache_w)
 
     def first_half(i):
         return (i // at.half_bit) % 2 == 0
@@ -484,7 +486,7 @@
     out_w = jnp.concatenate([part[:, own_width:] for part in query_parts], axis=0)
     queries = heads(widen(times(token_all, query_w, bf16)))
     gate_near, up_near, down_near = near_weights(
-        at, [w_gate, w_up, w_down], None, gathered_tokens, cache
+        at, [w_gate, w_up, w_down], None, cache
     )
     (mixed,) = attention_call(
         functools.partial(attend_kernel, scale),
@@ -512,7 +514,7 @@
     down_half = at.swap(after(down_near, up_half), at.half_bit)
     gate_w = whole(gate_near, gate_half, gate_far, at.swap(gate_half, at.far_bit))
     up_w = whole(up_near, up_half, up_far, at.swap(up_half, at.far_bit))
-    ffn_all = after(gather(at, ffn_in), down_half, down_far, gate_w, up_w)
+    ffn_all = after(gather(at, ffn_in), down_half, down_far, up_w)
     final_all = gather(at, after(grad_final.astype(bf16), other_cache))
     gate = times_transposed(ffn_all, gate_w)
     up = times_transposed(ffn_all, after(up_w, gate))
@@ -531,10 +533,10 @@
     up_grad = Gradient(at, [(ffn_all, grad_up_in)], True)
     grad_ffn_in = scatter(
         at,
-        [(after(grad_gate_in, gate_grad.there), gate_w), (grad_up_in, up_w)],
+        [(after(grad_gate_in, gate_grad.there, ), gate_w), (grad_up_in, up_w)],
         times,
         (),
-        (up_grad.there,),
+        (),
     )
     grad_residual = grad_final + norm_back(grad_ffn_in, ffn_normed, ffn_inverse, gain_ffn)
     gain_ffn_term = jnp.sum(grad_ffn_in * ffn_normed, axis=0)
@@ -545,7 +547,7 @@
     gate_grad.across(grad_branch)
     up_grad.across()
     gathered = branch_all
-    branch_all = after(branch_all, gate_grad.kept, up_grad.kept)
+    branch_all = after(branch_all, gate_grad.kept, up_grad.kept, )
     grad_mixed = heads(widen(times(branch_all, out_w, bf16)))
     grad_queries, grad_cache, grad_other_cache = attention_call(
         functools.partial(attend_back_kernel, scale),
@@ -560,13 +562,18 @@
     )
     given_cache = at.send(grad_other_cache, at.half_bit, second_half)
     grad_queries = narrow(grad_queries.reshape(group * count, width))
-    grad_token_in = scatter(at, [(grad_queries, query_w)])
+    output = residual + scatter(at, [(hidden, down_w)], times, (gathered,))
     gate_grad.to_twin()
     (gate_out,) = gate_grad.finish()
     query_grad = Gradient(at, [(token_all, grad_queries), (branch_all, mixed)])
 
     given_cache = after(
-        given_cache, gate_out, up_grad.back, query_grad.given, down_grad.given
+        given_cache,
+        gate_out,
+
+
+        query_grad.given,
+
     )
     up_grad.to_twin()
     grad_cache = (grad_cache + given_cache.astype(f32)).astype(bf16)
@@ -577,19 +584,31 @@
         )
     cache_grad = Gradient(at, [(memory_all, grad_cache)])
     down_grad.across(grad_cache)
-    before = (cache_grad.given, down_grad.back)
     cache_grad.across()
     grad_memory_in = scatter(
         at,
         [(after(grad_cache, cache_grad.there, down_grad.kept), cache_w)],
         times_transposed,
-        before,
-        (up_grad.twins,),
-    )
-    query_grad.across(cache_grad.kept)
+        (cache_grad.given, down_grad.back),
+        (),
+    )
+    query_grad.across(cache_grad.kept, )
     down_grad.to_twin()
     (up_out,) = up_grad.finish()
     cache_grad.to_twin()
+    grad_token_in = scatter(
+        at,
+        [(after(grad_queries, at.kept, cache_grad.kept), query_w)],
+        times_transposed,
+        (cache_grad.back,),
+        (
+            query_grad.back,
+            cache_grad.twins,
+            up_out,
+
+        ),
+    )
+
     cut = model_width // 2
     gain_memory_term = (
         jnp.concatenate(
@@ -603,30 +622,19 @@
     gain_attn_term = jnp.sum(grad_token_in * token_normed, axis=0)
     gain_terms = jnp.stack([gain_attn_term, gain_memory_term, gain_ffn_term])
     gain_grads = reduce_gains(at, gain_terms)
-
-    def left(value):
-        value = value.astype(bf16)
-        (value,) = local_call(
-            functools.partial(move_kernel, restored),
-            [sides],
-            [value],
-            [jax.ShapeDtypeStruct(value.shape, value.dtype)],
-        )
-        return value
-
-    output_term = scatter(
-        at,
-        [(after(hidden, at.kept, cache_grad.kept), down_w)],
-        times,
-        (cache_grad.back, gain_grads),
-        (query_grad.back, cache_grad.twins, up_out, down_grad.twins),
-    )
-    grad_tokens = left(
-        grad_residual + norm_back(grad_token_in, token_normed, token_inverse, gain_attn)
-    )
-    grad_memory = left(norm_back(grad_memory_in, memory_normed, memory_inverse, gain_memory))
-    output = left(residual + output_term)
-    leaving = [output, grad_tokens, grad_memory]
+    down_grad.twins = after(down_grad.twins, gain_terms)
+    cache_grad.twins = after(cache_grad.twins, gain_terms)
+    query_grad.back = query_grad.back
+
+    grad_tokens = grad_residual + norm_back(grad_token_in, token_normed, token_inverse, gain_attn)
+    grad_memory = norm_back(grad_memory_in, memory_normed, memory_inverse, gain_memory)
+    leaving = [a.astype(bf16) for a in (output, grad_tokens, grad_memory)]
+    leaving = local_call(
+        functools.partial(move_kernel, restored),
+        [sides],
+        leaving,
+        [jax.ShapeDtypeStruct(a.shape, a.dtype) for a in leaving],
+    )
     query_grad.to_twin()
     (down_out,) = down_grad.finish()
     query_out, out_out = query_grad.finish(own_width)

time: 754 us -> 685 us (0.908)
  waiting for transfers between devices: 383 us -> 322 us
  starting transfers between devices: 108 us -> 95.8 us
  local copies, waits for them, and re-layouts: 34.6 us -> 44.6 us
    all_to_all x1, waiting for transfers between devices: 30.9 us -> 0.01 us  [reduce_gains(): terms = lax.all_to_all(terms, AXES, split_axis=0, concat_axis=0, tiled=True)]
    ppermute x12, waiting for transfers between devices: 93.3 us -> 69.4 us  [send(): lax.ppermute(value, AXES, [(i, i ^ mask) for i in range(self.count) if ch...]
    all_to_all x3, waiting for transfers between devices: 24.5 us -> 6.27 us  [near_weights(): lax.all_to_all(blocks, GROUP, split_axis=0, concat_axis=0, tiled=True)]
    ppermute x26, waiting for transfers between devices: 191 us -> 208 us  [swap(): return lax.ppermute(value, AXES, [(i, i ^ mask) for i in range(self.count)])]
    unnamed x155, local copies, waits for them, and re-layouts: 22.2 us -> 30.9 us
    ppermute x26, starting transfers between devices: 40.8 us -> 32.2 us  [swap(): return lax.ppermute(value, AXES, [(i, i ^ mask) for i in range(self.count)])]
    all_gather x5, waiting for transfers between devices: 20.5 us -> 12.1 us  [gather(): return lax.all_gather(value, GROUP, axis=0, tiled=True)]
  transfers between devices with their start and end apart: 52 -> 52, of which waited for: 24 -> 27; matrix products, arithmetic and copies ran while one was open for 19% -> 21% of each run, Pallas kernels for 7% -> 8%
where the time goes in v3:
time: 685 us; the launch traced here: 675 us
  waiting for transfers between devices  322 us (47%)
  matrix products  110 us (16%)
  starting transfers between devices  95.8 us (14%)
  Pallas kernels  54.1 us (8%)
  local copies, waits for them, and re-layouts  44.6 us (7%)
  other arithmetic  34 us (5%)
  between operations  15.4 us (2%)
    ppermute x26, waiting for transfers between devices, swap(): return lax.ppermute(value, AXES, [(i, i ^ mask) for i in range(self.count)])  208 us
    dot_general x30, matrix products, dot(): lax.dot_general(left, right, (over, ((), ())), preferred_element_type=kind)  110 us
    ppermute x12, waiting for transfers between devices, send(): lax.ppermute(value, AXES, [(i, i ^ mask) for i in range(self.count) if ch...  69.4 us
    ppermute x26, starting transfers between devices, swap(): return lax.ppermute(value, AXES, [(i, i ^ mask) for i in range(self.count)])  32.2 us
    unnamed x155, local copies, waits for them, and re-layouts  30.9 us
    pallas_call x10, Pallas kernels, halves_call(): pl.pallas_call(kernel, grid_spec=pltpu.PrefetchScalarGridSpec(num_scalar_...  29.2 us
    all_to_all x5, waiting for transfers between devices, scatter(): kept = lax.all_to_all(kept, INNER, split_axis=0, concat_axis=0, tiled=True)  26.1 us
    ppermute x12, starting transfers between devices, send(): lax.ppermute(value, AXES, [(i, i ^ mask) for i in range(self.count) if ch...  22.6 us
  transfers between devices with their start and end apart: 52, of which 27 were waited for; matrix products, arithmetic and copies ran while one was open for 21% of the time, Pallas kernels for 8%

profile of v3, /device:TPU:0, one launch (start us, length us, event | category | flops | bytes accessed | tf_op | source)
XLA Modules:
  0.0 675.3 jit_solution(5525873865465973730)
XLA Ops:
  10.1 5.3 all-to-all-start
  18.4 6.3 all-to-all-done
  34.0 19.1 %collective-permute-done = bf16[512,512]{1,0:T(8,128)(2,1)} collective-permute-done((bf16[512,512]{1,0:T(8,128)(2,1)}, bf16[512,512]{1,0:T(8,128)(2,1)}, u32[]{:S(2)}, u32[]{:S(2)}) %collective-permute-start) | collective-permute-done | bytes 524320 | tf_op jit(solution)/shard_map/ppermute | solution.py:247
  53.1 11.2 %all-gather.6.cloned.1.call-done = bf16[1024,2048]{1,0:T(8,128)(2,1)} async-done(((bf16[128,2048]{1,0:T(8,128)(2,1)}), bf16[1024,2048]{1,0:T(8,128)(2,1)}) %all-gather.6.cloned.1.call-update) | async-done | bytes 4194320 | tf_op jit(solution)/shard_map/all_gather | solution.py:281
  67.6 4.2 all-to-all-start.1
  73.8 4.9 collective-permute-done.3
  78.8 5.9 fusion.102
  84.7 3.7 all-to-all-start.2
  91.8 3.9 collective-permute-start.4
  95.7 36.3 %collective-permute-done.5 = bf16[512,512]{1,0:T(8,128)(2,1)} collective-permute-done((bf16[512,512]{1,0:T(8,128)(2,1)}, bf16[512,512]{1,0:T(8,128)(2,1)}, u32[]{:S(2)}, u32[]{:S(2)}) %collective-permute-start.5) | collective-permute-done | bytes 524320 | tf_op jit(solution)/shard_map/ppermute | solution.py:247
  142.7 4.4 collective-permute-done.7
  148.9 5.5 collective-permute-done.4.okv_ref
  154.4 3.7 fusion.101
  158.2 7.4 %shard_map.242 = bf16[2,4,2,64,256]{4,3,2,1,0:T(8,128)(2,1)S(1)} custom-call(bf16[2,4,2,64,256]{4,3,2,1,0:T(8,128)(2,1)S(1)} %bitcast.79, bf16[2,4,2,64,512]{4,3,2,1,0:T(8,128)(2,1)S(1)} %bitcast.77, bf16[2,4,2,64,512]{4,3,2,1,0:T(8,128)(2,1)} %collective-permute-done.4.okv_ref, s32[2,2,256,2]{3,2,1,0:T(8,128)S(1)} %copy-done, ...), custom_call_target="tpu_custom_call" | custom-call | flops 1 | bytes 1 | tf_op jit(solution)/shard_map/pallas_call | solution.py:114
  167.8 6.9 %collective-permute-start.10 = (bf16[688,512]{1,0:T(8,128)(2,1)}, bf16[688,512]{1,0:T(8,128)(2,1)}, u32[]{:S(2)}, u32[]{:S(2)}) collective-permute-start(bf16[688,512]{1,0:T(8,128)(2,1)} %get-tuple-element.84), channel_id=1, source_target_pairs={{0,4},{1,5},{2,6},{3,7},{4,0},{5,1},{6,2},{7,3},{8,12},{9,13},{10,... | collective-permute-start | bytes 2113544 | tf_op jit(solution)/shard_map/ppermute | solution.py:247
  174.7 4.0 add_convert_fusion.5
  178.7 27.9 %collective-permute-done.10 = bf16[688,512]{1,0:T(8,128)(2,1)} collective-permute-done((bf16[688,512]{1,0:T(8,128)(2,1)}, bf16[688,512]{1,0:T(8,128)(2,1)}, u32[]{:S(2)}, u32[]{:S(2)}) %collective-permute-start.10) | collective-permute-done | bytes 704544 | tf_op jit(solution)/shard_map/ppermute | solution.py:247
  206.6 4.4 all-to-all-start.3
  213.3 15.8 %collective-permute-done.12 = bf16[688,512]{1,0:T(8,128)(2,1)} collective-permute-done((bf16[688,512]{1,0:T(8,128)(2,1)}, bf16[688,512]{1,0:T(8,128)(2,1)}, u32[]{:S(2)}, u32[]{:S(2)}) %collective-permute-start.12) | collective-permute-done | bytes 704544 | tf_op jit(solution)/shard_map/ppermute | solution.py:247
  229.1 20.2 %collective-permute-done.11 = bf16[688,512]{1,0:T(8,128)(2,1)} collective-permute-done((bf16[688,512]{1,0:T(8,128)(2,1)}, bf16[688,512]{1,0:T(8,128)(2,1)}, u32[]{:S(2)}, u32[]{:S(2)}) %collective-permute-start.11) | collective-permute-done | bytes 704544 | tf_op jit(solution)/shard_map/ppermute | solution.py:247
  274.0 18.6 %collective-permute-done.16 = bf16[688,512]{1,0:T(8,128)(2,1)S(1)} collective-permute-done((bf16[688,512]{1,0:T(8,128)(2,1)}, bf16[688,512]{1,0:T(8,128)(2,1)S(1)}, u32[]{:S(2)}, u32[]{:S(2)}) %collective-permute-start.16) | collective-permute-done | bytes 704544 | tf_op jit(solution)/shard_map/ppermute | solution.py:247
  296.4 11.2 %collective-permute-done.15 = bf16[688,512]{1,0:T(8,128)(2,1)S(1)} collective-permute-done((bf16[688,512]{1,0:T(8,128)(2,1)}, bf16[688,512]{1,0:T(8,128)(2,1)S(1)}, u32[]{:S(2)}, u32[]{:S(2)}) %collective-permute-start.15) | collective-permute-done | bytes 704544 | tf_op jit(solution)/shard_map/ppermute | solution.py:247
  308.6 8.4 %fusion.109 = f32[1024,688]{0,1:T(8,128)} fusion(bf16[1024,2048]{1,0:T(8,128)(2,1)} %all-gather.10.cloned.1.call-done, bf16[688,2048]{1,0:T(8,128)(2,1)} %copy-done.34), kind=kOutput, calls=%fused_computation.176 | convolution fusion | flops 2885681152 | bytes 9830400 | tf_op jit(solution)/shard_map/dot_general | solution.py:22
  316.9 6.6 fusion.110
  330.7 9.8 %multiply_convert_fusion.1 = (bf16[1024,688]{0,1:T(8,128)(2,1)S(1)}, bf16[1024,688]{0,1:T(8,128)(2,1)S(1)}, bf16[1024,688]{0,1:T(8,128)(2,1)}) fusion(f32[1024,688]{0,1:T(8,128)} %fusion.109, f32[1024,688]{0,1:T(8,128)} %fusion.110, bf16[1024,2048]{1,0:T(8,128)(2,1)} %all-gather.12.cloned.1.call-done, bf16[688,2048]{1,0:T(8,128)(2,1)} %constant_dynamic-update-slice_fusion.8), kind=kOutput, calls=%fused_computation.19 | convolution fusion | flops 2896248832 | bytes 16875520 | tf_op jit(solution)/shard_map/dot_general | solution.py:22
  340.5 4.7 fusion.74
  352.7 3.7 fusion.77
  358.9 4.4 all-to-all-start.4
  365.1 23.9 %all-to-all-done.4 = bf16[4,128,2048]{2,1,0:T(8,128)(2,1)} async-done(((bf16[4,128,2048]{2,1,0:T(8,128)(2,1)}), bf16[4,128,2048]{2,1,0:T(8,128)(2,1)}, u32[]{:S(2)}, u32[]{:S(2)}) %all-to-all-start.4) | async-done | bytes 2097184 | tf_op jit(solution)/shard_map/all_to_all | solution.py:299
  393.1 3.9 collective-permute-done.20
  397.0 3.8 fusion.29
  402.4 4.1 add_convert_fusion.8.kept_ref
  406.5 5.2 convolution_convert_fusion.3
  416.7 18.1 %collective-permute-done.21 = bf16[688,1024]{1,0:T(8,128)(2,1)S(1)} collective-permute-done((bf16[688,1024]{1,0:T(8,128)(2,1)S(1)}, bf16[688,1024]{1,0:T(8,128)(2,1)S(1)}, u32[]{:S(2)}, u32[]{:S(2)}) %collective-permute-start.21) | collective-permute-done | bytes 1409056 | tf_op jit(solution)/shard_map/ppermute | solution.py:247
  437.6 3.8 fusion.100
  441.3 9.8 %shard_map.243 = (bf16[2,4,2,64,256]{4,3,2,1,0:T(8,128)(2,1)S(1)}, f32[2,4,2,64,512]{4,3,2,1,0:T(8,128)}, bf16[2,4,2,64,512]{4,3,2,1,0:T(8,128)(2,1)}) custom-call(bf16[2,4,2,64,256]{4,3,2,1,0:T(8,128)(2,1)S(1)} %bitcast.80, bf16[2,4,2,64,512]{4,3,2,1,0:T(8,128)(2,1)S(1)} %bitcast.78, bf16[2,4,2,64,512]{4,3,2,1,0:T(8,128)(2,1)} %collective-permute-done.4.okv_ref, ...), custom_call_target="tpu_custom_call" | custom-call | flops 1 | bytes 1 | tf_op jit(solution)/shard_map/pallas_call | solution.py:114
  465.0 4.7 add_convert_fusion.6.kept_ref
  469.8 5.6 add_convert_fusion.2
  479.5 3.8 all-to-all-start.5
  483.3 16.4 %collective-permute-done.22 = bf16[2,4,2,64,512]{4,3,2,1,0:T(8,128)(2,1)} collective-permute-done((bf16[2,4,2,64,512]{4,3,2,1,0:T(8,128)(2,1)}, bf16[2,4,2,64,512]{4,3,2,1,0:T(8,128)(2,1)}, u32[]{:S(2)}, u32[]{:S(2)}) %collective-permute-start.22) | collective-permute-done | bytes 1048608 | tf_op jit(solution)/shard_map/ppermute | solution.py:250
  512.4 4.0 add_convert_fusion.1
  516.4 18.9 %collective-permute-done.28 = bf16[1024,512]{1,0:T(8,128)(2,1)S(1)} collective-permute-done((bf16[1024,512]{1,0:T(8,128)(2,1)S(1)}, bf16[1024,512]{1,0:T(8,128)(2,1)S(1)}, u32[]{:S(2)}, u32[]{:S(2)}) %collective-permute-start.28) | collective-permute-done | bytes 1048608 | tf_op jit(solution)/shard_map/ppermute | solution.py:247
  535.3 5.2 collective-permute-done.29.given_ref
  543.0 4.4 all-to-all-start.7
  547.5 4.1 multiply_reduce_fusion.1
  558.6 37.9 %collective-permute-done.31.given_ref = bf16[1024,512]{1,0:T(8,128)(2,1)S(1)} collective-permute-done((bf16[1024,512]{1,0:T(8,128)(2,1)S(1)}, bf16[1024,512]{1,0:T(8,128)(2,1)S(1)}, u32[]{:S(2)}, u32[]{:S(2)}) %collective-permute-start.31) | collective-permute-done | bytes 1048608 | tf_op jit(solution)/shard_map/ppermute | solution.py:250
  597.6 4.6 all-to-all-start.6
  650.9 5.5 all-to-all-start.8
  (331 shorter events, 204.0 us)
Async XLA Ops:
  10.1 14.5 %all-to-all-start = ((bf16[8,64,512]{2,1,0:T(8,128)(2,1)}), bf16[8,64,512]{2,1,0:T(8,128)(2,1)S(1)}, u32[]{:S(2)}, u32[]{:S(2)}) async-start(bf16[8,64,512]{2,1,0:T(8,128)(2,1)} %shard_map.238), calls=%async_computation | async-start | bytes 1048576 | tf_op jit(solution)/shard_map/all_to_all | solution.py:269
  15.4 48.9 %all-gather.6.cloned.1.call-start = ((), (), s32[]{:S(2)}) async-start(), calls=%async_computation.9 | async-start | bytes 4718592 | tf_op jit(solution)/shard_map/all_gather | solution.py:281
  24.7 129.8 %all-gather.8.cloned.1.call-start = ((), (), s32[]{:S(2)}) async-start(), calls=%async_computation.10 | async-start | bytes 4718592 | tf_op jit(solution)/shard_map/all_gather | solution.py:281
  24.9 5.6 collective-permute-start.2
  26.4 26.6 %collective-permute-start = (bf16[512,512]{1,0:T(8,128)(2,1)}, bf16[512,512]{1,0:T(8,128)(2,1)}, u32[]{:S(2)}, u32[]{:S(2)}) collective-permute-start(bf16[512,512]{1,0:T(8,128)(2,1)} %bitcast.117), channel_id=1, source_target_pairs={{0,4},{1,5},{2,6},{3,7},{4,0},{5,1},{6,2},{7,3},{8,12},{9,13},{10,... | collective-permute-start | bytes 1572872 | tf_op jit(solution)/shard_map/ppermute | solution.py:247
  29.0 24.0 %collective-permute-start.1 = (bf16[512,512]{1,0:T(8,128)(2,1)}, bf16[512,512]{1,0:T(8,128)(2,1)}, u32[]{:S(2)}, u32[]{:S(2)}) collective-permute-start(bf16[512,512]{1,0:T(8,128)(2,1)} %bitcast.118), channel_id=1, source_target_pairs={{0,16},{1,17},{2,18},{3,19},{4,20},{5,21},{6,22},{7,23},{8,24},{9,... | collective-permute-start | bytes 1572872 | tf_op jit(solution)/shard_map/ppermute | solution.py:247
  64.3 14.5 %collective-permute-start.3 = (bf16[512,512]{1,0:T(8,128)(2,1)}, bf16[512,512]{1,0:T(8,128)(2,1)}, u32[]{:S(2)}, u32[]{:S(2)}) collective-permute-start(bf16[512,512]{1,0:T(8,128)(2,1)} %collective-permute-done), channel_id=1, source_target_pairs={{0,16},{1,17},{2,18},{3,19},{4,20},{5,21},{6,22},{7,23},{8,24},{9,... | collective-permute-start | bytes 1572872 | tf_op jit(solution)/shard_map/ppermute | solution.py:247
  67.6 17.1 %all-to-all-start.1 = ((bf16[8,64,512]{2,1,0:T(8,128)(2,1)}), bf16[8,64,512]{2,1,0:T(8,128)(2,1)}, u32[]{:S(2)}, u32[]{:S(2)}) async-start(bf16[8,64,512]{2,1,0:T(8,128)(2,1)} %shard_map.239), calls=%async_computation.1 | async-start | bytes 1048576 | tf_op jit(solution)/shard_map/all_to_all | solution.py:269
  84.7 53.5 %all-to-all-start.2 = ((bf16[8,192,688]{2,1,0:T(8,128)(2,1)}), bf16[8,192,688]{2,1,0:T(8,128)(2,1)S(1)}, u32[]{:S(2)}, u32[]{:S(2)}) async-start(bf16[8,192,688]{2,1,0:T(8,128)(2,1)} %shard_map.240), calls=%async_computation.2 | async-start | bytes 4718592 | tf_op jit(solution)/shard_map/all_to_all | solution.py:269
  88.3 43.7 %collective-permute-start.5 = (bf16[512,512]{1,0:T(8,128)(2,1)}, bf16[512,512]{1,0:T(8,128)(2,1)}, u32[]{:S(2)}, u32[]{:S(2)}) collective-permute-start(bf16[512,512]{1,0:T(8,128)(2,1)} %bitcast.15), channel_id=1, source_target_pairs={{0,4},{1,5},{2,6},{3,7},{4,0},{5,1},{6,2},{7,3},{8,12},{9,13},{10,... | collective-permute-start | bytes 1572872 | tf_op jit(solution)/shard_map/ppermute | solution.py:247
  90.2 46.1 %collective-permute-start.6 = (bf16[512,512]{1,0:T(8,128)(2,1)}, bf16[512,512]{1,0:T(8,128)(2,1)}, u32[]{:S(2)}, u32[]{:S(2)}) collective-permute-start(bf16[512,512]{1,0:T(8,128)(2,1)} %bitcast.15), channel_id=1, source_target_pairs={{0,16},{1,17},{2,18},{3,19},{4,20},{5,21},{6,22},{7,23},{8,24},{9,... | collective-permute-start | bytes 1572872 | tf_op jit(solution)/shard_map/ppermute | solution.py:247
  91.8 62.6 %collective-permute-start.4 = (bf16[2,4,2,64,512]{4,3,2,1,0:T(8,128)(2,1)}, bf16[2,4,2,64,512]{4,3,2,1,0:T(8,128)(2,1)}, u32[]{:S(2)}, u32[]{:S(2)}) collective-permute-start(bf16[2,4,2,64,512]{4,3,2,1,0:T(8,128)(2,1)} %bitcast.76), channel_id=1, source_target_pairs={{0,4},{1,5},{2,6},{3,7},{8,12},{9,13},{10,14},{11,15},{16,20},{17,... | collective-permute-start | bytes 3145736 | tf_op jit(solution)/shard_map/ppermute | solution.py:250
  132.0 15.1 %collective-permute-start.7 = (bf16[512,512]{1,0:T(8,128)(2,1)}, bf16[512,512]{1,0:T(8,128)(2,1)}, u32[]{:S(2)}, u32[]{:S(2)}) collective-permute-start(bf16[512,512]{1,0:T(8,128)(2,1)} %collective-permute-done.5), channel_id=1, source_target_pairs={{0,16},{1,17},{2,18},{3,19},{4,20},{5,21},{6,22},{7,23},{8,24},{9,... | collective-permute-start | bytes 1572872 | tf_op jit(solution)/shard_map/ppermute | solution.py:247
  141.2 24.4 %collective-permute-start.8 = (bf16[688,512]{1,0:T(8,128)(2,1)}, bf16[688,512]{1,0:T(8,128)(2,1)}, u32[]{:S(2)}, u32[]{:S(2)}) collective-permute-start(bf16[688,512]{1,0:T(8,128)(2,1)} %get-tuple-element.84), channel_id=1, source_target_pairs={{0,16},{1,17},{2,18},{3,19},{4,20},{5,21},{6,22},{7,23},{8,24},{9,... | collective-permute-start | bytes 2113544 | tf_op jit(solution)/shard_map/ppermute | solution.py:247
  167.8 6.9 %collective-permute-start.9 = (bf16[512,2048]{1,0:T(8,128)(2,1)}, bf16[512,2048]{1,0:T(8,128)(2,1)}, u32[]{:S(2)}, u32[]{:S(2)}) collective-permute-start(bf16[512,2048]{1,0:T(8,128)(2,1)} %convolution_convert_fusion.1), channel_id=1, source_target_pairs={{0,8},{1,9},{2,10},{3,11},{4,12},{5,13},{6,14},{7,15},{8,0},{9,1},... | collective-permute-start | bytes 6291464 | tf_op jit(solution)/shard_map/ppermute | solution.py:247
  167.8 38.7 %collective-permute-start.10 = (bf16[688,512]{1,0:T(8,128)(2,1)}, bf16[688,512]{1,0:T(8,128)(2,1)}, u32[]{:S(2)}, u32[]{:S(2)}) collective-permute-start(bf16[688,512]{1,0:T(8,128)(2,1)} %get-tuple-element.84), channel_id=1, source_target_pairs={{0,4},{1,5},{2,6},{3,7},{4,0},{5,1},{6,2},{7,3},{8,12},{9,13},{10,... | collective-permute-start | bytes 2113544 | tf_op jit(solution)/shard_map/ppermute | solution.py:247
  206.6 44.9 %all-to-all-start.3 = ((bf16[4,128,2048]{2,1,0:T(8,128)(2,1)}), bf16[4,128,2048]{2,1,0:T(8,128)(2,1)}, u32[]{:S(2)}, u32[]{:S(2)}) async-start(bf16[4,128,2048]{2,1,0:T(8,128)(2,1)} %bitcast.109), calls=%async_computation.3 | async-start | bytes 4194304 | tf_op jit(solution)/shard_map/all_to_all | solution.py:299
  211.0 97.5 %all-gather.10.cloned.1.call-start = ((), (), s32[]{:S(2)}) async-start(), calls=%async_computation.11 | async-start | bytes 4718592 | tf_op jit(solution)/shard_map/all_gather | solution.py:281
  211.1 18.0 %collective-permute-start.12 = (bf16[688,512]{1,0:T(8,128)(2,1)}, bf16[688,512]{1,0:T(8,128)(2,1)}, u32[]{:S(2)}, u32[]{:S(2)}) collective-permute-start(bf16[688,512]{1,0:T(8,128)(2,1)} %copy-done.6), channel_id=1, source_target_pairs={{0,16},{1,17},{2,18},{3,19},{4,20},{5,21},{6,22},{7,23},{8,24},{9,... | collective-permute-start | bytes 2113544 | tf_op jit(solution)/shard_map/ppermute | solution.py:247
  211.4 37.8 %collective-permute-start.11 = (bf16[688,512]{1,0:T(8,128)(2,1)}, bf16[688,512]{1,0:T(8,128)(2,1)}, u32[]{:S(2)}, u32[]{:S(2)}) collective-permute-start(bf16[688,512]{1,0:T(8,128)(2,1)} %copy-done.6), channel_id=1, source_target_pairs={{0,4},{1,5},{2,6},{3,7},{4,0},{5,1},{6,2},{7,3},{8,12},{9,13},{10,... | collective-permute-start | bytes 2113544 | tf_op jit(solution)/shard_map/ppermute | solution.py:247
  255.7 74.9 %all-gather.12.cloned.1.call-start = ((), (), s32[]{:S(2)}) async-start(), calls=%async_computation.12 | async-start | bytes 4718592 | tf_op jit(solution)/shard_map/all_gather | solution.py:281
  258.4 50.2 %collective-permute-start.14 = (bf16[688,512]{1,0:T(8,128)(2,1)}, bf16[688,512]{1,0:T(8,128)(2,1)}, u32[]{:S(2)}, u32[]{:S(2)}) collective-permute-start(bf16[688,512]{1,0:T(8,128)(2,1)} %copy-done.4), channel_id=1, source_target_pairs={{0,16},{1,17},{2,18},{3,19},{4,20},{5,21},{6,22},{7,23},{8,24},{9,... | collective-permute-start | bytes 2113544 | tf_op jit(solution)/shard_map/ppermute | solution.py:247
  260.9 31.6 %collective-permute-start.16 = (bf16[688,512]{1,0:T(8,128)(2,1)}, bf16[688,512]{1,0:T(8,128)(2,1)S(1)}, u32[]{:S(2)}, u32[]{:S(2)}) collective-permute-start(bf16[688,512]{1,0:T(8,128)(2,1)} %collective-permute-done.10), channel_id=1, source_target_pairs={{0,16},{1,17},{2,18},{3,19},{4,20},{5,21},{6,22},{7,23},{8,24},{9,... | collective-permute-start | bytes 2113544 | tf_op jit(solution)/shard_map/ppermute | solution.py:247
  264.7 31.0 %collective-permute-start.13 = (bf16[688,512]{1,0:T(8,128)(2,1)S(1)}, bf16[688,512]{1,0:T(8,128)(2,1)}, u32[]{:S(2)}, u32[]{:S(2)}) collective-permute-start(bf16[688,512]{1,0:T(8,128)(2,1)S(1)} %copy-done.5), channel_id=1, source_target_pairs={{0,4},{1,5},{2,6},{3,7},{4,0},{5,1},{6,2},{7,3},{8,12},{9,13},{10,... | collective-permute-start | bytes 2113544 | tf_op jit(solution)/shard_map/ppermute | solution.py:247
  265.9 41.7 %collective-permute-start.15 = (bf16[688,512]{1,0:T(8,128)(2,1)}, bf16[688,512]{1,0:T(8,128)(2,1)S(1)}, u32[]{:S(2)}, u32[]{:S(2)}) collective-permute-start(bf16[688,512]{1,0:T(8,128)(2,1)} %collective-permute-done.11), channel_id=1, source_target_pairs={{0,16},{1,17},{2,18},{3,19},{4,20},{5,21},{6,22},{7,23},{8,24},{9,... | collective-permute-start | bytes 2113544 | tf_op jit(solution)/shard_map/ppermute | solution.py:247
  295.7 32.0 %collective-permute-start.17 = (bf16[688,512]{1,0:T(8,128)(2,1)}, bf16[688,512]{1,0:T(8,128)(2,1)}, u32[]{:S(2)}, u32[]{:S(2)}) collective-permute-start(bf16[688,512]{1,0:T(8,128)(2,1)} %collective-permute-done.13), channel_id=1, source_target_pairs={{0,16},{1,17},{2,18},{3,19},{4,20},{5,21},{6,22},{7,23},{8,24},{9,... | collective-permute-start | bytes 2113544 | tf_op jit(solution)/shard_map/ppermute | solution.py:247
  350.5 5.9 collective-permute-start.18
  358.9 30.1 %all-to-all-start.4 = ((bf16[4,128,2048]{2,1,0:T(8,128)(2,1)}), bf16[4,128,2048]{2,1,0:T(8,128)(2,1)}, u32[]{:S(2)}, u32[]{:S(2)}) async-start(bf16[4,128,2048]{2,1,0:T(8,128)(2,1)} %bitcast.105), calls=%async_computation.4 | async-start | bytes 4194304 | tf_op jit(solution)/shard_map/all_to_all | solution.py:299
  363.4 74.2 %all-gather.14.cloned.1.call-start = ((), (), s32[]{:S(2)}) async-start(), calls=%async_computation.13 | async-start | bytes 4718592 | tf_op jit(solution)/shard_map/all_gather | solution.py:281
  363.6 33.4 %collective-permute-start.20 = (bf16[688,1024]{1,0:T(8,128)(2,1)}, bf16[688,1024]{1,0:T(8,128)(2,1)}, u32[]{:S(2)}, u32[]{:S(2)}) collective-permute-start(bf16[688,1024]{1,0:T(8,128)(2,1)} %fusion.26), channel_id=1, source_target_pairs={{0,16},{1,17},{2,18},{3,19},{4,20},{5,21},{6,22},{7,23},{8,24},{9,... | collective-permute-start | bytes 4227080 | tf_op jit(solution)/shard_map/ppermute | solution.py:247
  400.9 33.9 %collective-permute-start.21 = (bf16[688,1024]{1,0:T(8,128)(2,1)S(1)}, bf16[688,1024]{1,0:T(8,128)(2,1)S(1)}, u32[]{:S(2)}, u32[]{:S(2)}) collective-permute-start(bf16[688,1024]{1,0:T(8,128)(2,1)S(1)} %fusion.29), channel_id=1, source_target_pairs={{0,16},{1,17},{2,18},{3,19},{4,20},{5,21},{6,22},{7,23},{8,24},{9,... | collective-permute-start | bytes 4227080 | tf_op jit(solution)/shard_map/ppermute | solution.py:247
  411.7 58.1 %collective-permute-start.19 = (bf16[512,2048]{1,0:T(8,128)(2,1)}, bf16[512,2048]{1,0:T(8,128)(2,1)}, u32[]{:S(2)}, u32[]{:S(2)}) collective-permute-start(bf16[512,2048]{1,0:T(8,128)(2,1)} %convolution_convert_fusion.3), channel_id=1, source_target_pairs={{0,8},{1,9},{2,10},{3,11},{4,12},{5,13},{6,14},{7,15},{8,0},{9,1},... | collective-permute-start | bytes 6291464 | tf_op jit(solution)/shard_map/ppermute | solution.py:247
  411.7 46.0 %collective-permute-start.23 = (bf16[688,1024]{1,0:T(8,128)(2,1)}, bf16[688,1024]{1,0:T(8,128)(2,1)}, u32[]{:S(2)}, u32[]{:S(2)}) collective-permute-start(bf16[688,1024]{1,0:T(8,128)(2,1)} %add_convert_fusion.8.kept_ref), channel_id=1, source_target_pairs={{4,0},{5,1},{6,2},{7,3},{8,12},{9,13},{10,14},{11,15},{20,16},{21,... | collective-permute-start | bytes 4227080 | tf_op jit(solution)/shard_map/ppermute | solution.py:250
  415.8 49.2 %collective-permute-start.26 = (bf16[688,1024]{1,0:T(8,128)(2,1)}, bf16[688,1024]{1,0:T(8,128)(2,1)}, u32[]{:S(2)}, u32[]{:S(2)}) collective-permute-start(bf16[688,1024]{1,0:T(8,128)(2,1)} %fusion.32), channel_id=1, source_target_pairs={{0,16},{1,17},{2,18},{3,19},{4,20},{5,21},{6,22},{7,23},{8,24},{9,... | collective-permute-start | bytes 4227080 | tf_op jit(solution)/shard_map/ppermute | solution.py:247
  451.2 48.4 %collective-permute-start.22 = (bf16[2,4,2,64,512]{4,3,2,1,0:T(8,128)(2,1)}, bf16[2,4,2,64,512]{4,3,2,1,0:T(8,128)(2,1)}, u32[]{:S(2)}, u32[]{:S(2)}) collective-permute-start(bf16[2,4,2,64,512]{4,3,2,1,0:T(8,128)(2,1)} %get-tuple-element.105), channel_id=1, source_target_pairs={{4,0},{5,1},{6,2},{7,3},{12,8},{13,9},{14,10},{15,11},{20,16},{21,... | collective-permute-start | bytes 3145736 | tf_op jit(solution)/shard_map/ppermute | solution.py:250
  455.6 44.1 %collective-permute-start.25 = (bf16[1024,512]{1,0:T(8,128)(2,1)}, bf16[1024,512]{1,0:T(8,128)(2,1)}, u32[]{:S(2)}, u32[]{:S(2)}) collective-permute-start(bf16[1024,512]{1,0:T(8,128)(2,1)} %pad_maximum_fusion.3), channel_id=1, source_target_pairs={{0,16},{1,17},{2,18},{3,19},{4,20},{5,21},{6,22},{7,23},{8,24},{9,... | collective-permute-start | bytes 3145736 | tf_op jit(solution)/shard_map/ppermute | solution.py:247
  460.5 14.9 %collective-permute-start.24 = (bf16[688,512]{1,0:T(8,128)(2,1)}, bf16[688,512]{1,0:T(8,128)(2,1)S(1)}, u32[]{:S(2)}, u32[]{:S(2)}) collective-permute-start(bf16[688,512]{1,0:T(8,128)(2,1)} %shard_map.244), channel_id=1, source_target_pairs={{0,8},{1,9},{2,10},{3,11},{12,4},{13,5},{14,6},{15,7},{16,24},{17,... | collective-permute-start | bytes 2113544 | tf_op jit(solution)/shard_map/ppermute | solution.py:250
  479.5 62.1 %all-to-all-start.5 = ((bf16[4,128,2048]{2,1,0:T(8,128)(2,1)}), bf16[4,128,2048]{2,1,0:T(8,128)(2,1)S(1)}, u32[]{:S(2)}, u32[]{:S(2)}) async-start(bf16[4,128,2048]{2,1,0:T(8,128)(2,1)} %bitcast.107), calls=%async_computation.5 | async-start | bytes 4194304 | tf_op jit(solution)/shard_map/all_to_all | solution.py:299
  508.3 32.2 %collective-permute-start.29 = (bf16[688,1024]{1,0:T(8,128)(2,1)S(1)}, bf16[688,1024]{1,0:T(8,128)(2,1)S(1)}, u32[]{:S(2)}, u32[]{:S(2)}) collective-permute-start(bf16[688,1024]{1,0:T(8,128)(2,1)S(1)} %copy-done.32), channel_id=1, source_target_pairs={{4,0},{5,1},{6,2},{7,3},{8,12},{9,13},{10,14},{11,15},{20,16},{21,... | collective-permute-start | bytes 4227080 | tf_op jit(solution)/shard_map/ppermute | solution.py:250
  509.6 25.7 %collective-permute-start.28 = (bf16[1024,512]{1,0:T(8,128)(2,1)S(1)}, bf16[1024,512]{1,0:T(8,128)(2,1)S(1)}, u32[]{:S(2)}, u32[]{:S(2)}) collective-permute-start(bf16[1024,512]{1,0:T(8,128)(2,1)S(1)} %get-tuple-element.152), channel_id=1, source_target_pairs={{0,16},{1,17},{2,18},{3,19},{4,20},{5,21},{6,22},{7,23},{8,24},{9,... | collective-permute-start | bytes 3145736 | tf_op jit(solution)/shard_map/ppermute | solution.py:247
  543.0 54.6 %all-to-all-start.7 = ((bf16[4,128,2048]{2,1,0:T(8,128)(2,1)}), bf16[4,128,2048]{2,1,0:T(8,128)(2,1)}, u32[]{:S(2)}, u32[]{:S(2)}) async-start(bf16[4,128,2048]{2,1,0:T(8,128)(2,1)} %bitcast.108), calls=%async_computation.7 | async-start | bytes 4194304 | tf_op jit(solution)/shard_map/all_to_all | solution.py:299
  552.5 44.1 %collective-permute-start.31 = (bf16[1024,512]{1,0:T(8,128)(2,1)S(1)}, bf16[1024,512]{1,0:T(8,128)(2,1)S(1)}, u32[]{:S(2)}, u32[]{:S(2)}) collective-permute-start(bf16[1024,512]{1,0:T(8,128)(2,1)S(1)} %get-tuple-element.137.kept_ref), channel_id=1, source_target_pairs={{4,0},{5,1},{6,2},{7,3},{8,12},{9,13},{10,14},{11,15},{20,16},{21,... | collective-permute-start | bytes 3145736 | tf_op jit(solution)/shard_map/ppermute | solution.py:250
  553.8 58.0 %collective-permute-start.34 = (bf16[688,1024]{1,0:T(8,128)(2,1)}, bf16[688,1024]{1,0:T(8,128)(2,1)}, u32[]{:S(2)}, u32[]{:S(2)}) collective-permute-start(bf16[688,1024]{1,0:T(8,128)(2,1)} %add_convert_fusion.7.kept_ref), channel_id=1, source_target_pairs={{4,0},{5,1},{6,2},{7,3},{8,12},{9,13},{10,14},{11,15},{20,16},{21,... | collective-permute-start | bytes 4227080 | tf_op jit(solution)/shard_map/ppermute | solution.py:250
  597.6 49.5 %all-to-all-start.6 = ((bf16[4,128,2048]{2,1,0:T(8,128)(2,1)}), bf16[4,128,2048]{2,1,0:T(8,128)(2,1)}, u32[]{:S(2)}, u32[]{:S(2)}) async-start(bf16[4,128,2048]{2,1,0:T(8,128)(2,1)} %bitcast.106), calls=%async_computation.6 | async-start | bytes 4194304 | tf_op jit(solution)/shard_map/all_to_all | solution.py:299
  607.3 25.8 %collective-permute-start.32 = (bf16[1024,512]{1,0:T(8,128)(2,1)S(1)}, bf16[1024,512]{1,0:T(8,128)(2,1)S(1)}, u32[]{:S(2)}, u32[]{:S(2)}) collective-permute-start(bf16[1024,512]{1,0:T(8,128)(2,1)S(1)} %fusion.5.kept_ref), channel_id=1, source_target_pairs={{4,0},{5,1},{6,2},{7,3},{8,12},{9,13},{10,14},{11,15},{20,16},{21,... | collective-permute-start | bytes 3145736 | tf_op jit(solution)/shard_map/ppermute | solution.py:250
  625.3 33.2 %collective-permute-start.37 = (bf16[688,512]{1,0:T(8,128)(2,1)}, bf16[688,512]{1,0:T(8,128)(2,1)}, u32[]{:S(2)}, u32[]{:S(2)}) collective-permute-start(bf16[688,512]{1,0:T(8,128)(2,1)} %shard_map.253), channel_id=1, source_target_pairs={{0,8},{1,9},{2,10},{3,11},{12,4},{13,5},{14,6},{15,7},{16,24},{17,... | collective-permute-start | bytes 2113544 | tf_op jit(solution)/shard_map/ppermute | solution.py:250
  631.0 16.1 %collective-permute-start.33 = (bf16[512,512]{1,0:T(8,128)(2,1)}, bf16[512,512]{1,0:T(8,128)(2,1)}, u32[]{:S(2)}, u32[]{:S(2)}) collective-permute-start(bf16[512,512]{1,0:T(8,128)(2,1)} %shard_map.246), channel_id=1, source_target_pairs={{0,8},{1,9},{2,10},{3,11},{12,4},{13,5},{14,6},{15,7},{16,24},{17,... | collective-permute-start | bytes 1572872 | tf_op jit(solution)/shard_map/ppermute | solution.py:250
  650.9 15.5 %all-to-all-start.8 = ((f32[32,1,192]{2,1,0:T(1,128)}), f32[32,1,192]{2,1,0:T(1,128)S(1)}, u32[]{:S(2)}, u32[]{:S(2)}) async-start(f32[32,1,192]{2,1,0:T(1,128)} %reshape.214), calls=%async_computation.8 | async-start | bytes 65536 | tf_op jit(solution)/shard_map/all_to_all | solution.py:370
  (75 other events, 522.8 us)
Sparse Core Ops, SparseCore 0:
  24.8 39.4 all-gather.5
  66.4 49.5 all-gather.7
  255.9 43.3 all-gather.9
  301.3 29.3 all-gather.11
  397.1 38.9 all-gather.13

commit v4 on v3

--- a/solution.py
+++ b/solution.py
@@ -514,7 +514,7 @@
     down_half = at.swap(after(down_near, up_half), at.half_bit)
     gate_w = whole(gate_near, gate_half, gate_far, at.swap(gate_half, at.far_bit))
     up_w = whole(up_near, up_half, up_far, at.swap(up_half, at.far_bit))
-    ffn_all = after(gather(at, ffn_in), down_half, down_far, up_w)
+    ffn_all = after(gather(at, ffn_in), down_half, down_far, gate_w, up_w)
     final_all = gather(at, after(grad_final.astype(bf16), other_cache))
     gate = times_transposed(ffn_all, gate_w)
     up = times_transposed(ffn_all, after(up_w, gate))

time: 685 us -> 685 us (level)
    unnamed x155 -> x157, local copies, waits for them, and re-layouts: 30.9 us -> 29.9 us
where the time goes in v4:
time: 685 us; the launch traced here: 675 us
  waiting for transfers between devices  323 us (47%)
  matrix products  110 us (16%)
  starting transfers between devices  95.1 us (14%)
  Pallas kernels  54.1 us (8%)
  local copies, waits for them, and re-layouts  43.5 us (6%)
  other arithmetic  34 us (5%)
  between operations  15.4 us (2%)
    ppermute x26, waiting for transfers between devices, swap(): return lax.ppermute(value, AXES, [(i, i ^ mask) for i in range(self.count)])  210 us
    dot_general x30, matrix products, dot(): lax.dot_general(left, right, (over, ((), ())), preferred_element_type=kind)  110 us
    ppermute x12, waiting for transfers between devices, send(): lax.ppermute(value, AXES, [(i, i ^ mask) for i in range(self.count) if ch...  69.4 us
    ppermute x26, starting transfers between devices, swap(): return lax.ppermute(value, AXES, [(i, i ^ mask) for i in range(self.count)])  31.5 us
    unnamed x157, local copies, waits for them, and re-layouts  29.9 us
    pallas_call x10, Pallas kernels, halves_call(): pl.pallas_call(kernel, grid_spec=pltpu.PrefetchScalarGridSpec(num_scalar_...  29.2 us
    all_to_all x5, waiting for transfers between devices, scatter(): kept = lax.all_to_all(kept, INNER, split_axis=0, concat_axis=0, tiled=True)  26 us
    ppermute x12, starting transfers between devices, send(): lax.ppermute(value, AXES, [(i, i ^ mask) for i in range(self.count) if ch...  22.6 us
  transfers between devices with their start and end apart: 52, of which 27 were waited for; matrix products, arithmetic and copies ran while one was open for 21% of the time, Pallas kernels for 8%

profile of v4, /device:TPU:0, one launch (start us, length us, event | category | flops | bytes accessed | tf_op | source)
XLA Modules:
  0.0 675.0 jit_solution(11576392167380358363)
XLA Ops:
  10.1 5.3 all-to-all-start
  18.4 6.3 all-to-all-done
  34.0 19.1 %collective-permute-done = bf16[512,512]{1,0:T(8,128)(2,1)} collective-permute-done((bf16[512,512]{1,0:T(8,128)(2,1)}, bf16[512,512]{1,0:T(8,128)(2,1)}, u32[]{:S(2)}, u32[]{:S(2)}) %collective-permute-start) | collective-permute-done | bytes 524320 | tf_op jit(solution)/shard_map/ppermute | solution.py:247
  53.1 11.2 %all-gather.6.cloned.1.call-done = bf16[1024,2048]{1,0:T(8,128)(2,1)} async-done(((bf16[128,2048]{1,0:T(8,128)(2,1)}), bf16[1024,2048]{1,0:T(8,128)(2,1)}) %all-gather.6.cloned.1.call-update) | async-done | bytes 4194320 | tf_op jit(solution)/shard_map/all_gather | solution.py:281
  67.6 4.1 all-to-all-start.1
  73.8 4.9 collective-permute-done.3
  78.8 5.9 fusion.102
  84.7 3.7 all-to-all-start.2
  91.8 3.9 collective-permute-start.4
  95.7 36.3 %collective-permute-done.5 = bf16[512,512]{1,0:T(8,128)(2,1)} collective-permute-done((bf16[512,512]{1,0:T(8,128)(2,1)}, bf16[512,512]{1,0:T(8,128)(2,1)}, u32[]{:S(2)}, u32[]{:S(2)}) %collective-permute-start.5) | collective-permute-done | bytes 524320 | tf_op jit(solution)/shard_map/ppermute | solution.py:247
  142.6 4.5 collective-permute-done.7
  148.9 5.5 collective-permute-done.4.okv_ref
  154.4 3.7 fusion.101
  158.2 7.4 %shard_map.242 = bf16[2,4,2,64,256]{4,3,2,1,0:T(8,128)(2,1)S(1)} custom-call(bf16[2,4,2,64,256]{4,3,2,1,0:T(8,128)(2,1)S(1)} %bitcast.79, bf16[2,4,2,64,512]{4,3,2,1,0:T(8,128)(2,1)S(1)} %bitcast.77, bf16[2,4,2,64,512]{4,3,2,1,0:T(8,128)(2,1)} %collective-permute-done.4.okv_ref, s32[2,2,256,2]{3,2,1,0:T(8,128)S(1)} %copy-done, ...), custom_call_target="tpu_custom_call" | custom-call | flops 1 | bytes 1 | tf_op jit(solution)/shard_map/pallas_call | solution.py:114
  167.8 6.9 %collective-permute-start.10 = (bf16[688,512]{1,0:T(8,128)(2,1)}, bf16[688,512]{1,0:T(8,128)(2,1)}, u32[]{:S(2)}, u32[]{:S(2)}) collective-permute-start(bf16[688,512]{1,0:T(8,128)(2,1)} %get-tuple-element.84), channel_id=1, source_target_pairs={{0,4},{1,5},{2,6},{3,7},{4,0},{5,1},{6,2},{7,3},{8,12},{9,13},{10,... | collective-permute-start | bytes 2113544 | tf_op jit(solution)/shard_map/ppermute | solution.py:247
  174.7 4.0 add_convert_fusion.5
  178.7 27.9 %collective-permute-done.10 = bf16[688,512]{1,0:T(8,128)(2,1)} collective-permute-done((bf16[688,512]{1,0:T(8,128)(2,1)}, bf16[688,512]{1,0:T(8,128)(2,1)}, u32[]{:S(2)}, u32[]{:S(2)}) %collective-permute-start.10) | collective-permute-done | bytes 704544 | tf_op jit(solution)/shard_map/ppermute | solution.py:247
  206.5 4.4 all-to-all-start.3
  213.3 15.8 %collective-permute-done.12 = bf16[688,512]{1,0:T(8,128)(2,1)} collective-permute-done((bf16[688,512]{1,0:T(8,128)(2,1)}, bf16[688,512]{1,0:T(8,128)(2,1)}, u32[]{:S(2)}, u32[]{:S(2)}) %collective-permute-start.12) | collective-permute-done | bytes 704544 | tf_op jit(solution)/shard_map/ppermute | solution.py:247
  229.0 20.2 %collective-permute-done.11 = bf16[688,512]{1,0:T(8,128)(2,1)} collective-permute-done((bf16[688,512]{1,0:T(8,128)(2,1)}, bf16[688,512]{1,0:T(8,128)(2,1)}, u32[]{:S(2)}, u32[]{:S(2)}) %collective-permute-start.11) | collective-permute-done | bytes 704544 | tf_op jit(solution)/shard_map/ppermute | solution.py:247
  272.9 19.6 %collective-permute-done.15 = bf16[688,512]{1,0:T(8,128)(2,1)S(1)} collective-permute-done((bf16[688,512]{1,0:T(8,128)(2,1)}, bf16[688,512]{1,0:T(8,128)(2,1)S(1)}, u32[]{:S(2)}, u32[]{:S(2)}) %collective-permute-start.15) | collective-permute-done | bytes 704544 | tf_op jit(solution)/shard_map/ppermute | solution.py:247
  295.6 12.0 %collective-permute-done.16 = bf16[688,512]{1,0:T(8,128)(2,1)S(1)} collective-permute-done((bf16[688,512]{1,0:T(8,128)(2,1)}, bf16[688,512]{1,0:T(8,128)(2,1)S(1)}, u32[]{:S(2)}, u32[]{:S(2)}) %collective-permute-start.16) | collective-permute-done | bytes 704544 | tf_op jit(solution)/shard_map/ppermute | solution.py:247
  308.6 8.3 %fusion.109 = f32[1024,688]{0,1:T(8,128)} fusion(bf16[1024,2048]{1,0:T(8,128)(2,1)} %all-gather.10.cloned.1.call-done, bf16[688,2048]{1,0:T(8,128)(2,1)} %copy-done.35), kind=kOutput, calls=%fused_computation.176 | convolution fusion | flops 2885681152 | bytes 9830400 | tf_op jit(solution)/shard_map/dot_general | solution.py:22
  316.9 6.6 fusion.110
  330.4 9.8 %multiply_convert_fusion.1 = (bf16[1024,688]{0,1:T(8,128)(2,1)S(1)}, bf16[1024,688]{0,1:T(8,128)(2,1)S(1)}, bf16[1024,688]{0,1:T(8,128)(2,1)}) fusion(f32[1024,688]{0,1:T(8,128)} %fusion.109, f32[1024,688]{0,1:T(8,128)} %fusion.110, bf16[1024,2048]{1,0:T(8,128)(2,1)} %all-gather.12.cloned.1.call-done, bf16[688,2048]{1,0:T(8,128)(2,1)} %constant_dynamic-update-slice_fusion.8), kind=kOutput, calls=%fused_computation.19 | convolution fusion | flops 2896248832 | bytes 16875520 | tf_op jit(solution)/shard_map/dot_general | solution.py:22
  340.2 4.7 fusion.74
  352.4 3.7 fusion.77
  358.6 4.4 all-to-all-start.4
  364.8 23.9 %all-to-all-done.4 = bf16[4,128,2048]{2,1,0:T(8,128)(2,1)} async-done(((bf16[4,128,2048]{2,1,0:T(8,128)(2,1)}), bf16[4,128,2048]{2,1,0:T(8,128)(2,1)}, u32[]{:S(2)}, u32[]{:S(2)}) %all-to-all-start.4) | async-done | bytes 2097184 | tf_op jit(solution)/shard_map/all_to_all | solution.py:299
  392.8 3.9 collective-permute-done.20
  396.7 3.8 fusion.29
  402.1 4.1 add_convert_fusion.8.kept_ref
  406.2 5.2 convolution_convert_fusion.3
  416.3 18.1 %collective-permute-done.21 = bf16[688,1024]{1,0:T(8,128)(2,1)S(1)} collective-permute-done((bf16[688,1024]{1,0:T(8,128)(2,1)S(1)}, bf16[688,1024]{1,0:T(8,128)(2,1)S(1)}, u32[]{:S(2)}, u32[]{:S(2)}) %collective-permute-start.21) | collective-permute-done | bytes 1409056 | tf_op jit(solution)/shard_map/ppermute | solution.py:247
  437.2 3.8 fusion.100
  441.0 9.8 %shard_map.243 = (bf16[2,4,2,64,256]{4,3,2,1,0:T(8,128)(2,1)S(1)}, f32[2,4,2,64,512]{4,3,2,1,0:T(8,128)}, bf16[2,4,2,64,512]{4,3,2,1,0:T(8,128)(2,1)}) custom-call(bf16[2,4,2,64,256]{4,3,2,1,0:T(8,128)(2,1)S(1)} %bitcast.80, bf16[2,4,2,64,512]{4,3,2,1,0:T(8,128)(2,1)S(1)} %bitcast.78, bf16[2,4,2,64,512]{4,3,2,1,0:T(8,128)(2,1)} %collective-permute-done.4.okv_ref, ...), custom_call_target="tpu_custom_call" | custom-call | flops 1 | bytes 1 | tf_op jit(solution)/shard_map/pallas_call | solution.py:114
  464.7 4.7 add_convert_fusion.6.kept_ref
  469.4 5.6 add_convert_fusion.2
  479.1 3.9 all-to-all-start.5
  483.0 16.4 %collective-permute-done.22 = bf16[2,4,2,64,512]{4,3,2,1,0:T(8,128)(2,1)} collective-permute-done((bf16[2,4,2,64,512]{4,3,2,1,0:T(8,128)(2,1)}, bf16[2,4,2,64,512]{4,3,2,1,0:T(8,128)(2,1)}, u32[]{:S(2)}, u32[]{:S(2)}) %collective-permute-start.22) | collective-permute-done | bytes 1048608 | tf_op jit(solution)/shard_map/ppermute | solution.py:250
  512.1 4.0 add_convert_fusion.1
  516.1 18.9 %collective-permute-done.28 = bf16[1024,512]{1,0:T(8,128)(2,1)S(1)} collective-permute-done((bf16[1024,512]{1,0:T(8,128)(2,1)S(1)}, bf16[1024,512]{1,0:T(8,128)(2,1)S(1)}, u32[]{:S(2)}, u32[]{:S(2)}) %collective-permute-start.28) | collective-permute-done | bytes 1048608 | tf_op jit(solution)/shard_map/ppermute | solution.py:247
  535.0 5.2 collective-permute-done.29.given_ref
  542.7 4.4 all-to-all-start.7
  547.2 4.1 multiply_reduce_fusion.1
  558.3 37.9 %collective-permute-done.31.given_ref = bf16[1024,512]{1,0:T(8,128)(2,1)S(1)} collective-permute-done((bf16[1024,512]{1,0:T(8,128)(2,1)S(1)}, bf16[1024,512]{1,0:T(8,128)(2,1)S(1)}, u32[]{:S(2)}, u32[]{:S(2)}) %collective-permute-start.31) | collective-permute-done | bytes 1048608 | tf_op jit(solution)/shard_map/ppermute | solution.py:250
  597.3 4.6 all-to-all-start.6
  650.6 5.5 all-to-all-start.8
  (333 shorter events, 202.0 us)
Async XLA Ops:
  10.1 14.5 %all-to-all-start = ((bf16[8,64,512]{2,1,0:T(8,128)(2,1)}), bf16[8,64,512]{2,1,0:T(8,128)(2,1)S(1)}, u32[]{:S(2)}, u32[]{:S(2)}) async-start(bf16[8,64,512]{2,1,0:T(8,128)(2,1)} %shard_map.238), calls=%async_computation | async-start | bytes 1048576 | tf_op jit(solution)/shard_map/all_to_all | solution.py:269
  15.4 48.9 %all-gather.6.cloned.1.call-start = ((), (), s32[]{:S(2)}) async-start(), calls=%async_computation.9 | async-start | bytes 4718592 | tf_op jit(solution)/shard_map/all_gather | solution.py:281
  24.7 129.7 %all-gather.8.cloned.1.call-start = ((), (), s32[]{:S(2)}) async-start(), calls=%async_computation.10 | async-start | bytes 4718592 | tf_op jit(solution)/shard_map/all_gather | solution.py:281
  24.9 5.6 collective-permute-start.2
  26.4 26.6 %collective-permute-start = (bf16[512,512]{1,0:T(8,128)(2,1)}, bf16[512,512]{1,0:T(8,128)(2,1)}, u32[]{:S(2)}, u32[]{:S(2)}) collective-permute-start(bf16[512,512]{1,0:T(8,128)(2,1)} %bitcast.117), channel_id=1, source_target_pairs={{0,4},{1,5},{2,6},{3,7},{4,0},{5,1},{6,2},{7,3},{8,12},{9,13},{10,... | collective-permute-start | bytes 1572872 | tf_op jit(solution)/shard_map/ppermute | solution.py:247
  29.0 24.0 %collective-permute-start.1 = (bf16[512,512]{1,0:T(8,128)(2,1)}, bf16[512,512]{1,0:T(8,128)(2,1)}, u32[]{:S(2)}, u32[]{:S(2)}) collective-permute-start(bf16[512,512]{1,0:T(8,128)(2,1)} %bitcast.118), channel_id=1, source_target_pairs={{0,16},{1,17},{2,18},{3,19},{4,20},{5,21},{6,22},{7,23},{8,24},{9,... | collective-permute-start | bytes 1572872 | tf_op jit(solution)/shard_map/ppermute | solution.py:247
  64.3 14.5 %collective-permute-start.3 = (bf16[512,512]{1,0:T(8,128)(2,1)}, bf16[512,512]{1,0:T(8,128)(2,1)}, u32[]{:S(2)}, u32[]{:S(2)}) collective-permute-start(bf16[512,512]{1,0:T(8,128)(2,1)} %collective-permute-done), channel_id=1, source_target_pairs={{0,16},{1,17},{2,18},{3,19},{4,20},{5,21},{6,22},{7,23},{8,24},{9,... | collective-permute-start | bytes 1572872 | tf_op jit(solution)/shard_map/ppermute | solution.py:247
  67.6 17.1 %all-to-all-start.1 = ((bf16[8,64,512]{2,1,0:T(8,128)(2,1)}), bf16[8,64,512]{2,1,0:T(8,128)(2,1)}, u32[]{:S(2)}, u32[]{:S(2)}) async-start(bf16[8,64,512]{2,1,0:T(8,128)(2,1)} %shard_map.239), calls=%async_computation.1 | async-start | bytes 1048576 | tf_op jit(solution)/shard_map/all_to_all | solution.py:269
  84.7 53.5 %all-to-all-start.2 = ((bf16[8,192,688]{2,1,0:T(8,128)(2,1)}), bf16[8,192,688]{2,1,0:T(8,128)(2,1)S(1)}, u32[]{:S(2)}, u32[]{:S(2)}) async-start(bf16[8,192,688]{2,1,0:T(8,128)(2,1)} %shard_map.240), calls=%async_computation.2 | async-start | bytes 4718592 | tf_op jit(solution)/shard_map/all_to_all | solution.py:269
  88.3 43.7 %collective-permute-start.5 = (bf16[512,512]{1,0:T(8,128)(2,1)}, bf16[512,512]{1,0:T(8,128)(2,1)}, u32[]{:S(2)}, u32[]{:S(2)}) collective-permute-start(bf16[512,512]{1,0:T(8,128)(2,1)} %bitcast.15), channel_id=1, source_target_pairs={{0,4},{1,5},{2,6},{3,7},{4,0},{5,1},{6,2},{7,3},{8,12},{9,13},{10,... | collective-permute-start | bytes 1572872 | tf_op jit(solution)/shard_map/ppermute | solution.py:247
  90.2 46.0 %collective-permute-start.6 = (bf16[512,512]{1,0:T(8,128)(2,1)}, bf16[512,512]{1,0:T(8,128)(2,1)}, u32[]{:S(2)}, u32[]{:S(2)}) collective-permute-start(bf16[512,512]{1,0:T(8,128)(2,1)} %bitcast.15), channel_id=1, source_target_pairs={{0,16},{1,17},{2,18},{3,19},{4,20},{5,21},{6,22},{7,23},{8,24},{9,... | collective-permute-start | bytes 1572872 | tf_op jit(solution)/shard_map/ppermute | solution.py:247
  91.8 62.6 %collective-permute-start.4 = (bf16[2,4,2,64,512]{4,3,2,1,0:T(8,128)(2,1)}, bf16[2,4,2,64,512]{4,3,2,1,0:T(8,128)(2,1)}, u32[]{:S(2)}, u32[]{:S(2)}) collective-permute-start(bf16[2,4,2,64,512]{4,3,2,1,0:T(8,128)(2,1)} %bitcast.76), channel_id=1, source_target_pairs={{0,4},{1,5},{2,6},{3,7},{8,12},{9,13},{10,14},{11,15},{16,20},{17,... | collective-permute-start | bytes 3145736 | tf_op jit(solution)/shard_map/ppermute | solution.py:250
  132.0 15.1 %collective-permute-start.7 = (bf16[512,512]{1,0:T(8,128)(2,1)}, bf16[512,512]{1,0:T(8,128)(2,1)}, u32[]{:S(2)}, u32[]{:S(2)}) collective-permute-start(bf16[512,512]{1,0:T(8,128)(2,1)} %collective-permute-done.5), channel_id=1, source_target_pairs={{0,16},{1,17},{2,18},{3,19},{4,20},{5,21},{6,22},{7,23},{8,24},{9,... | collective-permute-start | bytes 1572872 | tf_op jit(solution)/shard_map/ppermute | solution.py:247
  141.2 24.5 %collective-permute-start.8 = (bf16[688,512]{1,0:T(8,128)(2,1)}, bf16[688,512]{1,0:T(8,128)(2,1)}, u32[]{:S(2)}, u32[]{:S(2)}) collective-permute-start(bf16[688,512]{1,0:T(8,128)(2,1)} %get-tuple-element.84), channel_id=1, source_target_pairs={{0,16},{1,17},{2,18},{3,19},{4,20},{5,21},{6,22},{7,23},{8,24},{9,... | collective-permute-start | bytes 2113544 | tf_op jit(solution)/shard_map/ppermute | solution.py:247
  167.8 6.9 %collective-permute-start.9 = (bf16[512,2048]{1,0:T(8,128)(2,1)}, bf16[512,2048]{1,0:T(8,128)(2,1)}, u32[]{:S(2)}, u32[]{:S(2)}) collective-permute-start(bf16[512,2048]{1,0:T(8,128)(2,1)} %convolution_convert_fusion.1), channel_id=1, source_target_pairs={{0,8},{1,9},{2,10},{3,11},{4,12},{5,13},{6,14},{7,15},{8,0},{9,1},... | collective-permute-start | bytes 6291464 | tf_op jit(solution)/shard_map/ppermute | solution.py:247
  167.8 38.7 %collective-permute-start.10 = (bf16[688,512]{1,0:T(8,128)(2,1)}, bf16[688,512]{1,0:T(8,128)(2,1)}, u32[]{:S(2)}, u32[]{:S(2)}) collective-permute-start(bf16[688,512]{1,0:T(8,128)(2,1)} %get-tuple-element.84), channel_id=1, source_target_pairs={{0,4},{1,5},{2,6},{3,7},{4,0},{5,1},{6,2},{7,3},{8,12},{9,13},{10,... | collective-permute-start | bytes 2113544 | tf_op jit(solution)/shard_map/ppermute | solution.py:247
  206.5 44.9 %all-to-all-start.3 = ((bf16[4,128,2048]{2,1,0:T(8,128)(2,1)}), bf16[4,128,2048]{2,1,0:T(8,128)(2,1)}, u32[]{:S(2)}, u32[]{:S(2)}) async-start(bf16[4,128,2048]{2,1,0:T(8,128)(2,1)} %bitcast.109), calls=%async_computation.3 | async-start | bytes 4194304 | tf_op jit(solution)/shard_map/all_to_all | solution.py:299
  211.0 97.6 %all-gather.10.cloned.1.call-start = ((), (), s32[]{:S(2)}) async-start(), calls=%async_computation.11 | async-start | bytes 4718592 | tf_op jit(solution)/shard_map/all_gather | solution.py:281
  211.0 18.0 %collective-permute-start.12 = (bf16[688,512]{1,0:T(8,128)(2,1)}, bf16[688,512]{1,0:T(8,128)(2,1)}, u32[]{:S(2)}, u32[]{:S(2)}) collective-permute-start(bf16[688,512]{1,0:T(8,128)(2,1)} %copy-done.6), channel_id=1, source_target_pairs={{0,16},{1,17},{2,18},{3,19},{4,20},{5,21},{6,22},{7,23},{8,24},{9,... | collective-permute-start | bytes 2113544 | tf_op jit(solution)/shard_map/ppermute | solution.py:247
  211.4 37.8 %collective-permute-start.11 = (bf16[688,512]{1,0:T(8,128)(2,1)}, bf16[688,512]{1,0:T(8,128)(2,1)}, u32[]{:S(2)}, u32[]{:S(2)}) collective-permute-start(bf16[688,512]{1,0:T(8,128)(2,1)} %copy-done.6), channel_id=1, source_target_pairs={{0,4},{1,5},{2,6},{3,7},{4,0},{5,1},{6,2},{7,3},{8,12},{9,13},{10,... | collective-permute-start | bytes 2113544 | tf_op jit(solution)/shard_map/ppermute | solution.py:247
  255.7 74.7 %all-gather.12.cloned.1.call-start = ((), (), s32[]{:S(2)}) async-start(), calls=%async_computation.12 | async-start | bytes 4718592 | tf_op jit(solution)/shard_map/all_gather | solution.py:281
  258.4 50.2 %collective-permute-start.14 = (bf16[688,512]{1,0:T(8,128)(2,1)}, bf16[688,512]{1,0:T(8,128)(2,1)}, u32[]{:S(2)}, u32[]{:S(2)}) collective-permute-start(bf16[688,512]{1,0:T(8,128)(2,1)} %copy-done.4), channel_id=1, source_target_pairs={{0,16},{1,17},{2,18},{3,19},{4,20},{5,21},{6,22},{7,23},{8,24},{9,... | collective-permute-start | bytes 2113544 | tf_op jit(solution)/shard_map/ppermute | solution.py:247
  260.9 31.6 %collective-permute-start.15 = (bf16[688,512]{1,0:T(8,128)(2,1)}, bf16[688,512]{1,0:T(8,128)(2,1)S(1)}, u32[]{:S(2)}, u32[]{:S(2)}) collective-permute-start(bf16[688,512]{1,0:T(8,128)(2,1)} %collective-permute-done.10), channel_id=1, source_target_pairs={{0,16},{1,17},{2,18},{3,19},{4,20},{5,21},{6,22},{7,23},{8,24},{9,... | collective-permute-start | bytes 2113544 | tf_op jit(solution)/shard_map/ppermute | solution.py:247
  263.8 31.7 %collective-permute-start.13 = (bf16[688,512]{1,0:T(8,128)(2,1)S(1)}, bf16[688,512]{1,0:T(8,128)(2,1)}, u32[]{:S(2)}, u32[]{:S(2)}) collective-permute-start(bf16[688,512]{1,0:T(8,128)(2,1)S(1)} %copy-done.5), channel_id=1, source_target_pairs={{0,4},{1,5},{2,6},{3,7},{4,0},{5,1},{6,2},{7,3},{8,12},{9,13},{10,... | collective-permute-start | bytes 2113544 | tf_op jit(solution)/shard_map/ppermute | solution.py:247
  265.1 42.5 %collective-permute-start.16 = (bf16[688,512]{1,0:T(8,128)(2,1)}, bf16[688,512]{1,0:T(8,128)(2,1)S(1)}, u32[]{:S(2)}, u32[]{:S(2)}) collective-permute-start(bf16[688,512]{1,0:T(8,128)(2,1)} %collective-permute-done.11), channel_id=1, source_target_pairs={{0,16},{1,17},{2,18},{3,19},{4,20},{5,21},{6,22},{7,23},{8,24},{9,... | collective-permute-start | bytes 2113544 | tf_op jit(solution)/shard_map/ppermute | solution.py:247
  295.6 32.1 %collective-permute-start.17 = (bf16[688,512]{1,0:T(8,128)(2,1)}, bf16[688,512]{1,0:T(8,128)(2,1)}, u32[]{:S(2)}, u32[]{:S(2)}) collective-permute-start(bf16[688,512]{1,0:T(8,128)(2,1)} %collective-permute-done.13), channel_id=1, source_target_pairs={{0,16},{1,17},{2,18},{3,19},{4,20},{5,21},{6,22},{7,23},{8,24},{9,... | collective-permute-start | bytes 2113544 | tf_op jit(solution)/shard_map/ppermute | solution.py:247
  350.2 5.9 collective-permute-start.18
  358.6 30.1 %all-to-all-start.4 = ((bf16[4,128,2048]{2,1,0:T(8,128)(2,1)}), bf16[4,128,2048]{2,1,0:T(8,128)(2,1)}, u32[]{:S(2)}, u32[]{:S(2)}) async-start(bf16[4,128,2048]{2,1,0:T(8,128)(2,1)} %bitcast.105), calls=%async_computation.4 | async-start | bytes 4194304 | tf_op jit(solution)/shard_map/all_to_all | solution.py:299
  363.1 74.2 %all-gather.14.cloned.1.call-start = ((), (), s32[]{:S(2)}) async-start(), calls=%async_computation.13 | async-start | bytes 4718592 | tf_op jit(solution)/shard_map/all_gather | solution.py:281
  363.3 33.4 %collective-permute-start.20 = (bf16[688,1024]{1,0:T(8,128)(2,1)}, bf16[688,1024]{1,0:T(8,128)(2,1)}, u32[]{:S(2)}, u32[]{:S(2)}) collective-permute-start(bf16[688,1024]{1,0:T(8,128)(2,1)} %fusion.26), channel_id=1, source_target_pairs={{0,16},{1,17},{2,18},{3,19},{4,20},{5,21},{6,22},{7,23},{8,24},{9,... | collective-permute-start | bytes 4227080 | tf_op jit(solution)/shard_map/ppermute | solution.py:247
  400.5 33.9 %collective-permute-start.21 = (bf16[688,1024]{1,0:T(8,128)(2,1)S(1)}, bf16[688,1024]{1,0:T(8,128)(2,1)S(1)}, u32[]{:S(2)}, u32[]{:S(2)}) collective-permute-start(bf16[688,1024]{1,0:T(8,128)(2,1)S(1)} %fusion.29), channel_id=1, source_target_pairs={{0,16},{1,17},{2,18},{3,19},{4,20},{5,21},{6,22},{7,23},{8,24},{9,... | collective-permute-start | bytes 4227080 | tf_op jit(solution)/shard_map/ppermute | solution.py:247
  411.4 58.1 %collective-permute-start.19 = (bf16[512,2048]{1,0:T(8,128)(2,1)}, bf16[512,2048]{1,0:T(8,128)(2,1)}, u32[]{:S(2)}, u32[]{:S(2)}) collective-permute-start(bf16[512,2048]{1,0:T(8,128)(2,1)} %convolution_convert_fusion.3), channel_id=1, source_target_pairs={{0,8},{1,9},{2,10},{3,11},{4,12},{5,13},{6,14},{7,15},{8,0},{9,1},... | collective-permute-start | bytes 6291464 | tf_op jit(solution)/shard_map/ppermute | solution.py:247
  411.4 46.0 %collective-permute-start.23 = (bf16[688,1024]{1,0:T(8,128)(2,1)}, bf16[688,1024]{1,0:T(8,128)(2,1)}, u32[]{:S(2)}, u32[]{:S(2)}) collective-permute-start(bf16[688,1024]{1,0:T(8,128)(2,1)} %add_convert_fusion.8.kept_ref), channel_id=1, source_target_pairs={{4,0},{5,1},{6,2},{7,3},{8,12},{9,13},{10,14},{11,15},{20,16},{21,... | collective-permute-start | bytes 4227080 | tf_op jit(solution)/shard_map/ppermute | solution.py:250
  415.5 49.2 %collective-permute-start.26 = (bf16[688,1024]{1,0:T(8,128)(2,1)}, bf16[688,1024]{1,0:T(8,128)(2,1)}, u32[]{:S(2)}, u32[]{:S(2)}) collective-permute-start(bf16[688,1024]{1,0:T(8,128)(2,1)} %fusion.32), channel_id=1, source_target_pairs={{0,16},{1,17},{2,18},{3,19},{4,20},{5,21},{6,22},{7,23},{8,24},{9,... | collective-permute-start | bytes 4227080 | tf_op jit(solution)/shard_map/ppermute | solution.py:247
  450.8 48.5 %collective-permute-start.22 = (bf16[2,4,2,64,512]{4,3,2,1,0:T(8,128)(2,1)}, bf16[2,4,2,64,512]{4,3,2,1,0:T(8,128)(2,1)}, u32[]{:S(2)}, u32[]{:S(2)}) collective-permute-start(bf16[2,4,2,64,512]{4,3,2,1,0:T(8,128)(2,1)} %get-tuple-element.105), channel_id=1, source_target_pairs={{4,0},{5,1},{6,2},{7,3},{12,8},{13,9},{14,10},{15,11},{20,16},{21,... | collective-permute-start | bytes 3145736 | tf_op jit(solution)/shard_map/ppermute | solution.py:250
  455.2 44.1 %collective-permute-start.25 = (bf16[1024,512]{1,0:T(8,128)(2,1)}, bf16[1024,512]{1,0:T(8,128)(2,1)}, u32[]{:S(2)}, u32[]{:S(2)}) collective-permute-start(bf16[1024,512]{1,0:T(8,128)(2,1)} %pad_maximum_fusion.3), channel_id=1, source_target_pairs={{0,16},{1,17},{2,18},{3,19},{4,20},{5,21},{6,22},{7,23},{8,24},{9,... | collective-permute-start | bytes 3145736 | tf_op jit(solution)/shard_map/ppermute | solution.py:247
  460.2 14.8 %collective-permute-start.24 = (bf16[688,512]{1,0:T(8,128)(2,1)}, bf16[688,512]{1,0:T(8,128)(2,1)S(1)}, u32[]{:S(2)}, u32[]{:S(2)}) collective-permute-start(bf16[688,512]{1,0:T(8,128)(2,1)} %shard_map.244), channel_id=1, source_target_pairs={{0,8},{1,9},{2,10},{3,11},{12,4},{13,5},{14,6},{15,7},{16,24},{17,... | collective-permute-start | bytes 2113544 | tf_op jit(solution)/shard_map/ppermute | solution.py:250
  479.1 62.2 %all-to-all-start.5 = ((bf16[4,128,2048]{2,1,0:T(8,128)(2,1)}), bf16[4,128,2048]{2,1,0:T(8,128)(2,1)S(1)}, u32[]{:S(2)}, u32[]{:S(2)}) async-start(bf16[4,128,2048]{2,1,0:T(8,128)(2,1)} %bitcast.107), calls=%async_computation.5 | async-start | bytes 4194304 | tf_op jit(solution)/shard_map/all_to_all | solution.py:299
  508.0 32.2 %collective-permute-start.29 = (bf16[688,1024]{1,0:T(8,128)(2,1)S(1)}, bf16[688,1024]{1,0:T(8,128)(2,1)S(1)}, u32[]{:S(2)}, u32[]{:S(2)}) collective-permute-start(bf16[688,1024]{1,0:T(8,128)(2,1)S(1)} %copy-done.33), channel_id=1, source_target_pairs={{4,0},{5,1},{6,2},{7,3},{8,12},{9,13},{10,14},{11,15},{20,16},{21,... | collective-permute-start | bytes 4227080 | tf_op jit(solution)/shard_map/ppermute | solution.py:250
  509.3 25.7 %collective-permute-start.28 = (bf16[1024,512]{1,0:T(8,128)(2,1)S(1)}, bf16[1024,512]{1,0:T(8,128)(2,1)S(1)}, u32[]{:S(2)}, u32[]{:S(2)}) collective-permute-start(bf16[1024,512]{1,0:T(8,128)(2,1)S(1)} %get-tuple-element.152), channel_id=1, source_target_pairs={{0,16},{1,17},{2,18},{3,19},{4,20},{5,21},{6,22},{7,23},{8,24},{9,... | collective-permute-start | bytes 3145736 | tf_op jit(solution)/shard_map/ppermute | solution.py:247
  542.7 54.6 %all-to-all-start.7 = ((bf16[4,128,2048]{2,1,0:T(8,128)(2,1)}), bf16[4,128,2048]{2,1,0:T(8,128)(2,1)}, u32[]{:S(2)}, u32[]{:S(2)}) async-start(bf16[4,128,2048]{2,1,0:T(8,128)(2,1)} %bitcast.108), calls=%async_computation.7 | async-start | bytes 4194304 | tf_op jit(solution)/shard_map/all_to_all | solution.py:299
  552.2 44.1 %collective-permute-start.31 = (bf16[1024,512]{1,0:T(8,128)(2,1)S(1)}, bf16[1024,512]{1,0:T(8,128)(2,1)S(1)}, u32[]{:S(2)}, u32[]{:S(2)}) collective-permute-start(bf16[1024,512]{1,0:T(8,128)(2,1)S(1)} %get-tuple-element.137.kept_ref), channel_id=1, source_target_pairs={{4,0},{5,1},{6,2},{7,3},{8,12},{9,13},{10,14},{11,15},{20,16},{21,... | collective-permute-start | bytes 3145736 | tf_op jit(solution)/shard_map/ppermute | solution.py:250
  553.5 58.0 %collective-permute-start.34 = (bf16[688,1024]{1,0:T(8,128)(2,1)}, bf16[688,1024]{1,0:T(8,128)(2,1)}, u32[]{:S(2)}, u32[]{:S(2)}) collective-permute-start(bf16[688,1024]{1,0:T(8,128)(2,1)} %add_convert_fusion.7.kept_ref), channel_id=1, source_target_pairs={{4,0},{5,1},{6,2},{7,3},{8,12},{9,13},{10,14},{11,15},{20,16},{21,... | collective-permute-start | bytes 4227080 | tf_op jit(solution)/shard_map/ppermute | solution.py:250
  597.3 49.5 %all-to-all-start.6 = ((bf16[4,128,2048]{2,1,0:T(8,128)(2,1)}), bf16[4,128,2048]{2,1,0:T(8,128)(2,1)}, u32[]{:S(2)}, u32[]{:S(2)}) async-start(bf16[4,128,2048]{2,1,0:T(8,128)(2,1)} %bitcast.106), calls=%async_computation.6 | async-start | bytes 4194304 | tf_op jit(solution)/shard_map/all_to_all | solution.py:299
  607.0 25.8 %collective-permute-start.32 = (bf16[1024,512]{1,0:T(8,128)(2,1)S(1)}, bf16[1024,512]{1,0:T(8,128)(2,1)S(1)}, u32[]{:S(2)}, u32[]{:S(2)}) collective-permute-start(bf16[1024,512]{1,0:T(8,128)(2,1)S(1)} %fusion.5.kept_ref), channel_id=1, source_target_pairs={{4,0},{5,1},{6,2},{7,3},{8,12},{9,13},{10,14},{11,15},{20,16},{21,... | collective-permute-start | bytes 3145736 | tf_op jit(solution)/shard_map/ppermute | solution.py:250
  625.0 33.2 %collective-permute-start.37 = (bf16[688,512]{1,0:T(8,128)(2,1)}, bf16[688,512]{1,0:T(8,128)(2,1)}, u32[]{:S(2)}, u32[]{:S(2)}) collective-permute-start(bf16[688,512]{1,0:T(8,128)(2,1)} %shard_map.253), channel_id=1, source_target_pairs={{0,8},{1,9},{2,10},{3,11},{12,4},{13,5},{14,6},{15,7},{16,24},{17,... | collective-permute-start | bytes 2113544 | tf_op jit(solution)/shard_map/ppermute | solution.py:250
  630.7 16.1 %collective-permute-start.33 = (bf16[512,512]{1,0:T(8,128)(2,1)}, bf16[512,512]{1,0:T(8,128)(2,1)}, u32[]{:S(2)}, u32[]{:S(2)}) collective-permute-start(bf16[512,512]{1,0:T(8,128)(2,1)} %shard_map.246), channel_id=1, source_target_pairs={{0,8},{1,9},{2,10},{3,11},{12,4},{13,5},{14,6},{15,7},{16,24},{17,... | collective-permute-start | bytes 1572872 | tf_op jit(solution)/shard_map/ppermute | solution.py:250
  650.6 15.5 %all-to-all-start.8 = ((f32[32,1,192]{2,1,0:T(1,128)}), f32[32,1,192]{2,1,0:T(1,128)S(1)}, u32[]{:S(2)}, u32[]{:S(2)}) async-start(f32[32,1,192]{2,1,0:T(1,128)} %reshape.214), calls=%async_computation.8 | async-start | bytes 65536 | tf_op jit(solution)/shard_map/all_to_all | solution.py:370
  (76 other events, 528.7 us)
Sparse Core Ops, SparseCore 0:
  24.8 39.4 all-gather.5
  66.4 49.5 all-gather.7
  255.8 43.3 all-gather.9
  301.3 29.0 all-gather.11
  396.8 38.9 all-gather.13
